TPU v7x, 128 devices: a whole 4x4x4 slice. The times are simulated.
128 devices in a mesh: section: 2 (over y_hi), ep: 32 (over x, z, core), tp: 2 (over y_lo).
Axes of the slice: x: 4, y: 4 (y_hi: 2, y_lo: 2; y = y_hi * 2 + y_lo), z: 4, core: 2. Of those that a mesh axis runs over, the one named last changes fastest.
Arguments:
- x_in: bfloat16 [2, 2048, 1536], P(None, 'ep'), may hold values from -6 to 6
- cotangent: bfloat16 [2, 2048, 1536], P(None, ('ep', 'tp')), may hold values from -6 to 6
- norm1_gain: float32 [2, 1536], P('section'), may hold values from 0.5 to 1.5
- wq: bfloat16 [2, 1536, 1536], P('section', None, 'tp'), may hold values from -0.15625 to 0.15625
- wk: bfloat16 [2, 1536, 512], P('section', None, 'tp'), may hold values from -0.15625 to 0.15625
- wv: bfloat16 [2, 1536, 512], P('section', None, 'tp'), may hold values from -0.15625 to 0.15625
- wo: bfloat16 [2, 1536, 1536], P('section', 'tp'), may hold values from -4 to 4
- norm2_gain: float32 [2, 1536], P('section'), may hold values from 0.5 to 1.5
- router: bfloat16 [2, 1536, 40], P('section'), may hold values from -0.078125 to 0.078125
- w_gate: bfloat16 [2, 1536, 20480], P('section', None, 'ep'), may hold values from -0.15625 to 0.15625
- w_up: bfloat16 [2, 1536, 20480], P('section', None, 'ep'), may hold values from -0.15625 to 0.15625
- w_down: bfloat16 [2, 20480, 1536], P('section', 'ep'), may hold values from -1.5 to 1.5
- routes: int32 [2, 2, 2048, 8], P('section', None, 'ep'), may hold values from 0 to 39, all different within a row; in each aligned block of 32 rows (0 to 31, 32 to 63, ..., all dimensions but the last counted through in order) at most 8 rows name the same one
Outputs:
- activations: bfloat16 [2, 2, 2048, 1536], P('section', None, 'ep')
- input_grads: bfloat16 [2, 2, 2048, 1536], P('section', None, ('ep', 'tp'))
- grad_norm1: float32 [2, 1536], P('section')
- grad_wq: float32 [2, 1536, 1536], P('section', None, 'tp')
- grad_wk: float32 [2, 1536, 512], P('section', None, 'tp')
- grad_wv: float32 [2, 1536, 512], P('section', None, 'tp')
- grad_wo: float32 [2, 1536, 1536], P('section', 'tp')
- grad_norm2: float32 [2, 1536], P('section')
- grad_router: float32 [2, 1536, 40], P('section')
- grad_gate: float32 [2, 1536, 20480], P('section', None, 'ep')
- grad_up: float32 [2, 1536, 20480], P('section', None, 'ep')
- grad_down: float32 [2, 20480, 1536], P('section', 'ep')
Inputs may be any that keep to these rules, and one draw needn't show every extreme that they name: `routes`: each row names 8 different experts; in each aligned block of 32 rows (all leading dimensions taken together) no expert is named more than 8 times, a bound that some block reaches.
All inputs are finite; a program needn't handle non-finite values.
Results may differ from a plain program's by a relative error of at most 0.033.
Values may be sent and summed in bfloat16 or wider, within the bound.
No kernel may reach another device: no remote copies, remote signals or barrier semaphores. Data moves between devices by JAX's collectives and lax.ppermute only.
A program may use at most 256 MiB of HBM per device.

v0:
```python
import jax
import jax.numpy as jnp
import numpy as np
from jax import lax
from jax.sharding import PartitionSpec as P

HEAD_SIZE = 64
EFF = 512
TOPK = 8
BLOCK = 128


epsilon = 1e-05
highest_precision = lax.Precision.HIGHEST


def in_one_piece(arrays, axis, dim, along):
    both = jnp.concatenate(arrays, axis=along)
    result, at, gathered = (lax.all_gather(both, axis, axis=dim, tiled=True), 0, [])
    for a in arrays:
        gathered.append(lax.slice_in_dim(result, at, at + a.shape[along], axis=along))
        at += a.shape[along]
    return tuple(gathered)


def cut_along(value, dim, count):
    before, after = (value.shape[:dim], value.shape[dim + 1 :])
    return jnp.moveaxis(value.reshape(*before, count, -1, *after), dim, 0)


def sum_at_owner(value, axis, dim):
    pieces = cut_along(value, dim, lax.axis_size(axis))
    arrived = lax.all_to_all(pieces, axis, split_axis=0, concat_axis=0, tiled=True)
    return arrived.astype(jnp.float32).sum(axis=0)


def in_order(pieces, dim):
    pieces = jnp.moveaxis(pieces, 0, dim)
    shape = pieces.shape
    return pieces.reshape(*shape[:dim], shape[dim] * shape[dim + 1], *shape[dim + 2 :])


def from_everyone(value, axis):
    count = lax.axis_size(axis)
    return lax.all_to_all(
        jnp.broadcast_to(value[None], (count, *value.shape)), axis, 0, 0, tiled=True
    )


def collect(value, axis, dim):
    return in_order(from_everyone(value, axis), dim)


def side_by_side(arrays, axis, dim, along):
    widths = [a.shape[along] for a in arrays]
    both = jnp.concatenate(arrays, axis=along)
    result = lax.psum_scatter(both, axis, scatter_dimension=dim, tiled=True)
    return tuple(jnp.split(result, [sum(widths[:k]) for k in range(1, len(widths))], axis=along))


def from_behind(value, axis, steps):
    count = lax.axis_size(axis)
    initial, last = (max(0, -steps), min(count, count - steps))
    return lax.ppermute(value, axis, [(source, source + steps) for source in range(initial, last)])


def inverse_root(values):
    return lax.rsqrt(jnp.mean(values * values, axis=-1, keepdims=True) + epsilon)


def norm_back(values, gradient, gain):
    scale_row = inverse_root(values)
    weighted = gradient * gain
    return scale_row * weighted - values * scale_row**3 * jnp.mean(
        weighted * values, axis=-1, keepdims=True
    )


def apply_rotation(values, cosine_table, sine_values):
    half_dim = values.shape[-1] // 2
    first_half = values[..., :half_dim]
    second_half = values[..., half_dim:]
    cos_wide = cosine_table[:, None, :]
    sin_wide = sine_values[:, None, :]
    return jnp.concatenate(
        [
            first_half * cos_wide - second_half * sin_wide,
            second_half * cos_wide + first_half * sin_wide,
        ],
        axis=-1,
    )


def angles(positions, head_dim):
    half_dim = head_dim // 2
    frequency = 10000.0 ** (-jnp.arange(half_dim, dtype=jnp.float32) * 2.0 / head_dim)
    phase_grid = positions.astype(jnp.float32)[:, None] * frequency[None, :]
    return (jnp.cos(phase_grid), jnp.sin(phase_grid))


def slots_of(route_rows, experts):
    expert_hits = (
        route_rows[:, :, None] == jnp.arange(experts, dtype=jnp.int32)[None, None, :]
    ).astype(jnp.int32)
    per_row = jnp.sum(expert_hits, axis=1)
    before = jnp.cumsum(per_row, axis=0) - per_row
    return jnp.sum(expert_hits * before[:, None, :], axis=-1)


def body(
    x_in, cotangent, norm1_gain, wq, wk, wv, wo, norm2_gain, router, w_gate, w_up, w_down, routes
):
    sections = lax.axis_size("section")
    rank_count = lax.axis_size("ep")
    halves = lax.axis_size("tp")
    section_id = lax.axis_index("section")
    rank_id = lax.axis_index("ep")
    half_id = lax.axis_index("tp")
    micro_count = x_in.shape[0]
    seq_rows = x_in.shape[1]
    model_width = x_in.shape[2]
    own_rows = seq_rows // halves
    sequence_length = seq_rows * rank_count
    heads_q = wq.shape[2] // HEAD_SIZE
    heads_kv = wk.shape[2] // HEAD_SIZE
    group_size = heads_q // heads_kv
    experts = router.shape[2]
    blocks_dev = w_gate.shape[2] // BLOCK
    expert_blocks = EFF // BLOCK
    slot_count = (own_rows * TOPK * 5 + 4 * experts - 1) // (4 * experts)
    gain_one = norm1_gain[0]
    query_w = wq[0]
    key_weight = wk[0]
    value_weight = wv[0]
    output_w = wo[0]
    gain_two = norm2_gain[0]
    router_w = router[0]
    gate_blocks = w_gate[0].reshape(model_width, blocks_dev, BLOCK)
    up_blocks = w_up[0].reshape(model_width, blocks_dev, BLOCK)
    down_blocks = w_down[0].reshape(blocks_dev, BLOCK, model_width)
    positions = rank_id * seq_rows + jnp.arange(seq_rows, dtype=jnp.int32)
    cosine_table, sine_values = angles(positions, HEAD_SIZE)
    causal = positions[:, None] >= jnp.arange(sequence_length, dtype=jnp.int32)[None, :]
    span_count = min((blocks_dev - 1) // expert_blocks + 2, experts)
    firsts = np.arange(rank_count) * blocks_dev // expert_blocks
    span_expert = np.minimum(firsts[:, None] + np.arange(span_count)[None, :], experts - 1)
    local_first = rank_id * blocks_dev // expert_blocks
    local_which = (
        rank_id * blocks_dev + jnp.arange(blocks_dev, dtype=jnp.int32)
    ) // expert_blocks - local_first

    def pack_rows(buffer):
        packed = jnp.take(buffer, jnp.asarray(span_expert, dtype=jnp.int32), axis=0)
        return packed

    def unpack_rows(arrived):
        unpacked = jnp.take(arrived, local_which, axis=1)
        return unpacked

    def attention_scores(query_rotated, keys_wide, log_total):
        scores = (
            jnp.einsum(
                "qgjd,kgd->gjqk", query_rotated, keys_wide, preferred_element_type=jnp.float32
            )
            * 0.125
        )
        scores = jnp.where(causal[None, None], scores, -1e30)
        return scores if log_total is None else jnp.exp(scores - log_total)

    total_ticks = micro_count + sections - 1
    micro_ids = jnp.arange(micro_count, dtype=jnp.int32)
    incoming = jnp.zeros((seq_rows, model_width), jnp.bfloat16)
    activations = jnp.zeros((micro_count, seq_rows, model_width), jnp.bfloat16)
    saved_list = []
    for tick_index in range(total_ticks):
        micro_index = tick_index - section_id
        micro_slot = jnp.clip(micro_index, 0, micro_count - 1)
        first_input = lax.dynamic_index_in_dim(x_in, micro_slot, 0, keepdims=False)
        inputs = jnp.where(section_id == 0, first_input, incoming).astype(jnp.float32)
        route_all = lax.dynamic_index_in_dim(routes[0], micro_slot, 0, keepdims=False)
        route_rows = lax.dynamic_slice_in_dim(route_all, half_id * own_rows, own_rows, 0)
        forward_normalized_rows = (inputs * inverse_root(inputs) * gain_one).astype(jnp.bfloat16)
        query_projected = jnp.dot(
            forward_normalized_rows, query_w, preferred_element_type=jnp.float32
        ).reshape(seq_rows, heads_q, HEAD_SIZE)
        key_projected = jnp.dot(
            forward_normalized_rows, key_weight, preferred_element_type=jnp.float32
        ).reshape(seq_rows, heads_kv, HEAD_SIZE)
        forward_value_rows = jnp.dot(
            forward_normalized_rows, value_weight, preferred_element_type=jnp.float32
        ).astype(jnp.bfloat16)
        forward_query_rotated = (
            apply_rotation(query_projected, cosine_table, sine_values)
            .astype(jnp.bfloat16)
            .reshape(seq_rows, heads_kv, group_size, HEAD_SIZE)
        )
        key_rot = (
            apply_rotation(key_projected, cosine_table, sine_values)
            .astype(jnp.bfloat16)
            .reshape(seq_rows, heads_kv * HEAD_SIZE)
        )
        forward_keys_all, forward_values_all = in_one_piece(
            (key_rot, forward_value_rows), "ep", 0, 1
        )
        forward_keys_wide = forward_keys_all.reshape(sequence_length, heads_kv, HEAD_SIZE)
        forward_values_wide = forward_values_all.reshape(sequence_length, heads_kv, HEAD_SIZE)
        forward_scores = attention_scores(forward_query_rotated, forward_keys_wide, None)
        row_peak = jnp.max(forward_scores, axis=-1, keepdims=True)
        forward_log_total = row_peak + jnp.log(
            jnp.sum(jnp.exp(forward_scores - row_peak), axis=-1, keepdims=True)
        )
        forward_probs_low = jnp.exp(forward_scores - forward_log_total).astype(jnp.bfloat16)
        forward_attended = (
            jnp.einsum(
                "gjqk,kgd->qgjd",
                forward_probs_low,
                forward_values_wide,
                preferred_element_type=jnp.float32,
            )
            .astype(jnp.bfloat16)
            .reshape(seq_rows, heads_q * HEAD_SIZE)
        )
        attn_rows = sum_at_owner(
            jnp.dot(forward_attended, output_w, preferred_element_type=jnp.float32).astype(
                jnp.bfloat16
            ),
            "tp",
            0,
        )
        forward_own_inputs = lax.dynamic_slice_in_dim(inputs, half_id * own_rows, own_rows, 0)
        forward_residual = forward_own_inputs + attn_rows
        forward_mixed_rows = (forward_residual * inverse_root(forward_residual) * gain_two).astype(
            jnp.bfloat16
        )
        logits = jnp.dot(forward_mixed_rows, router_w, preferred_element_type=jnp.float32)
        forward_expert_hits = (
            route_rows[:, :, None] == jnp.arange(experts, dtype=jnp.int32)[None, None, :]
        ).astype(jnp.float32)
        chosen = jnp.sum(forward_expert_hits * logits[:, None, :], axis=-1)
        forward_gate_weights = jax.nn.softmax(chosen, axis=-1)
        slot_ids = slots_of(route_rows, experts)
        forward_target = route_rows * slot_count + slot_ids
        forward_source = (
            jnp.full((experts * slot_count,), -1, jnp.int32)
            .at[forward_target.reshape(-1)]
            .set(jnp.arange(own_rows * TOPK, dtype=jnp.int32))
        )
        forward_filled = forward_source >= 0
        forward_source_pair = jnp.maximum(forward_source, 0)
        forward_buffer = jnp.where(
            forward_filled[:, None],
            forward_mixed_rows[forward_source_pair // TOPK],
            jnp.zeros((), jnp.bfloat16),
        ).reshape(experts, slot_count, model_width)
        forward_arrived = unpack_rows(
            lax.all_to_all(pack_rows(forward_buffer), "ep", split_axis=0, concat_axis=0, tiled=True)
        )
        forward_gate_pre = jnp.einsum(
            "skcd,dkh->skch", forward_arrived, gate_blocks, preferred_element_type=jnp.float32
        )
        forward_up_pre = jnp.einsum(
            "skcd,dkh->skch", forward_arrived, up_blocks, preferred_element_type=jnp.float32
        )
        forward_hidden = (jax.nn.silu(forward_gate_pre) * forward_up_pre).astype(jnp.bfloat16)
        block_out = jnp.einsum(
            "skch,khd->skcd", forward_hidden, down_blocks, preferred_element_type=jnp.float32
        ).astype(jnp.bfloat16)
        returned = lax.all_to_all(block_out, "ep", split_axis=0, concat_axis=0, tiled=True)
        expert_out = jnp.sum(
            returned.reshape(experts, expert_blocks, slot_count, model_width),
            axis=1,
            dtype=jnp.float32,
        )
        forward_picked = expert_out.reshape(experts * slot_count, model_width)[forward_target]
        out_rows = (
            forward_residual + jnp.sum(forward_gate_weights[..., None] * forward_picked, axis=1)
        ).astype(jnp.bfloat16)
        out_full = collect(out_rows, "tp", 0)
        forward_kept_state = (
            forward_own_inputs,
            forward_normalized_rows,
            forward_query_rotated,
            forward_keys_all,
            forward_values_all,
            forward_log_total,
            forward_attended,
            forward_residual,
            forward_mixed_rows,
            forward_gate_weights,
            forward_expert_hits,
            forward_target,
            forward_source,
            forward_picked,
            forward_arrived,
            forward_gate_pre,
            forward_up_pre,
        )
        out_full, kept_state = (out_full, forward_kept_state)
        activations = jnp.where((micro_ids == micro_index)[:, None, None], out_full, activations)
        saved_list.append(kept_state)
        if tick_index + 1 < total_ticks:
            incoming = from_behind(out_full, "section", 1)
    stacked = jax.tree.map(lambda *leaves: jnp.stack(leaves), *saved_list)
    coming = jnp.zeros((own_rows, model_width), jnp.bfloat16)
    input_grads = jnp.zeros((micro_count, own_rows, model_width), jnp.bfloat16)
    totals = None
    for tick_index in range(total_ticks):
        micro_index = tick_index - (sections - 1 - section_id)
        micro_slot = jnp.clip(micro_index, 0, micro_count - 1)
        is_live = (micro_index >= 0) & (micro_index < micro_count)
        given_grad = lax.dynamic_index_in_dim(cotangent, micro_slot, 0, keepdims=False)
        grad_rows = jnp.where(section_id == sections - 1, given_grad, coming).astype(jnp.float32)
        grad_rows = jnp.where(is_live, grad_rows, 0.0)
        kept_state = jax.tree.map(
            lambda leaf_arr: lax.dynamic_index_in_dim(
                leaf_arr, micro_slot + section_id, 0, keepdims=False
            ),
            stacked,
        )
        (
            own_inputs,
            normalized_rows,
            backward_query_rotated,
            keys_all,
            values_all,
            backward_log_total,
            attended,
            residual,
            mixed_rows,
            gate_weights,
            expert_hits,
            target,
            source,
            picked,
            backward_arrived,
            gate_pre,
            up_pre,
        ) = kept_state
        scaled = (gate_weights[..., None] * grad_rows[:, None, :]).astype(jnp.bfloat16)
        weight_grad = jnp.sum(picked * grad_rows[:, None, :], axis=-1)
        chosen_grad = gate_weights * (
            weight_grad - jnp.sum(gate_weights * weight_grad, axis=-1, keepdims=True)
        )
        logit_grad = jnp.sum(expert_hits * chosen_grad[:, :, None], axis=1)
        router_acc = jnp.einsum(
            "td,te->de", mixed_rows.astype(jnp.float32), logit_grad, precision=highest_precision
        )
        mixed_grad = jnp.einsum(
            "te,de->td", logit_grad, router_w.astype(jnp.float32), precision=highest_precision
        )
        filled = source >= 0
        source_pair = jnp.maximum(source, 0)
        grad_buffer = jnp.where(
            filled[:, None],
            scaled.reshape(own_rows * TOPK, model_width)[source_pair],
            jnp.zeros((), jnp.bfloat16),
        ).reshape(experts, slot_count, model_width)
        arrived_grad = unpack_rows(
            lax.all_to_all(pack_rows(grad_buffer), "ep", split_axis=0, concat_axis=0, tiled=True)
        )
        hidden = (jax.nn.silu(gate_pre) * up_pre).astype(jnp.bfloat16)
        down_acc = jnp.einsum(
            "skch,skcd->khd", hidden, arrived_grad, preferred_element_type=jnp.float32
        )
        hidden_grad = jnp.einsum(
            "skcd,khd->skch", arrived_grad, down_blocks, preferred_element_type=jnp.float32
        )
        sigmoid_gate = jax.nn.sigmoid(gate_pre)
        gate_grad = (
            hidden_grad * up_pre * sigmoid_gate * (1.0 + gate_pre * (1.0 - sigmoid_gate))
        ).astype(jnp.bfloat16)
        up_grad = (hidden_grad * gate_pre * sigmoid_gate).astype(jnp.bfloat16)
        gate_acc = jnp.einsum(
            "skcd,skch->dkh", backward_arrived, gate_grad, preferred_element_type=jnp.float32
        )
        up_acc = jnp.einsum(
            "skcd,skch->dkh", backward_arrived, up_grad, preferred_element_type=jnp.float32
        )
        row_grads = jnp.einsum(
            "skch,dkh->skcd", gate_grad, gate_blocks, preferred_element_type=jnp.float32
        ) + jnp.einsum("skch,dkh->skcd", up_grad, up_blocks, preferred_element_type=jnp.float32)
        folding = (local_which[:, None] == jnp.arange(span_count, dtype=jnp.int32)[None, :]).astype(
            jnp.float32
        )
        outgoing = jnp.einsum("ks,nkcd->nscd", folding, row_grads, precision=highest_precision)
        came_back = lax.all_to_all(
            outgoing.astype(jnp.bfloat16), "ep", split_axis=0, concat_axis=0, tiled=True
        ).astype(outgoing.dtype)
        spread = jnp.asarray(
            (span_expert.reshape(-1)[:, None] == np.arange(experts)[None, :]).astype(np.float32)
        )
        buffer_grad = jnp.einsum(
            "xe,xcd->ecd",
            spread,
            came_back.reshape(rank_count * span_count, slot_count, model_width),
            precision=highest_precision,
        )
        mixed_grad = mixed_grad + jnp.sum(
            buffer_grad.reshape(experts * slot_count, model_width)[target], axis=1
        )
        gain_two_acc = jnp.sum(mixed_grad * residual * inverse_root(residual), axis=0)
        resid_grad = grad_rows + norm_back(residual, mixed_grad, gain_two)
        full_grad = collect(resid_grad.astype(jnp.bfloat16), "tp", 0).astype(resid_grad.dtype)
        out_grad = full_grad.astype(jnp.bfloat16)
        output_acc = jnp.einsum("sh,sd->hd", attended, out_grad, preferred_element_type=jnp.float32)
        attended_grad = (
            jnp.einsum("sd,hd->sh", out_grad, output_w, preferred_element_type=jnp.float32)
            .astype(jnp.bfloat16)
            .reshape(seq_rows, heads_kv, group_size, HEAD_SIZE)
        )
        backward_keys_wide = keys_all.reshape(sequence_length, heads_kv, HEAD_SIZE)
        values_wide = values_all.reshape(sequence_length, heads_kv, HEAD_SIZE)
        probabilities = attention_scores(
            backward_query_rotated, backward_keys_wide, backward_log_total
        )
        probs_low = probabilities.astype(jnp.bfloat16)
        prob_grad = jnp.einsum(
            "qgjd,kgd->gjqk", attended_grad, values_wide, preferred_element_type=jnp.float32
        )
        values_part = jnp.einsum(
            "gjqk,qgjd->kgd", probs_low, attended_grad, preferred_element_type=jnp.float32
        ).reshape(sequence_length, heads_kv * HEAD_SIZE)
        row_inner = jnp.sum(probabilities * prob_grad, axis=-1, keepdims=True)
        score_grad = (probabilities * (prob_grad - row_inner)).astype(jnp.bfloat16)
        query_part = 0.125 * jnp.einsum(
            "gjqk,kgd->qgjd", score_grad, backward_keys_wide, preferred_element_type=jnp.float32
        )
        keys_part = 0.125 * jnp.einsum(
            "gjqk,qgjd->kgd", score_grad, backward_query_rotated, preferred_element_type=jnp.float32
        ).reshape(sequence_length, heads_kv * HEAD_SIZE)
        key_sum, value_sum = tuple(
            (
                part.astype(jnp.float32)
                for part in side_by_side(
                    (keys_part.astype(jnp.bfloat16), values_part.astype(jnp.bfloat16)), "ep", 0, 1
                )
            )
        )
        query_grad = (
            apply_rotation(
                query_part.reshape(seq_rows, heads_q, HEAD_SIZE), cosine_table, -sine_values
            )
            .astype(jnp.bfloat16)
            .reshape(seq_rows, heads_q * HEAD_SIZE)
        )
        key_grad = (
            apply_rotation(
                key_sum.reshape(seq_rows, heads_kv, HEAD_SIZE), cosine_table, -sine_values
            )
            .astype(jnp.bfloat16)
            .reshape(seq_rows, heads_kv * HEAD_SIZE)
        )
        value_grad = value_sum.astype(jnp.bfloat16)
        query_acc = jnp.einsum(
            "sd,sh->dh", normalized_rows, query_grad, preferred_element_type=jnp.float32
        )
        key_acc = jnp.einsum(
            "sd,sh->dh", normalized_rows, key_grad, preferred_element_type=jnp.float32
        )
        value_acc = jnp.einsum(
            "sd,sh->dh", normalized_rows, value_grad, preferred_element_type=jnp.float32
        )
        total_term = jnp.einsum(
            "sh,dh->sd", query_grad, query_w, preferred_element_type=jnp.float32
        )
        total_term = total_term + jnp.einsum(
            "sh,dh->sd", key_grad, key_weight, preferred_element_type=jnp.float32
        )
        normed_grad = sum_at_owner(
            (
                total_term
                + jnp.einsum(
                    "sh,dh->sd", value_grad, value_weight, preferred_element_type=jnp.float32
                )
            ).astype(jnp.bfloat16),
            "tp",
            0,
        )
        gain_one_acc = jnp.sum(normed_grad * own_inputs * inverse_root(own_inputs), axis=0)
        input_grad = resid_grad + norm_back(own_inputs, normed_grad, gain_one)
        input_grad, increments = (
            input_grad,
            (
                gain_one_acc,
                query_acc,
                key_acc,
                value_acc,
                output_acc,
                gain_two_acc,
                router_acc,
                gate_acc,
                up_acc,
                down_acc,
            ),
        )
        totals = (
            increments
            if totals is None
            else tuple((total_arr + incr_arr for total_arr, incr_arr in zip(totals, increments)))
        )
        input_low = input_grad.astype(jnp.bfloat16)
        input_grads = jnp.where((micro_ids == micro_index)[:, None, None], input_low, input_grads)
        if tick_index + 1 < total_ticks:
            coming = from_behind(input_low, "section", -1)
    ep_sums = (
        lax.psum(totals[1].astype(jnp.bfloat16), "ep").astype(jnp.float32),
        lax.psum(totals[2].astype(jnp.bfloat16), "ep").astype(jnp.float32),
        lax.psum(totals[3].astype(jnp.bfloat16), "ep").astype(jnp.float32),
        lax.psum(totals[4].astype(jnp.bfloat16), "ep").astype(jnp.float32),
        lax.psum(totals[0].astype(jnp.bfloat16), "ep").astype(jnp.float32),
        lax.psum(totals[5].astype(jnp.bfloat16), "ep").astype(jnp.float32),
        lax.psum(totals[6].astype(jnp.bfloat16), "ep").astype(jnp.float32),
    )
    tp_sums = (
        lax.psum(totals[7].astype(jnp.bfloat16), "tp").astype(jnp.float32),
        lax.psum(totals[8].astype(jnp.bfloat16), "tp").astype(jnp.float32),
        lax.psum(totals[9].astype(jnp.bfloat16), "tp").astype(jnp.float32),
        lax.psum(ep_sums[4].astype(jnp.bfloat16), "tp").astype(jnp.float32),
        lax.psum(ep_sums[5].astype(jnp.bfloat16), "tp").astype(jnp.float32),
        lax.psum(ep_sums[6].astype(jnp.bfloat16), "tp").astype(jnp.float32),
    )
    return (
        activations[None],
        input_grads[None],
        tp_sums[3][None],
        ep_sums[0][None],
        ep_sums[1][None],
        ep_sums[2][None],
        ep_sums[3][None],
        tp_sums[4][None],
        tp_sums[5][None],
        tp_sums[0].reshape(1, model_width, blocks_dev * BLOCK),
        tp_sums[1].reshape(1, model_width, blocks_dev * BLOCK),
        tp_sums[2].reshape(1, blocks_dev * BLOCK, model_width),
    )


def solution(mesh):
    placed = (
        P(None, "ep", None),
        P(None, ("ep", "tp"), None),
        P("section", None),
        P("section", None, "tp"),
        P("section", None, "tp"),
        P("section", None, "tp"),
        P("section", "tp", None),
        P("section", None),
        P("section", None, None),
        P("section", None, "ep"),
        P("section", None, "ep"),
        P("section", "ep", None),
        P("section", None, "ep", None),
    )
    return jax.shard_map(
        body,
        mesh=mesh,
        in_specs=placed,
        out_specs=(
            P("section", None, "ep", None),
            P("section", None, ("ep", "tp"), None),
            P("section", None),
            P("section", None, "tp"),
            P("section", None, "tp"),
            P("section", None, "tp"),
            P("section", "tp", None),
            P("section", None),
            P("section", None, None),
            P("section", None, "ep"),
            P("section", None, "ep"),
            P("section", "ep", None),
        ),
        check_vma=False,
    )
```

profile of v0, /device:TPU:1, one launch (start us, length us, event | category | flops | bytes accessed | tf_op | source)
XLA Modules:
  0.0 1655.0 jit_solution(5694919444471690853)
XLA Ops:
  28.7 35.5 %all-gather.4.cloned.1.call-done = bf16[2048,512]{1,0:T(8,128)(2,1)} async-done(((bf16[64,512]{1,0:T(8,128)(2,1)}), bf16[2048,512]{1,0:T(8,128)(2,1)}) %all-gather.4.cloned.1.call-update) | async-done | bytes 2097168 | tf_op jit(solution)/shard_map/all_gather | solution.py:19
  97.6 6.5 all-to-all-start.1
  112.8 22.4 %all-to-all-done.1 = bf16[32,3,8,1536]{3,2,1,0:T(8,128)(2,1)} async-done(((bf16[32,3,8,1536]{3,2,1,0:T(8,128)(2,1)}), bf16[32,3,8,1536]{3,2,1,0:T(8,128)(2,1)}, u32[]{:S(2)}, u32[]{:S(2)}) %all-to-all-start.1) | async-done | bytes 2359328 | tf_op jit(solution)/shard_map/all_to_all | solution.py:256
  157.1 46.7 %all-to-all-done.2 = bf16[32,5,8,1536]{3,2,1,0:T(8,128)(2,1)} async-done(((bf16[32,5,8,1536]{3,2,1,0:T(8,128)(2,1)}), bf16[32,5,8,1536]{3,2,1,0:T(8,128)(2,1)}, u32[]{:S(2)}, u32[]{:S(2)}) %all-to-all-start.2) | async-done | bytes 3932192 | tf_op jit(solution)/shard_map/all_to_all | solution.py:268
  215.8 6.1 all_to_all.120
  245.7 37.0 %all-gather.6.cloned.1.call-done = bf16[2048,512]{1,0:T(8,128)(2,1)} async-done(((bf16[64,512]{1,0:T(8,128)(2,1)}), bf16[2048,512]{1,0:T(8,128)(2,1)}) %all-gather.6.cloned.1.call-update) | async-done | bytes 2097168 | tf_op jit(solution)/shard_map/all_gather | solution.py:19
  319.7 37.6 %all_to_all.121 = bf16[32,3,8,1536]{3,2,1,0:T(8,128)(2,1)} all-to-all(bf16[32,3,8,1536]{3,2,1,0:T(8,128)(2,1)} %bitcast.1334), channel_id=1, replica_groups=mesh['section'=2,'ep'=32,'tp'=2] {'ep'}, dimensions={0} | all-to-all | bytes 4718592 | tf_op jit(solution)/shard_map/all_to_all | solution.py:256
  378.8 46.9 %all-to-all-done.6 = bf16[32,5,8,1536]{3,2,1,0:T(8,128)(2,1)} async-done(((bf16[32,5,8,1536]{3,2,1,0:T(8,128)(2,1)}), bf16[32,5,8,1536]{3,2,1,0:T(8,128)(2,1)}, u32[]{:S(2)}, u32[]{:S(2)}) %all-to-all-start.6) | async-done | bytes 3932192 | tf_op jit(solution)/shard_map/all_to_all | solution.py:268
  437.6 6.1 all_to_all.122
  461.8 39.8 %all-gather.8.cloned.1.call-done = bf16[2048,512]{1,0:T(8,128)(2,1)} async-done(((bf16[64,512]{1,0:T(8,128)(2,1)}), bf16[2048,512]{1,0:T(8,128)(2,1)}) %all-gather.8.cloned.1.call-update) | async-done | bytes 2097168 | tf_op jit(solution)/shard_map/all_gather | solution.py:19
  534.6 6.3 all-to-all-start.9
  552.9 19.1 %all-to-all-done.9 = bf16[32,3,8,1536]{3,2,1,0:T(8,128)(2,1)} async-done(((bf16[32,3,8,1536]{3,2,1,0:T(8,128)(2,1)}), bf16[32,3,8,1536]{3,2,1,0:T(8,128)(2,1)}, u32[]{:S(2)}, u32[]{:S(2)}) %all-to-all-start.9) | async-done | bytes 2359328 | tf_op jit(solution)/shard_map/all_to_all | solution.py:256
  592.0 16.5 all-to-all-done.12
  620.8 11.5 fusion.93
  645.1 25.9 %all-to-all-done.13 = bf16[32,3,8,1536]{3,2,1,0:T(8,128)(2,1)} async-done(((bf16[32,3,8,1536]{3,2,1,0:T(8,128)(2,1)}), bf16[32,3,8,1536]{3,2,1,0:T(8,128)(2,1)}, u32[]{:S(2)}, u32[]{:S(2)}) %all-to-all-start.13) | async-done | bytes 2359328 | tf_op jit(solution)/shard_map/all_to_all | solution.py:386
  671.1 5.7 all-to-all-start.10
  708.4 17.4 %all-to-all-done.10 = bf16[32,5,8,1536]{3,2,1,0:T(8,128)(2,1)} async-done(((bf16[32,5,8,1536]{3,2,1,0:T(8,128)(2,1)}), bf16[32,5,8,1536]{3,2,1,0:T(8,128)(2,1)}, u32[]{:S(2)}, u32[]{:S(2)}) %all-to-all-start.10) | async-done | bytes 3932192 | tf_op jit(solution)/shard_map/all_to_all | solution.py:268
  775.8 73.7 %reduce-scatter.10.cloned.1.call-done = bf16[64,512]{1,0:T(8,128)(2,1)} async-done(((bf16[2048,512]{1,0:T(8,128)(2,1)}), bf16[64,512]{1,0:T(8,128)(2,1)}) %reduce-scatter.10.cloned.1.call-update) | async-done | bytes 65552
  882.4 41.5 %all_to_all.123 = bf16[32,3,8,1536]{3,2,1,0:T(8,128)(2,1)} all-to-all(bf16[32,3,8,1536]{3,2,1,0:T(8,128)(2,1)} %bitcast.1335), channel_id=1, replica_groups=mesh['section'=2,'ep'=32,'tp'=2] {'ep'}, dimensions={0} | all-to-all | bytes 4718592 | tf_op jit(solution)/shard_map/all_to_all | solution.py:359
  936.1 11.1 fusion.90
  959.1 26.4 %all-to-all-done.17 = bf16[32,3,8,1536]{3,2,1,0:T(8,128)(2,1)} async-done(((bf16[32,3,8,1536]{3,2,1,0:T(8,128)(2,1)}), bf16[32,3,8,1536]{3,2,1,0:T(8,128)(2,1)}, u32[]{:S(2)}, u32[]{:S(2)}) %all-to-all-start.17) | async-done | bytes 2359328 | tf_op jit(solution)/shard_map/all_to_all | solution.py:386
  1043.5 57.4 %reduce-scatter.12.cloned.1.call-done = bf16[64,512]{1,0:T(8,128)(2,1)} async-done(((bf16[2048,512]{1,0:T(8,128)(2,1)}), bf16[64,512]{1,0:T(8,128)(2,1)}) %reduce-scatter.12.cloned.1.call-update) | async-done | bytes 65552
  1134.5 10.3 all-to-all-start.20
  1157.3 18.5 %all-to-all-done.20 = bf16[32,3,8,1536]{3,2,1,0:T(8,128)(2,1)} async-done(((bf16[32,3,8,1536]{3,2,1,0:T(8,128)(2,1)}), bf16[32,3,8,1536]{3,2,1,0:T(8,128)(2,1)}, u32[]{:S(2)}, u32[]{:S(2)}) %all-to-all-start.20) | async-done | bytes 2359328 | tf_op jit(solution)/shard_map/all_to_all | solution.py:359
  1188.0 11.1 fusion.87
  1201.1 5.8 all-to-all-start.21
  1226.7 11.3 all-to-all-done.21
  1294.9 58.7 %reduce-scatter.14.cloned.1.call-done = bf16[64,512]{1,0:T(8,128)(2,1)} async-done(((bf16[2048,512]{1,0:T(8,128)(2,1)}), bf16[64,512]{1,0:T(8,128)(2,1)}) %reduce-scatter.14.cloned.1.call-update) | async-done | bytes 65552
  1398.3 78.5 %all-reduce.7.cloned.1.call-done = (bf16[1,1536,768]{2,1,0:T(8,128)(2,1)}, bf16[1,1536,256]{2,1,0:T(8,128)(2,1)}, bf16[1,1536,256]{2,1,0:T(8,128)(2,1)}, bf16[1,768,1536]{2,1,0:T(8,128)(2,1)}, bf16[1536,40]{0,1:T(8,128)(2,1)}) async-done(((bf16[1,1536,768]{2,1,0:T(8,128)(2,1)}, bf16[1,1536,256]{2,1,0:T(8,128)(2,1)}, bf16[1,1536,256]{2,1,0:T(8,128)(2,1)}, bf16[1,768,1536]{2,1,0:T(8,128)(2,1)}, ...) | async-done | bytes 6414352 | tf_op jit(solution)/shard_map/psum | solution.py:506
  1506.8 65.9 %all-reduce = (bf16[1536]{0:T(1024)(128)(2,1)S(1)}, bf16[1536]{0:T(1024)(128)(2,1)S(1)}) all-reduce(bf16[1536]{0:T(1024)(128)(2,1)S(1)} %add_convert_fusion.19, bf16[1536]{0:T(1024)(128)(2,1)S(1)} %add_convert_fusion.18), channel_id=1, replica_groups=mesh['section'=2,'ep'=32,'tp'=2] {'ep'}, use_global_device_ids=true, to_apply=%region_78.81 | all-reduce | flops 3072 | bytes 12288 | tf_op jit(solution)/shard_map/psum | solution.py:510
  1572.8 6.1 all-reduce.2
  1592.7 44.8 %all-reduce.9.cloned.1.call-done = (bf16[1,1536,40]{1,2,0:T(8,128)(2,1)}, bf16[1,1536,640]{2,1,0:T(8,128)(2,1)}, bf16[1,1536,640]{2,1,0:T(8,128)(2,1)}, bf16[1,640,1536]{2,1,0:T(8,128)(2,1)}) async-done(((bf16[1,1536,40]{1,2,0:T(8,128)(2,1)}, bf16[1,1536,640]{2,1,0:T(8,128)(2,1)}, bf16[1,1536,640]{2,1,0:T(8,128)(2,1)}, bf16[1,640,1536]{2,1,0:T(8,128)(2,1)}), (bf16[1,1536,40]{1,2,0:T(8,128)(2,1)}, ...) | async-done | bytes 6021136 | tf_op jit(solution)/shard_map/psum | solution.py:520
  (1022 shorter events, 728.5 us)
Async XLA Ops:
  7.2 57.1 %all-gather.4.cloned.1.call-start = ((), (), s32[]{:S(2)}) async-start(), calls=%async_computation.27 | async-start | bytes 2162688 | tf_op jit(solution)/shard_map/all_gather | solution.py:19
  80.4 7.8 all-to-all-start
  97.6 37.5 %all-to-all-start.1 = ((bf16[32,3,8,1536]{3,2,1,0:T(8,128)(2,1)}), bf16[32,3,8,1536]{3,2,1,0:T(8,128)(2,1)}, u32[]{:S(2)}, u32[]{:S(2)}) async-start(bf16[32,3,8,1536]{3,2,1,0:T(8,128)(2,1)} %bitcast.1330), calls=%async_computation.1 | async-start | bytes 4718592 | tf_op jit(solution)/shard_map/all_to_all | solution.py:256
  149.1 54.7 %all-to-all-start.2 = ((bf16[32,5,8,1536]{3,2,1,0:T(8,128)(2,1)}), bf16[32,5,8,1536]{3,2,1,0:T(8,128)(2,1)}, u32[]{:S(2)}, u32[]{:S(2)}) async-start(bf16[32,5,8,1536]{3,2,1,0:T(8,128)(2,1)} %copy.665), calls=%async_computation.2 | async-start | bytes 7864320 | tf_op jit(solution)/shard_map/all_to_all | solution.py:268
  154.6 128.1 %all-gather.6.cloned.1.call-start = ((), (), s32[]{:S(2)}) async-start(), calls=%async_computation.28 | async-start | bytes 2162688 | tf_op jit(solution)/shard_map/all_gather | solution.py:19
  221.9 7.2 collective-permute-start
  299.0 8.5 all-to-all-start.4
  371.6 54.0 %all-to-all-start.6 = ((bf16[32,5,8,1536]{3,2,1,0:T(8,128)(2,1)}), bf16[32,5,8,1536]{3,2,1,0:T(8,128)(2,1)}, u32[]{:S(2)}, u32[]{:S(2)}) async-start(bf16[32,5,8,1536]{3,2,1,0:T(8,128)(2,1)} %copy.676), calls=%async_computation.6 | async-start | bytes 7864320 | tf_op jit(solution)/shard_map/all_to_all | solution.py:268
  376.5 125.2 %all-gather.8.cloned.1.call-start = ((), (), s32[]{:S(2)}) async-start(), calls=%async_computation.29 | async-start | bytes 2162688 | tf_op jit(solution)/shard_map/all_gather | solution.py:19
  443.6 7.2 collective-permute-start.1
  517.1 8.0 all-to-all-start.8
  534.6 37.5 %all-to-all-start.9 = ((bf16[32,3,8,1536]{3,2,1,0:T(8,128)(2,1)}), bf16[32,3,8,1536]{3,2,1,0:T(8,128)(2,1)}, u32[]{:S(2)}, u32[]{:S(2)}) async-start(bf16[32,3,8,1536]{3,2,1,0:T(8,128)(2,1)} %bitcast.1331), calls=%async_computation.9 | async-start | bytes 4718592 | tf_op jit(solution)/shard_map/all_to_all | solution.py:256
  572.0 36.5 %all-to-all-start.12 = ((bf16[32,3,8,1536]{3,2,1,0:T(8,128)(2,1)}), bf16[32,3,8,1536]{3,2,1,0:T(8,128)(2,1)}, u32[]{:S(2)}, u32[]{:S(2)}) async-start(bf16[32,3,8,1536]{3,2,1,0:T(8,128)(2,1)} %bitcast.1332), calls=%async_computation.12 | async-start | bytes 4718592 | tf_op jit(solution)/shard_map/all_to_all | solution.py:359
  634.3 36.7 %all-to-all-start.13 = ((bf16[32,3,8,1536]{3,2,1,0:T(8,128)(2,1)}), bf16[32,3,8,1536]{3,2,1,0:T(8,128)(2,1)}, u32[]{:S(2)}, u32[]{:S(2)}) async-start(bf16[32,3,8,1536]{3,2,1,0:T(8,128)(2,1)} %copy.701), calls=%async_computation.13 | async-start | bytes 4718592 | tf_op jit(solution)/shard_map/all_to_all | solution.py:386
  671.1 54.7 %all-to-all-start.10 = ((bf16[32,5,8,1536]{3,2,1,0:T(8,128)(2,1)}), bf16[32,5,8,1536]{3,2,1,0:T(8,128)(2,1)}, u32[]{:S(2)}, u32[]{:S(2)}) async-start(bf16[32,5,8,1536]{3,2,1,0:T(8,128)(2,1)} %copy.687), calls=%async_computation.10 | async-start | bytes 7864320 | tf_op jit(solution)/shard_map/all_to_all | solution.py:268
  745.4 7.1 all-to-all-start.14
  748.8 100.7 %reduce-scatter.10.cloned.1.call-start = ((), (), s32[]{:S(2)}) async-start(), calls=%async_computation.30 | async-start | bytes 2162688
  856.2 7.1 all-to-all-start.15
  866.2 6.9 collective-permute-start.2
  949.3 36.1 %all-to-all-start.17 = ((bf16[32,3,8,1536]{3,2,1,0:T(8,128)(2,1)}), bf16[32,3,8,1536]{3,2,1,0:T(8,128)(2,1)}, u32[]{:S(2)}, u32[]{:S(2)}) async-start(bf16[32,3,8,1536]{3,2,1,0:T(8,128)(2,1)} %copy.721), calls=%async_computation.17 | async-start | bytes 4718592 | tf_op jit(solution)/shard_map/all_to_all | solution.py:386
  1000.9 8.3 all-to-all-start.18
  1004.4 96.6 %reduce-scatter.12.cloned.1.call-start = ((), (), s32[]{:S(2)}) async-start(), calls=%async_computation.31 | async-start | bytes 2162688
  1107.7 7.1 all-to-all-start.19
  1117.6 6.9 collective-permute-start.3
  1134.5 41.3 %all-to-all-start.20 = ((bf16[32,3,8,1536]{3,2,1,0:T(8,128)(2,1)}), bf16[32,3,8,1536]{3,2,1,0:T(8,128)(2,1)}, u32[]{:S(2)}, u32[]{:S(2)}) async-start(bf16[32,3,8,1536]{3,2,1,0:T(8,128)(2,1)} %bitcast.1333), calls=%async_computation.20 | async-start | bytes 4718592 | tf_op jit(solution)/shard_map/all_to_all | solution.py:359
  1201.1 36.8 %all-to-all-start.21 = ((bf16[32,3,8,1536]{3,2,1,0:T(8,128)(2,1)}), bf16[32,3,8,1536]{3,2,1,0:T(8,128)(2,1)}, u32[]{:S(2)}, u32[]{:S(2)}) async-start(bf16[32,3,8,1536]{3,2,1,0:T(8,128)(2,1)} %copy.738), calls=%async_computation.21 | async-start | bytes 4718592 | tf_op jit(solution)/shard_map/all_to_all | solution.py:386
  1253.4 8.6 all-to-all-start.22
  1256.8 96.8 %reduce-scatter.14.cloned.1.call-start = ((), (), s32[]{:S(2)}) async-start(), calls=%async_computation.32 | async-start | bytes 2162688
  1279.8 197.0 %all-reduce.7.cloned.1.call-start = ((), (), s32[]{:S(2)}) async-start(), calls=%async_computation.33 | async-start | bytes 12828672 | tf_op jit(solution)/shard_map/psum | solution.py:506
  1358.8 278.6 %all-reduce.9.cloned.1.call-start = ((), (), s32[]{:S(2)}) async-start(), calls=%async_computation.34 | async-start | bytes 12042240 | tf_op jit(solution)/shard_map/psum | solution.py:520
  1480.7 7.1 all-to-all-start.11
  1495.5 9.8 all-to-all-start.23
  (249 other events, 3150.5 us)
Sparse Core Ops, SparseCore 0:
  16.6 47.5 all-gather.3
  234.8 47.8 all-gather.5
  453.7 47.8 all-gather.7
  770.4 79.0 reduce-scatter.9
  1027.2 73.7 reduce-scatter.11
  1279.9 73.7 reduce-scatter.13
  1358.9 117.8 all-reduce.6
  1480.3 157.1 all-reduce.8
where the time goes:
time: 1670 us; the launch traced here: 1650 us
  waiting for transfers between devices  719 us (43%)
  matrix products  238 us (14%)
  local copies, waits for them, and re-layouts  237 us (14%)
  other arithmetic  170 us (10%)
  blocking collectives  163 us (10%)
  starting transfers between devices  109 us (7%)
  between operations  18.5 us (1%)
    unnamed x11, waiting for transfers between devices  190 us
    all_gather x3, waiting for transfers between devices, in_one_piece(): lax.all_gather(both, axis, axis=dim, tiled=True)  112 us
    all_to_all x3, waiting for transfers between devices, body(): lax.all_to_all(block_out, 'ep', split_axis=0, concat_axis=0, tiled=True)  111 us
    psum x1, waiting for transfers between devices, body(): lax.psum(totals[1].astype(jnp.bfloat16), 'ep').astype(jnp.float32)  78.5 us
    psum x1, blocking collectives, body(): lax.psum(totals[0].astype(jnp.bfloat16), 'ep').astype(jnp.float32)  65.9 us
    all_to_all x3, waiting for transfers between devices, body(): lax.all_to_all(outgoing.astype(jnp.bfloat16), 'ep', split_axis=0, concat_...  63.6 us
    unnamed x511, local copies, waits for them, and re-layouts  46.1 us
    psum x1, waiting for transfers between devices, body(): lax.psum(ep_sums[6].astype(jnp.bfloat16), 'tp').astype(jnp.float32)  44.8 us
  transfers between devices with their start and end apart: 32, of which 30 were waited for; matrix products, arithmetic and copies ran while one was open for 16% of the time, Pallas kernels for 0%

commit v1 on v0

v1 whole, which is shorter than its diff:
```python
import jax
import jax.numpy as jnp
import numpy as np
from jax import lax
from jax.experimental import pallas as pl
from jax.experimental.pallas import tpu as pltpu
from jax.sharding import PartitionSpec as P

HEAD = 64
TOPK = 8
BLOCK = 128
EXPERT_BLOCKS = 4
SIDE = 4
CHIPS = SIDE * SIDE
LANES = 128
SLOTS = 8
GROUP = 32
epsilon = 1e-05
bf16 = jnp.bfloat16
f32 = jnp.float32


def nn(a, b):
    return lax.dot_general(a, b, (((1,), (0,)), ((), ())), preferred_element_type=f32)


def nt(a, b):
    return lax.dot_general(a, b, (((1,), (1,)), ((), ())), preferred_element_type=f32)


def tn(a, b):
    return lax.dot_general(a, b, (((0,), (0,)), ((), ())), preferred_element_type=f32)


def iota(shape, dim):
    return lax.broadcasted_iota(jnp.int32, shape, dim)


def whole_spec(shape, **more):
    return pl.BlockSpec(shape, lambda m: (0,) * len(shape), **more)


def micro_spec(shape):
    return pl.BlockSpec((None, *shape), lambda m: (m, *(0,) * len(shape)))


def local_call(kernel, outs, operands, scratch=(), flops=0, smem=0, vmem=40, each=(), sums=(), micros=1):
    each = list(each)
    moved = sum(int(np.prod(v.shape)) * v.dtype.itemsize for v in [*operands, *each])
    moved += sum(micros * int(np.prod(s)) * jnp.dtype(d).itemsize for s, d in outs)
    params = dict(
        scratch_shapes=[pltpu.VMEM(s, d) for s, d in scratch],
        compiler_params=pltpu.CompilerParams(vmem_limit_bytes=vmem * 1024 * 1024),
        cost_estimate=pl.CostEstimate(flops=flops, bytes_accessed=moved, transcendentals=0),
    )
    scalars = [pl.BlockSpec(memory_space=pltpu.SMEM)] * smem
    if not each:
        return pl.pallas_call(
            kernel,
            out_shape=[jax.ShapeDtypeStruct(s, d) for s, d in outs],
            in_specs=scalars + [pl.BlockSpec(memory_space=pltpu.VMEM)] * (len(operands) - smem),
            out_specs=[pl.BlockSpec(memory_space=pltpu.VMEM)] * len(outs),
            **params,
        )(*operands)
    return pl.pallas_call(
        kernel,
        grid=(micros,),
        out_shape=[jax.ShapeDtypeStruct((micros, *s), d) for s, d in outs]
        + [jax.ShapeDtypeStruct(s, d) for s, d in sums],
        in_specs=scalars
        + [whole_spec(v.shape, pipeline_mode=pl.Buffered(1)) for v in operands[smem:]]
        + [micro_spec(v.shape[1:]) for v in each],
        out_specs=[micro_spec(s) for s, d in outs] + [whole_spec(s) for s, d in sums],
        **params,
    )(*operands, *each)


def turn(values, cosine, sine):
    lane = iota(values.shape, 1) % HEAD
    partner = jnp.where(
        lane < HEAD // 2,
        pltpu.roll(values, LANES - HEAD // 2, 1),
        pltpu.roll(values, HEAD // 2, 1),
    )
    return values * cosine + partner * sine


def project_kernel(x_ref, gain_ref, w_ref, cos_ref, sin_ref, a_ref, q_ref, kv_ref):
    x = x_ref[...].astype(f32)
    root = lax.rsqrt(jnp.mean(x * x, axis=-1, keepdims=True) + epsilon)
    a = (x * root * gain_ref[...]).astype(bf16)
    a_ref[...] = a
    both = nn(a, w_ref[...])
    cosine, sine = cos_ref[...], sin_ref[...]
    for i in range(3):
        at = slice(i * LANES, (i + 1) * LANES)
        q_ref[:, at] = turn(both[:, at], cosine, sine).astype(bf16)
    kv_ref[:, :LANES] = turn(both[:, 3 * LANES : 4 * LANES], cosine, sine).astype(bf16)
    kv_ref[:, LANES:] = both[:, 4 * LANES :].astype(bf16)


def head_rows(values, j):
    pair = values[:, j // 2 * LANES : (j // 2 + 1) * LANES]
    if j % 2 != j // 3:
        pair = pltpu.roll(pair, HEAD, 1)
    low = iota(pair.shape, 1) < HEAD
    return jnp.where(low if j < 3 else jnp.logical_not(low), pair, 0.0)


def spread_heads(source_ref, target_ref, scale):
    rows = source_ref.shape[0]
    values = source_ref[...].astype(f32)
    for j in range(6):
        target_ref[j * rows : (j + 1) * rows, :] = (head_rows(values, j) * scale).astype(bf16)


def join_heads(wide, rows):
    heads = []
    for j in range(6):
        at = HEAD if j >= 3 else 0
        heads.append(wide[at : at + HEAD, j * rows : (j + 1) * rows])
    return [jnp.concatenate(heads[2 * p : 2 * p + 2], axis=0).T for p in range(3)]


def in_reach(row_ref, kb, rows, shape):
    ahead = iota((rows, shape[1]), 1) % rows - iota((rows, shape[1]), 0)
    count = shape[0] // rows
    parts = [ahead + (row_ref[0] - row_ref[1 + kb * count + i]) >= 0 for i in range(count)]
    return jnp.concatenate(parts, axis=0)


def attend_kernel(
    row_ref, wo_ref, q_ref, kv0, kv1, kv2, kv3, o_ref, l_ref, y_ref, qp, st
):
    rows = q_ref.shape[0]
    step = kv0.shape[0]
    spread_heads(q_ref, qp, 0.125)
    peak = None
    for kb, kv_ref in enumerate((kv0, kv1, kv2, kv3)):
        s = nt(kv_ref[:, :LANES], qp[...])
        s = jnp.where(in_reach(row_ref, kb, rows, s.shape), s, -1e30)
        st[kb * step : (kb + 1) * step, :] = s
        top = jnp.max(s, axis=0, keepdims=True)
        peak = top if peak is None else jnp.maximum(peak, top)
    total, wide = 0.0, 0.0
    for kb, kv_ref in enumerate((kv0, kv1, kv2, kv3)):
        p = jnp.exp(st[kb * step : (kb + 1) * step, :] - peak)
        total = total + jnp.sum(p, axis=0, keepdims=True)
        wide = wide + tn(kv_ref[:, LANES:], p.astype(bf16))
    wide = wide / total
    l_ref[...] = jnp.broadcast_to(peak + jnp.log(total), l_ref.shape)
    for p, part in enumerate(join_heads(wide, rows)):
        o_ref[:, p * LANES : (p + 1) * LANES] = part.astype(bf16)
    y_ref[...] = nn(o_ref[...], wo_ref[...]).astype(bf16)


def attend_back_kernel(
    row_ref, wo_ref, cos_ref, sin_ref, q_ref, kv0, kv1, kv2, kv3, da_ref, l_ref, o_ref,
    dq_ref, dkv0, dkv1, dkv2, dkv3, qp, dp, dob, prod,
):
    rows = q_ref.shape[0]
    spread_heads(q_ref, qp, 0.125)
    dob[...] = nt(da_ref[...], wo_ref[...]).astype(bf16)
    spread_heads(dob, dp, 1.0)
    both = dob[...].astype(f32) * o_ref[...].astype(f32)
    for j in range(6):
        prod[j * rows : (j + 1) * rows, :] = head_rows(both, j)
    inner = lax.dot_general(
        jnp.ones((8, LANES), f32),
        prod[...],
        (((1,), (1,)), ((), ())),
        precision=lax.Precision.HIGHEST,
        preferred_element_type=f32,
    )[0:1, :]
    log_total = l_ref[0:1, :]
    wide = 0.0
    for kb, (kv_ref, dkv_ref) in enumerate(((kv0, dkv0), (kv1, dkv1), (kv2, dkv2), (kv3, dkv3))):
        keys_here, values_here = kv_ref[:, :LANES], kv_ref[:, LANES:]
        s = nt(keys_here, qp[...])
        p = jnp.where(in_reach(row_ref, kb, rows, s.shape), jnp.exp(s - log_total), 0.0)
        ds = (p * (nt(values_here, dp[...]) - inner)).astype(bf16)
        dkv_ref[:, :LANES] = nn(ds, qp[...]).astype(bf16)
        dkv_ref[:, LANES:] = nn(p.astype(bf16), dp[...]).astype(bf16)
        wide = wide + tn(keys_here, ds)
    for p, part in enumerate(join_heads(wide * 0.125, rows)):
        dq_ref[:, p * LANES : (p + 1) * LANES] = turn(part, cos_ref[...], -sin_ref[...]).astype(bf16)


def after_keys_kernel(
    dkv0, dkv1, dkv2, dkv3, dq_ref, x_ref, w_ref, cos_ref, sin_ref, g_ref, y_ref, gain_ref
):
    whole = dkv0[...].astype(f32) + dkv1[...].astype(f32)
    whole = whole + (dkv2[...].astype(f32) + dkv3[...].astype(f32))
    g_ref[:, : 3 * LANES] = dq_ref[...]
    g_ref[:, 3 * LANES : 4 * LANES] = turn(whole[:, :LANES], cos_ref[...], -sin_ref[...]).astype(bf16)
    g_ref[:, 4 * LANES :] = whole[:, LANES:].astype(bf16)
    y = nt(g_ref[...], w_ref[...])
    y_ref[...] = y.astype(bf16)
    x = x_ref[...].astype(f32)
    root = lax.rsqrt(jnp.mean(x * x, axis=-1, keepdims=True) + epsilon)
    gain_ref[...] = jnp.broadcast_to(jnp.sum(y * (x * root), axis=0, keepdims=True), gain_ref.shape)


CHUNK = 256
HALF = CHUNK // GROUP * SLOTS


def picks(tgt_ref, ch):
    at = slice(ch * CHUNK, (ch + 1) * CHUNK)
    rows = iota((HALF, CHUNK), 0)
    return rows == tgt_ref[0:1, at], rows == tgt_ref[1:2, at]


def one_hot(pick_a, pick_b):
    return jnp.concatenate([pick_a.astype(f32), pick_b.astype(f32)], axis=0).astype(bf16)


def row_of(table, expert):
    return jnp.sum(jnp.where(iota(table.shape, 0) == expert, table, 0.0), axis=0, keepdims=True)


def two_of(refs, ch):
    return jnp.concatenate([refs[2 * ch][...], refs[2 * ch + 1][...]], axis=0)


def put_two(refs, ch, value):
    rows = value.shape[0] // 2
    refs[2 * ch][...] = value[:rows]
    refs[2 * ch + 1][...] = value[rows:]


def experts_kernel(s_ref, router, wg, wu, wd, *refs):
    tokens_in, refs = refs[: 2 * SIDE], refs[2 * SIDE :]
    tgt, mask, *refs = refs
    tokens_out, refs = refs[: 2 * SIDE], refs[2 * SIDE :]
    gates, slots_in, g_ref, u_ref, hidden, weights, scaled = refs
    chunks = SIDE
    for ch in range(chunks):
        at = slice(ch * CHUNK, (ch + 1) * CHUNK)
        z = nt(router[...], two_of(tokens_in, ch))
        chosen = mask[:, at]
        z = jnp.where(chosen > 0.0, z, -1e30)
        e = jnp.exp(z - jnp.max(z, axis=0, keepdims=True)) * chosen
        gates[:, at] = e / jnp.sum(e, axis=0, keepdims=True)
    rows = slots_in.shape[0] // 2
    for ch in range(chunks):
        pick_a, pick_b = picks(tgt, ch)
        got = nn(one_hot(pick_a, pick_b), two_of(tokens_in, ch)).astype(bf16)
        here = gates[:, ch * CHUNK : (ch + 1) * CHUNK]
        for which, pick in enumerate((pick_a, pick_b)):
            at = which * rows + ch * HALF
            slots_in[at : at + HALF, :] = got[which * HALF : (which + 1) * HALF]
            weight = jnp.sum(jnp.where(pick, row_of(here, s_ref[which]), 0.0), axis=1, keepdims=True)
            weights[at : at + HALF, :] = jnp.broadcast_to(weight, (HALF, LANES))
    hidden[...] = jnp.zeros_like(hidden)
    for k in range(wg.shape[1] // BLOCK):
        at = slice(k * BLOCK, (k + 1) * BLOCK)
        here = pl.ds(pl.multiple_of(s_ref[2 + k] * rows, rows), rows)
        both = nn(slots_in[here, :], jnp.concatenate([wg[:, at], wu[:, at]], axis=1))
        g, u = both[:, :BLOCK], both[:, BLOCK:]
        g_ref[:, at] = g
        u_ref[:, at] = u
        hidden[here, at] = (g * jax.nn.sigmoid(g) * u).astype(bf16)
    for at in range(0, wd.shape[1], CHUNK):
        part = nn(hidden[...], wd[:, at : at + CHUNK])
        scaled[:, at : at + CHUNK] = (part * weights[:, 0:1]).astype(bf16)
    for ch in range(chunks):
        at = ch * HALF
        both = jnp.concatenate([scaled[at : at + HALF], scaled[rows + at : rows + at + HALF]], axis=0)
        put_two(tokens_out, ch, tn(one_hot(*picks(tgt, ch)), both).astype(bf16))


def experts_back_kernel(s_ref, router, wg, wu, wd, *refs):
    grads_in, refs = refs[: 2 * SIDE], refs[2 * SIDE :]
    tokens_in, refs = refs[: 2 * SIDE], refs[2 * SIDE :]
    tgt, gates, g_ref, u_ref, *refs = refs
    grads_out, refs = refs[: 2 * SIDE], refs[2 * SIDE :]
    dgu_ref, h_ref, dy, router_grad, inner, back = refs
    chunks = SIDE
    rows = dy.shape[0] // 2
    for ch in range(chunks):
        pick_a, pick_b = picks(tgt, ch)
        here = gates[:, ch * CHUNK : (ch + 1) * CHUNK]
        got = nn(one_hot(pick_a, pick_b), two_of(grads_in, ch))
        for which, pick in enumerate((pick_a, pick_b)):
            weight = jnp.sum(jnp.where(pick, row_of(here, s_ref[which]), 0.0), axis=1, keepdims=True)
            at = which * rows + ch * HALF
            dy[at : at + HALF, :] = (got[which * HALF : (which + 1) * HALF] * weight).astype(bf16)
    inner[...] = jnp.zeros_like(inner)
    back[...] = jnp.zeros_like(back)
    for k in range(wg.shape[1] // BLOCK):
        at = slice(k * BLOCK, (k + 1) * BLOCK)
        here = pl.ds(pl.multiple_of(s_ref[2 + k] * rows, rows), rows)
        dh = nt(dy[here, :], wd[at, :])
        g, u = g_ref[:, at], u_ref[:, at]
        sig = jax.nn.sigmoid(g)
        swish = g * sig
        h = (swish * u).astype(bf16)
        h_ref[:, at] = h
        inner[here, :] += jnp.broadcast_to(
            jnp.sum(h.astype(f32) * dh, axis=1, keepdims=True), (rows, LANES)
        )
        dg = (dh * u * sig * (1.0 + g * (1.0 - sig))).astype(bf16)
        du = (dh * swish).astype(bf16)
        both = jnp.concatenate([dg, du], axis=1)
        dgu_ref[:, 2 * k * BLOCK : 2 * (k + 1) * BLOCK] = both
        back[here, :] += nt(both, jnp.concatenate([wg[:, at], wu[:, at]], axis=1))
    for ch in range(chunks):
        pick_a, pick_b = picks(tgt, ch)
        span = slice(ch * CHUNK, (ch + 1) * CHUNK)
        sums = []
        for which, pick in enumerate((pick_a, pick_b)):
            at = which * rows + ch * HALF
            column = inner[at : at + HALF, 0:1]
            sums.append(jnp.sum(jnp.where(pick, column, 0.0), axis=0, keepdims=True))
        table = gates[:, span]
        expert = iota(table.shape, 0)
        dz = jnp.where(expert == s_ref[0], sums[0], 0.0) + jnp.where(expert == s_ref[1], sums[1], 0.0)
        dz = dz - table * (sums[0] + sums[1])
        high = dz.astype(bf16)
        lower = (dz - high.astype(f32)).astype(bf16)
        both = jnp.concatenate([high, lower], axis=0)
        at = ch * HALF
        moved = jnp.concatenate([back[at : at + HALF, :], back[rows + at : rows + at + HALF, :]], axis=0)
        value = tn(
            jnp.concatenate([one_hot(pick_a, pick_b), high], axis=0),
            jnp.concatenate([moved.astype(bf16), router[...]], axis=0),
        )
        put_two(grads_out, ch, value.astype(bf16))
        part = nn(both, two_of(tokens_in, ch))
        part = part[: table.shape[0]] + part[table.shape[0] :]
        if ch == 0:
            begin = pl.program_id(0) == 0
            router_grad[...] = part + jnp.where(begin, 0.0, router_grad[...])
        else:
            router_grad[...] += part


def expert_weights_kernel(s_ref, b_own, o0, o1, o2, o3, g_own, g_other, h, dy, gate, up, down):
    rows, size = h.shape[0], o0.shape[0]
    begin = pl.program_id(0) == 0
    for k in range(h.shape[1] // BLOCK):
        at = slice(k * BLOCK, (k + 1) * BLOCK)
        wide = slice(2 * k * BLOCK, 2 * (k + 1) * BLOCK)
        here = pl.ds(pl.multiple_of(s_ref[2 + k] * rows, rows), rows)
        first = s_ref[2 + k] == 0
        theirs = [jnp.where(first, o0[...], o2[...]), jnp.where(first, o1[...], o3[...])]
        both = tn(
            jnp.concatenate([b_own[here, :], *theirs], axis=0),
            jnp.concatenate([g_own[:, wide], g_other[:, wide]], axis=0),
        )
        low = tn(h[:, at], dy[here, :])
        gate[:, at] = both[:, :BLOCK] + jnp.where(begin, 0.0, gate[:, at])
        up[:, at] = both[:, BLOCK:] + jnp.where(begin, 0.0, up[:, at])
        down[at, :] = low + jnp.where(begin, 0.0, down[at, :])


def ring(stage, steps):
    pairs = []
    for x in range(SIDE):
        for z in range(SIDE):
            for core in range(2):
                along_x = (core == 0) == (stage == 0)
                to = ((x + steps) % SIDE, z) if along_x else (x, (z + steps) % SIDE)
                pairs.append(((x * SIDE + z) * 2 + core, (to[0] * SIDE + to[1]) * 2 + core))
    return pairs


def other_core(value):
    return lax.ppermute(value, "ep", [(i, i ^ 1) for i in range(2 * CHIPS)])


def other_half(value):
    return lax.ppermute(value, "tp", [(0, 1), (1, 0)])


def other_both(value):
    pairs = [(2 * i + t, 2 * (i ^ 1) + 1 - t) for i in range(2 * CHIPS) for t in range(2)]
    return lax.ppermute(value, ("ep", "tp"), pairs)


def in_order(own, other, place, dim):
    return jnp.concatenate(
        [jnp.where(place == 0, own, other), jnp.where(place == 0, other, own)], axis=dim
    )


def from_ring(value, stage):
    return [value] + [lax.ppermute(value, "ep", ring(stage, -d)) for d in range(1, SIDE)]


def to_ring(pieces, stage):
    return [pieces[0]] + [
        lax.ppermute(pieces[d], "ep", ring(stage, d)) for d in range(1, SIDE)
    ]


def everyone(value):
    return from_ring(jnp.concatenate(from_ring(value, 0), axis=1), 1)


def added(pieces):
    pieces = [p.astype(f32) for p in pieces]
    return (pieces[0] + pieces[1]) + (pieces[2] + pieces[3])


def pieces_of(value):
    size = value.shape[1] // SIDE
    return [value[:, d * size : (d + 1) * size] for d in range(SIDE)]


def to_owners(pieces, beside=()):
    joined, *beside = pin(added(to_ring(pieces, 1)).astype(bf16), *beside)
    return to_ring(pieces_of(joined), 0), beside


def pin(*values):
    return lax.optimization_barrier(values)


SAME_CORE = [[2 * chip + core for chip in range(CHIPS)] for core in range(2)]


def exchange(pieces, groups=SAME_CORE):
    return lax.all_to_all(pieces, "ep", 0, 0, tiled=True, axis_index_groups=groups)


def broadcast(value, count=CHIPS, groups=SAME_CORE):
    return exchange(jnp.broadcast_to(value[None], (count, *value.shape)), groups)


def half_of(value, place, dim=0):
    size = value.shape[dim] // 2
    mine = lax.dynamic_slice_in_dim(value, place * size, size, dim)
    rest = lax.dynamic_slice_in_dim(value, (1 - place) * size, size, dim)
    return mine, rest


def body(
    x_in, cotangent, norm1_gain, wq, wk, wv, wo, norm2_gain, router, w_gate, w_up, w_down, routes
):
    section = lax.axis_index("section")
    rank = lax.axis_index("ep")
    half = lax.axis_index("tp")
    chip, core = rank // 2, rank % 2
    x, z = chip // SIDE, chip % SIDE
    micros, core_rows, width = x_in.shape
    own_rows = core_rows // 2
    chip_rows = core_rows * 2
    length = chip_rows * CHIPS
    experts = router.shape[2]
    blocks = w_gate.shape[2] // BLOCK
    gain_one = norm1_gain.reshape(1, width)
    gain_two = norm2_gain.reshape(1, width)
    gate_w, up_w, down_w = w_gate[0], w_up[0], w_down[0]
    expert_rows = -(-experts // 16) * 16
    router_t = jnp.pad(router[0].T, ((0, expert_rows - experts), (0, 0)))

    qkv_w = jnp.concatenate([half_of(w[0], core, 1)[0] for w in (wq, wk, wv)], axis=1)
    out_w = half_of(wo[0], core)[0]

    first_row = (chip * chip_rows).astype(jnp.int32)
    positions = (first_row + jnp.arange(chip_rows, dtype=jnp.int32)).astype(f32)
    quarter = HEAD // 2
    frequency = 10000.0 ** (-jnp.arange(quarter, dtype=f32) * 2.0 / HEAD)
    phase = positions[:, None] * frequency[None, :]
    cosine = jnp.tile(jnp.cos(phase), (1, 4))
    sine = jnp.concatenate([-jnp.sin(phase), jnp.sin(phase)] * 2, axis=1)

    def chips_met(which_core):
        inner, outer = jnp.arange(CHIPS) % SIDE, jnp.arange(CHIPS) // SIDE
        by_x = jnp.where(which_core == 0, inner, outer)
        by_z = jnp.where(which_core == 0, outer, inner)
        return ((x + by_x) % SIDE) * SIDE + (z + by_z) % SIDE

    row_scalars = jnp.concatenate(
        [first_row.reshape(1), chips_met(core) * chip_rows]
    ).astype(jnp.int32)

    first_expert = rank * blocks // EXPERT_BLOCKS
    which = (rank * blocks + jnp.arange(blocks)) // EXPERT_BLOCKS - first_expert
    scalars = jnp.concatenate(
        [jnp.stack([first_expert, first_expert + 1]), which]
    ).astype(jnp.int32)

    tokens = CHIPS * own_rows
    slot_rows = 2 * 2 * CHIPS * SLOTS
    hidden_width = blocks * BLOCK
    both_rows = micros * chip_rows
    cosines, sines = jnp.tile(cosine, (micros, 1)), jnp.tile(sine, (micros, 1))

    def prepare(own_routes):
        all_routes = broadcast(own_routes.reshape(-1, LANES), 2 * CHIPS, None)
        met = jnp.concatenate([chips_met(core) * 2 + core, chips_met(1 - core) * 2 + 1 - core])
        all_routes = jnp.take(all_routes, met, axis=0)
        both_routes = all_routes.reshape(2 * CHIPS, micros, own_rows, TOPK).transpose(1, 0, 2, 3)
        both_routes = both_routes.reshape(micros, 2 * CHIPS * own_rows, TOPK)
        named = (
            both_routes[:, None, :, :] == jnp.arange(expert_rows, dtype=jnp.int32)[None, :, None, None]
        )
        masks = jnp.any(named, axis=-1).astype(f32)
        wanted = jnp.stack([first_expert, first_expert + 1]).astype(jnp.int32)
        hits = jnp.any(both_routes[:, None, :, :] == wanted[None, :, None, None], axis=-1)
        hits = hits.reshape(micros, 2, 2 * CHIPS, own_rows).astype(jnp.int32)
        before = jnp.cumsum(hits, axis=-1) - hits
        base = (jnp.arange(2 * CHIPS, dtype=jnp.int32) % (CHUNK // GROUP)) * SLOTS
        targets = jnp.where(hits > 0, base[None, None, :, None] + before, -1)
        targets = targets.reshape(micros, 2, 2 * CHIPS * own_rows)
        return targets, masks

    def project(x128):
        a, q, kv = local_call(
            project_kernel,
            [((both_rows, width), bf16), ((both_rows, 3 * LANES), bf16), ((both_rows, 2 * LANES), bf16)],
            [x128.reshape(both_rows, width), gain_one, qkv_w, cosines, sines],
            flops=2 * both_rows * width * 5 * LANES,
            vmem=16,
        )
        return a, q.reshape(micros, chip_rows, -1), kv.reshape(micros, chip_rows, -1)

    def attend(q, kv):
        return local_call(
            attend_kernel,
            [((chip_rows, 3 * LANES), bf16), ((8, 6 * chip_rows), f32), ((chip_rows, width), bf16)],
            [row_scalars, out_w],
            each=[q, *kv],
            scratch=[((6 * chip_rows, LANES), bf16), ((length, 6 * chip_rows), f32)],
            flops=8 * micros * length * 6 * chip_rows * LANES,
            smem=1,
            vmem=32,
            micros=micros,
        )

    def attend_back(q, kv, grad, log_total, o):
        return local_call(
            attend_back_kernel,
            [((chip_rows, 3 * LANES), bf16)] + [((length // SIDE, 2 * LANES), bf16)] * SIDE,
            [row_scalars, out_w, cosine, sine],
            each=[q, *kv, grad, log_total, o],
            scratch=[
                ((6 * chip_rows, LANES), bf16),
                ((6 * chip_rows, LANES), bf16),
                ((chip_rows, 3 * LANES), bf16),
                ((6 * chip_rows, LANES), f32),
            ],
            flops=20 * micros * length * 6 * chip_rows * LANES,
            smem=1,
            vmem=32,
            micros=micros,
        )

    def after_keys(arrived, dq, x128):
        dqkv, y, gain = local_call(
            after_keys_kernel,
            [((both_rows, 5 * LANES), bf16), ((both_rows, width), bf16), ((8, width), f32)],
            [v.reshape(both_rows, -1) for v in (*arrived, dq, x128)] + [qkv_w, cosines, sines],
            flops=2 * both_rows * width * 5 * LANES,
            vmem=16,
        )
        return dqkv, y.reshape(micros, chip_rows, width), gain[:1]

    piece = ((tokens // SIDE, width), bf16)

    def run_experts(arrived):
        result = local_call(
            experts_kernel,
            [piece] * (2 * SIDE)
            + [
                ((expert_rows, 2 * tokens), f32),
                ((slot_rows, width), bf16),
                ((slot_rows // 2, hidden_width), f32),
                ((slot_rows // 2, hidden_width), f32),
            ],
            [scalars, router_t, gate_w, up_w, down_w],
            each=[*arrived, targets, masks],
            scratch=[
                ((slot_rows, hidden_width), bf16),
                ((slot_rows, LANES), f32),
                ((slot_rows, width), bf16),
            ],
            flops=10 * micros * slot_rows * hidden_width * width,
            smem=1,
            vmem=48,
            micros=micros,
        )
        return result[: 2 * SIDE], result[2 * SIDE :]

    def run_experts_back(grads, arrived, gates, g, u):
        result = local_call(
            experts_back_kernel,
            [piece] * (2 * SIDE)
            + [
                ((slot_rows // 2, 2 * hidden_width), bf16),
                ((slot_rows // 2, hidden_width), bf16),
                ((slot_rows, width), bf16),
            ],
            [scalars, router_t, gate_w, up_w, down_w],
            each=[*grads, *arrived, targets, gates, g, u],
            sums=[((expert_rows, width), f32)],
            scratch=[((slot_rows, LANES), f32), ((slot_rows, width), f32)],
            flops=10 * micros * slot_rows * hidden_width * width,
            smem=1,
            vmem=52,
            micros=micros,
        )
        return result[: 2 * SIDE], result[2 * SIDE :]

    def sum_four(part):
        mine, rest = half_of(part, core, 1)
        mine, rest = half_of(mine.astype(f32) + other_core(rest).astype(f32), half, 1)
        return mine + other_half(rest.astype(bf16)).astype(f32)

    def to_four(rows32):
        rows64 = in_order(rows32, other_half(rows32), half, 1)
        return in_order(rows64, other_core(rows64), core, 1)

    def tokens_out(rows32):
        arrived = everyone(rows32)
        return arrived + [other_core(p) for p in arrived]

    def over_cores(parts):
        return [
            (own.astype(f32) + other_core(other).astype(f32)).astype(bf16)
            for own, other in zip(parts[:SIDE], parts[SIDE:])
        ]

    def tokens_back(parts, beside=()):
        pieces, beside = to_owners(over_cores(parts), beside)
        return added(pieces), beside

    def inverse_root(values):
        return lax.rsqrt(jnp.mean(values * values, axis=-1, keepdims=True) + epsilon)

    def norm_back(values, root, gradient, gain):
        weighted = gradient * gain
        return root * weighted - values * root**3 * jnp.mean(weighted * values, axis=-1, keepdims=True)

    def forward(own, x128, sent=None):
        nonlocal targets, masks
        a, q, kv = project(x128)
        if sent is not None:
            kv, own_routes = pin(
                kv, lax.dynamic_slice_in_dim(routes[0], half * own_rows, own_rows, 1)
            )
            targets, masks = prepare(own_routes)
        kv_all = everyone(kv)
        if sent is not None:
            *kv_all, targets, masks = pin(*kv_all, targets, masks)
        o, log_total, y = attend(q, kv_all)
        residual = own.astype(f32) + sum_four(y)
        mixed = (residual * inverse_root(residual) * gain_two).astype(bf16)
        arrived = tokens_out(mixed if sent is None else jnp.where(section == 0, mixed, sent))
        parts, rest = run_experts(arrived)
        return parts, (own, x128, a, q, kv_all, o, log_total, residual, arrived, *rest)

    def backward(grad_rows, grads, kept, first=(), second=()):
        residual, arrived, gates, _, g, u = kept[7:]
        parts, (dgu, h, dy, router_grad) = run_experts_back(grads, arrived, gates, g, u)
        *parts, first = pin(*parts, first)
        if second:
            *parts, rows = pin(*parts, second[0])
            second = [other_half(rows)]
        mixed_grad, second = tokens_back(parts, second)
        root = inverse_root(residual)
        gain_two_grad = jnp.sum(mixed_grad * residual * root, axis=(0, 1))
        resid_grad = grad_rows.astype(f32) + norm_back(residual, root, mixed_grad, gain_two)
        return resid_grad, (dgu, h, dy), router_grad, gain_two_grad, [first, *second]

    targets = masks = None
    own_x = lax.dynamic_slice_in_dim(x_in, half * own_rows, own_rows, 1)
    x128 = in_order(x_in, other_core(x_in), core, 1)
    parts, kept = forward(own_x, x128, cotangent)
    upper_grads = kept[8]
    out = (kept[7] + tokens_back(parts)[0]).astype(bf16)
    same = lax.ppermute(out, "section", [(0, 1)])
    rows64 = in_order(same, lax.ppermute(out, ("section", "tp"), [(0, 3), (1, 2)]), half, 1)
    whole = in_order(rows64, other_core(rows64), core, 1)
    last_parts, kept = forward(
        jnp.where(section == 0, own_x, same), jnp.where(section == 0, x128, whole)
    )
    own, x128, a, q, kv_all, o, log_total, residual = kept[:8]
    own, slots_in = own.astype(f32), kept[10]

    resid_grad, *_ = backward(cotangent, upper_grads, kept)
    low, *joined = pin(resid_grad.astype(bf16), *over_cores(last_parts))
    pieces = to_ring(joined, 1)
    dq, *dkv = attend_back(q, kv_all, to_four(low), log_total, o)
    *dkv, joined = pin(*dkv, added(pieces).astype(bf16))
    dkv, _ = to_owners(dkv)
    *dkv, joined = pin(*dkv, joined)
    pieces = to_ring(pieces_of(joined), 0)
    _, y, _ = after_keys(dkv, dq, x128)
    normed_grad, out = pin(sum_four(y), (residual + added(pieces)).astype(bf16))
    root = inverse_root(own)
    upper = (resid_grad + norm_back(own, root, normed_grad, gain_one)).astype(bf16)
    coming = lax.ppermute(upper, "section", [(1, 0)])
    coming, other_out = pin(jnp.where(section == 0, coming, cotangent), other_half(out))
    activations = in_order(out, other_out, half, 1)

    size = slot_rows // SIDE
    other_slots = []

    def next_slots(*values):
        at = len(other_slots) * size
        *values, rows = pin(*values, slots_in[:, at : at + size])
        other_slots.append(other_half(rows))
        return values

    def slots_done(*values):
        *values, other_slots[-1] = pin(*values, other_slots[-1])
        return values

    (coming,) = next_slots(coming)
    arrived = from_ring(coming, 0)
    (arrived,) = next_slots(*slots_done(jnp.concatenate(arrived, axis=1)))
    arrived = next_slots(*slots_done(*from_ring(arrived, 1)))
    grads = arrived + [other_core(p) for p in arrived]
    resid_grad, (dgu, h, dy), router_grad, gain_two_grad, last_slots = backward(
        coming, grads, kept, other_slots[2], [slots_in[:, 3 * size :]]
    )
    other_slots[2:] = last_slots
    out_grad, dgu_sent = pin(to_four(resid_grad.astype(bf16)), dgu)
    other_dgu = other_half(dgu_sent)
    out_w_grad = tn(o.reshape(both_rows, -1), out_grad.reshape(both_rows, width)).astype(bf16)
    out_w_grad = jnp.sum(
        exchange(out_w_grad.reshape(CHIPS, -1, width)).astype(f32), axis=0
    ).astype(bf16)
    dq, *dkv = attend_back(q, kv_all, out_grad, log_total, o)
    *dkv, out_w_grad, other_dgu = pin(*dkv, out_w_grad, other_dgu)
    all_out = lax.all_gather(out_w_grad, "ep")
    q_grad = tn(a, dq.reshape(both_rows, -1)).astype(bf16).reshape(CHIPS, -1, 3 * LANES)
    q_grad = exchange(q_grad)
    gate_grad, up_grad, down_part = local_call(
        expert_weights_kernel,
        [],
        [scalars],
        each=[slots_in, *other_slots, dgu, other_dgu, h, dy],
        sums=[((width, hidden_width), f32), ((width, hidden_width), f32), ((hidden_width, width), f32)],
        flops=10 * slot_rows * hidden_width * width,
        smem=1,
        vmem=56,
        micros=micros,
    )
    down_part = down_part.astype(bf16)
    arrived, (gate_grad, up_grad, down_part, q_grad) = to_owners(
        dkv, (gate_grad, up_grad, down_part, q_grad)
    )
    other_down = other_half(down_part)
    q_grad = jnp.sum(q_grad.astype(f32), axis=0).astype(bf16)
    dqkv, y, gain_one_grad = after_keys(arrived, dq, x128)
    small = jnp.concatenate([router_grad[:experts], gain_one_grad, gain_two_grad[None]], axis=0)
    kv_width, all_width = 2 * LANES, 5 * LANES
    small_count = small.size
    per_chip = -(-small_count // (CHIPS * 8 * LANES)) * 8 * LANES
    small = jnp.pad(small.reshape(-1), (0, CHIPS * per_chip - small_count)).astype(bf16)
    kv_grad = tn(a, dqkv[:, 3 * LANES :]).astype(bf16).reshape(CHIPS, -1, kv_width)
    lines = kv_grad.shape[1]
    summed = exchange(
        jnp.concatenate([kv_grad, small.reshape(CHIPS, -1, kv_width)], axis=1)
    )
    summed, all_out, q_grad, y = pin(summed, all_out, q_grad, y)
    summed = jnp.sum(summed.astype(f32), axis=0).astype(bf16)
    small = jnp.pad(
        summed[lines:].reshape(-1, LANES), ((0, -per_chip // LANES % 5), (0, 0))
    ).reshape(-1, all_width)
    wide = jnp.concatenate(
        [jnp.concatenate([q_grad, summed[:lines]], axis=1), small], axis=0
    )
    normed_grad = sum_four(y)
    wide, normed_grad, other_down = pin(broadcast(wide), normed_grad, other_down)
    input_grads = (resid_grad + norm_back(own, root, normed_grad, gain_one)).astype(bf16)
    down_grad = down_part.astype(f32) + other_down.astype(f32)
    small = wide[:, lines:].reshape(CHIPS, -1)[:, :per_chip].reshape(-1)[:small_count]
    small = small.reshape(experts + 2, width)
    small = small.astype(f32) + other_core(small).astype(f32)
    small = small + other_half(small.astype(bf16)).astype(f32)
    wide = wide[:, :lines].reshape(width, all_width)
    other_wide = other_core(wide)

    def both_cores(start, end):
        return in_order(wide[:, start:end], other_wide[:, start:end], core, 1).astype(f32)

    grad_q = both_cores(0, 3 * LANES)
    grad_k = both_cores(3 * LANES, 4 * LANES)
    grad_v = both_cores(4 * LANES, 5 * LANES)
    all_out = all_out.reshape(CHIPS, 2, -1, width)
    grad_out = jnp.concatenate(
        [all_out[:, c].reshape(-1, width) for c in range(2)], axis=0
    ).astype(f32)
    return (
        activations[None],
        input_grads[None],
        small[experts][None],
        grad_q[None],
        grad_k[None],
        grad_v[None],
        grad_out[None],
        small[experts + 1][None],
        small[:experts].T[None],
        gate_grad[None],
        up_grad[None],
        down_grad[None],
    )


def solution(mesh):
    ep = "ep"
    ep_tp = ("ep", "tp")
    placed = (
        P(None, ep, None),
        P(None, ep_tp, None),
        P("section", None),
        P("section", None, "tp"),
        P("section", None, "tp"),
        P("section", None, "tp"),
        P("section", "tp", None),
        P("section", None),
        P("section", None, None),
        P("section", None, ep),
        P("section", None, ep),
        P("section", ep, None),
        P("section", None, ep, None),
    )
    return jax.shard_map(
        body,
        mesh=mesh,
        in_specs=placed,
        out_specs=(
            P("section", None, ep, None),
            P("section", None, ep_tp, None),
            P("section", None),
            P("section", None, "tp"),
            P("section", None, "tp"),
            P("section", None, "tp"),
            P("section", "tp", None),
            P("section", None),
            P("section", None, None),
            P("section", None, ep),
            P("section", None, ep),
            P("section", ep, None),
        ),
        check_vma=False,
    )
```

time: 1670 us -> 737 us (0.44)
  waiting for transfers between devices: 719 us -> 288 us
  matrix products: 238 us -> 5.81 us
  local copies, waits for them, and re-layouts: 237 us -> 48.3 us
  blocking collectives: 163 us -> 0 us
  Pallas kernels: 0 us -> 126 us
  other arithmetic: 170 us -> 54.7 us
  starting transfers between devices: 109 us -> 184 us
    all_to_all x20 -> x5, waiting for transfers between devices: 280 us -> 19.3 us  [exchange(): lax.all_to_all(pieces, 'ep', 0, 0, tiled=True, axis_index_groups=groups)]
    ppermute x4 -> x121, waiting for transfers between devices: 13 us -> 268 us  [the longest x36 104 us: to_ring(): lax.ppermute(pieces[d], 'ep', ring(stage, d))]
    dot_general x99 -> x3, matrix products: 238 us -> 5.81 us  [tn(): lax.dot_general(a, b, (((0,), (0,)), ((), ())), preferred_element_type=f32)]
    unnamed x11 -> x1, waiting for transfers between devices: 190 us -> 0.02 us
    ppermute x4 -> x121, starting transfers between devices: 11.9 us -> 157 us  [the longest x38 58.1 us: other_core(): return lax.ppermute(value, 'ep', [(i, i ^ 1) for i in range(2 * CHIPS)])]
    pallas_call x0 -> x13, Pallas kernels: none -> 126 us  [the longest x9 120 us: local_call(): pl.pallas_call(kernel, grid=(micros,), out_shape=[jax.ShapeDtypeStruct((m...]
    psum x2 -> x0, waiting for transfers between devices: 123 us -> none  [the longest x1 78.5 us: body(): lax.psum(totals[1].astype(jnp.bfloat16), 'ep').astype(jnp.float32)]
    all_gather x3 -> x1, waiting for transfers between devices: 112 us -> 0.01 us  [body(): all_out = lax.all_gather(out_w_grad, 'ep')]
  transfers between devices with their start and end apart: 32 -> 127, of which waited for: 30 -> 77; matrix products, arithmetic and copies ran while one was open for 16% -> 8% of each run, Pallas kernels for 0% -> 10%
where the time goes in v1:
time: 737 us; the launch traced here: 723 us
  waiting for transfers between devices  288 us (39%)
  starting transfers between devices  184 us (25%)
  Pallas kernels  126 us (17%)
  other arithmetic  54.7 us (7%)
  local copies, waits for them, and re-layouts  48.3 us (7%)
  between operations  16.8 us (2%)
    pallas_call x9, Pallas kernels, local_call(): pl.pallas_call(kernel, grid=(micros,), out_shape=[jax.ShapeDtypeStruct((m...  120 us
    ppermute x36, waiting for transfers between devices, to_ring(): lax.ppermute(pieces[d], 'ep', ring(stage, d))  104 us
    ppermute x30, waiting for transfers between devices, from_ring(): lax.ppermute(value, 'ep', ring(stage, -d))  86.7 us
    ppermute x38, starting transfers between devices, other_core(): return lax.ppermute(value, 'ep', [(i, i ^ 1) for i in range(2 * CHIPS)])  58.1 us
    ppermute x36, starting transfers between devices, to_ring(): lax.ppermute(pieces[d], 'ep', ring(stage, d))  43.8 us
    ppermute x14, waiting for transfers between devices, other_half(): return lax.ppermute(value, 'tp', [(0, 1), (1, 0)])  40.9 us
    ppermute x30, starting transfers between devices, from_ring(): lax.ppermute(value, 'ep', ring(stage, -d))  32 us
    unnamed x288, local copies, waits for them, and re-layouts  27.5 us
  transfers between devices with their start and end apart: 127, of which 77 were waited for; matrix products, arithmetic and copies ran while one was open for 8% of the time, Pallas kernels for 10%

profile of v1, /device:TPU:1, one launch (start us, length us, event | category | flops | bytes accessed | tf_op | source)
XLA Modules:
  0.0 723.4 jit_solution(7020319644570666257)
XLA Ops:
  23.6 7.5 %all-to-all-start = ((s32[32,4,128]{2,1,0:T(4,128)}), s32[32,4,128]{2,1,0:T(4,128)S(1)}, u32[]{:S(2)}, u32[]{:S(2)}) async-start(s32[32,4,128]{2,1,0:T(4,128)} %broadcast_in_dim.37), calls=%async_computation | async-start | bytes 131072 | tf_op jit(solution)/shard_map/all_to_all | solution.py:425
  32.6 5.9 all-to-all-done
  62.6 8.5 %shard_map.221 = (bf16[2,128,384]{2,1,0:T(8,128)(2,1)}, f32[2,8,768]{2,1,0:T(8,128)}, bf16[2,128,1536]{2,1,0:T(8,128)(2,1)S(1)}) custom-call(s32[17]{0:T(128)S(1)} %pad_add_fusion.row_ref, bf16[384,1536]{1,0:T(8,128)(2,1)S(1)} %copy-done.11, bf16[2,128,384]{2,1,0:T(8,128)(2,1)S(1)} %bitcast.133, bf16[2,512,256]{2,1,0:T(8,128)(2,1)S(1)} %copy-done.34, ...), custom_call_target="tpu_custom_call" | custom-call | flops 3221225472 | bytes 4505668 | tf_op jit(solution)/shard_map/pallas_call | solution.py:65
  99.2 6.2 collective-permute-done.12.refs_1_
  110.5 5.4 collective-permute-done.14.refs_3_
  121.7 16.6 %shard_map.222 = (bf16[2,128,1536]{2,1,0:T(8,128)(2,1)S(1)}, bf16[2,128,1536]{2,1,0:T(8,128)(2,1)S(1)}, bf16[2,128,1536]{2,1,0:T(8,128)(2,1)S(1)}, bf16[2,128,15...) custom-call(s32[7]{0:T(128)S(1)} %pad_add_fusion.2.s_ref, ...), custom_call_target="tpu_custom_call" | custom-call | flops 10066329600 | bytes 25198620 | tf_op jit(solution)/shard_map/pallas_call | solution.py:65
  146.4 6.9 collective-permute-done.21
  153.3 8.7 %collective-permute-done.23 = bf16[2,128,1536]{2,1,0:T(8,128)(2,1)S(1)} collective-permute-done((bf16[2,128,1536]{2,1,0:T(8,128)(2,1)S(1)}, bf16[2,128,1536]{2,1,0:T(8,128)(2,1)S(1)}, u32[]{:S(2)}, u32[]{:S(2)}) %collective-permute-start.23) | collective-permute-done | bytes 786464 | tf_op jit(solution)/shard_map/ppermute | solution.py:394
  181.8 6.1 collective-permute-done.30
  204.9 11.1 %collective-permute-done.35.kv1 = bf16[2,512,256]{2,1,0:T(8,128)(2,1)S(1)} collective-permute-done((bf16[2,512,256]{2,1,0:T(8,128)(2,1)S(1)}, bf16[2,512,256]{2,1,0:T(8,128)(2,1)S(1)}, u32[]{:S(2)}, u32[]{:S(2)}) %collective-permute-start.35) | collective-permute-done | bytes 524320 | tf_op jit(solution)/shard_map/ppermute | solution.py:389
  219.7 7.7 %shard_map.224 = (bf16[2,128,384]{2,1,0:T(8,128)(2,1)S(1)}, f32[2,8,768]{2,1,0:T(8,128)S(1)}, bf16[2,128,1536]{2,1,0:T(8,128)(2,1)S(1)}) custom-call(s32[17]{0:T(128)S(1)} %pad_add_fusion.row_ref, bf16[384,1536]{1,0:T(8,128)(2,1)S(1)} %copy-done.12, bf16[2,128,384]{2,1,0:T(8,128)(2,1)S(1)} %bitcast.130, bf16[2,512,256]{2,1,0:T(8,128)(2,1)S(1)} %pad_maximum_fusion.9.kv0, ...), custom_call_target="tpu_custom_call" | custom-call | flops 3221225472 | bytes 4505668 | tf_op jit(solution)/shard_map/pallas_call | solution.py:65
  252.7 6.9 collective-permute-done.43.refs_1_.refs_9_
  275.5 16.6 %shard_map.225 = (bf16[2,128,1536]{2,1,0:T(8,128)(2,1)S(1)}, bf16[2,128,1536]{2,1,0:T(8,128)(2,1)S(1)}, bf16[2,128,1536]{2,1,0:T(8,128)(2,1)S(1)}, bf16[2,128,15...) custom-call(s32[7]{0:T(128)S(1)} %pad_add_fusion.2.s_ref, ...), custom_call_target="tpu_custom_call" | custom-call | flops 10066329600 | bytes 25198620 | tf_op jit(solution)/shard_map/pallas_call | solution.py:65
  292.6 17.3 %shard_map.226 = (bf16[2,128,1536]{2,1,0:T(8,128)(2,1)}, bf16[2,128,1536]{2,1,0:T(8,128)(2,1)}, bf16[2,128,1536]{2,1,0:T(8,128)(2,1)}, bf16[2,128,1536]{2,1,0:T(...) custom-call(s32[7]{0:T(128)S(1)} %pad_add_fusion.2.s_ref, ...), custom_call_target="tpu_custom_call" | custom-call | flops 10066329600 | bytes 33062940 | tf_op jit(solution)/shard_map/pallas_call | solution.py:65
  321.6 16.3 %collective-permute-done.52 = bf16[2,128,1536]{2,1,0:T(8,128)(2,1)S(1)} collective-permute-done((bf16[2,128,1536]{2,1,0:T(8,128)(2,1)S(1)}, bf16[2,128,1536]{2,1,0:T(8,128)(2,1)S(1)}, u32[]{:S(2)}, u32[]{:S(2)}) %collective-permute-start.52) | collective-permute-done | bytes 786464 | tf_op jit(solution)/shard_map/ppermute | solution.py:394
  361.2 11.3 %shard_map.227 = (bf16[2,128,384]{2,1,0:T(8,128)(2,1)S(1)}, bf16[2,512,256]{2,1,0:T(8,128)(2,1)S(1)}, bf16[2,512,256]{2,1,0:T(8,128)(2,1)S(1)}, bf16[2,512,256]{2,1,0:T(8,128)(2,1)S(1)}, bf16[2,512,256]{2,1,0:T(8,128)(2,1)S(1)}) custom-call(s32[17]{0:T(128)S(1)} %pad_add_fusion.row_ref, bf16[384,1536]{1,0:T(8,128)(2,1)S(1)} %copy-done.12, ...), custom_call_target="tpu_custom_call" | custom-call | flops 8053063680 | bytes 6930500 | tf_op jit(solution)/shard_map/pallas_call | solution.py:65
  372.6 6.5 collective-permute-done.67
  384.3 5.6 collective-permute-done.69
  389.9 6.5 collective-permute-done.70
  424.3 5.5 collective-permute-done.80
  450.6 15.7 %collective-permute-done.86.refs_1_ = bf16[2,128,1536]{2,1,0:T(8,128)(2,1)S(1)} collective-permute-done((bf16[2,128,1536]{2,1,0:T(8,128)(2,1)S(1)}, bf16[2,128,1536]{2,1,0:T(8,128)(2,1)S(1)}, u32[]{:S(2)}, u32[]{:S(2)}) %collective-permute-start.86) | collective-permute-done | bytes 786464 | tf_op jit(solution)/shard_map/ppermute | solution.py:389
  480.5 17.1 %shard_map.229 = (bf16[2,128,1536]{2,1,0:T(8,128)(2,1)}, bf16[2,128,1536]{2,1,0:T(8,128)(2,1)}, bf16[2,128,1536]{2,1,0:T(8,128)(2,1)}, bf16[2,128,1536]{2,1,0:T(...) custom-call(s32[7]{0:T(128)S(1)} %pad_add_fusion.2.s_ref, ...), custom_call_target="tpu_custom_call" | custom-call | flops 10066329600 | bytes 33062940 | tf_op jit(solution)/shard_map/pallas_call | solution.py:65
  506.5 7.5 %collective-permute-done.97 = bf16[2,128,1536]{2,1,0:T(8,128)(2,1)S(1)} collective-permute-done((bf16[2,128,1536]{2,1,0:T(8,128)(2,1)S(1)}, bf16[2,128,1536]{2,1,0:T(8,128)(2,1)S(1)}, u32[]{:S(2)}, u32[]{:S(2)}) %collective-permute-start.97) | collective-permute-done | bytes 786464 | tf_op jit(solution)/shard_map/ppermute | solution.py:394
  514.0 8.5 %collective-permute-done.99 = bf16[2,128,1536]{2,1,0:T(8,128)(2,1)S(1)} collective-permute-done((bf16[2,128,1536]{2,1,0:T(8,128)(2,1)S(1)}, bf16[2,128,1536]{2,1,0:T(8,128)(2,1)S(1)}, u32[]{:S(2)}, u32[]{:S(2)}) %collective-permute-start.99) | collective-permute-done | bytes 786464 | tf_op jit(solution)/shard_map/ppermute | solution.py:394
  547.3 5.9 all-to-all-start.1
  561.8 11.3 %shard_map.230 = (bf16[2,128,384]{2,1,0:T(8,128)(2,1)S(1)}, bf16[2,512,256]{2,1,0:T(8,128)(2,1)S(1)}, bf16[2,512,256]{2,1,0:T(8,128)(2,1)S(1)}, bf16[2,512,256]{2,1,0:T(8,128)(2,1)S(1)}, bf16[2,512,256]{2,1,0:T(8,128)(2,1)S(1)}) custom-call(s32[17]{0:T(128)S(1)} %pad_add_fusion.row_ref, bf16[384,1536]{1,0:T(8,128)(2,1)S(1)} %copy-done.13, ...), custom_call_target="tpu_custom_call" | custom-call | flops 8053063680 | bytes 6930500 | tf_op jit(solution)/shard_map/pallas_call | solution.py:65
  581.2 6.7 all-to-all-start.2
  592.7 13.4 %shard_map.231 = (f32[1536,640]{1,0:T(8,128)}, f32[1536,640]{1,0:T(8,128)}, f32[640,1536]{1,0:T(8,128)}) custom-call(s32[7]{0:T(128)} %copy-done.37, bf16[2,512,1536]{2,1,0:T(8,128)(2,1)} %get-tuple-element.245.b_own, bf16[2,128,1536]{2,1,0:T(8,128)(2,1)} %copy-done.130, bf16[2,128,1536]{2,1,0:T(8,128)(2,1)} %copy-done.131, ...), custom_call_target="tpu_custom_call" | custom-call | flops 5033164800 | bytes 12714012 | tf_op jit(solution)/shard_map/pallas_call | solution.py:65
  611.2 5.9 collective-permute-done.110
  639.6 8.2 %all-to-all-done.3 = bf16[16,112,256]{2,1,0:T(8,128)(2,1)S(1)} async-done(((bf16[16,112,256]{2,1,0:T(8,128)(2,1)}), bf16[16,112,256]{2,1,0:T(8,128)(2,1)S(1)}, u32[]{:S(2)}, u32[]{:S(2)}) %all-to-all-start.3) | async-done | bytes 917536 | tf_op jit(solution)/shard_map/all_to_all | solution.py:425
  648.7 5.4 collective-permute-start.115
  665.0 19.1 %collective-permute-done.116 = bf16[2,32,1536]{2,1,0:T(8,128)(2,1)S(1)} collective-permute-done((bf16[2,32,1536]{2,1,0:T(8,128)(2,1)S(1)}, bf16[2,32,1536]{2,1,0:T(8,128)(2,1)S(1)}, u32[]{:S(2)}, u32[]{:S(2)}) %collective-permute-start.116) | collective-permute-done | bytes 196640 | tf_op jit(solution)/shard_map/ppermute | solution.py:374
  (692 shorter events, 399.0 us)
Async XLA Ops:
  18.7 21.4 %collective-permute-start.1 = (bf16[2,128,256]{2,1,0:T(8,128)(2,1)S(1)}, bf16[2,128,256]{2,1,0:T(8,128)(2,1)}, u32[]{:S(2)}, u32[]{:S(2)}) collective-permute-start(bf16[2,128,256]{2,1,0:T(8,128)(2,1)S(1)} %bitcast.122), channel_id=1, source_target_pairs={{0,48},{2,14},{4,52},{6,2},{8,56},{10,6},{12,60},{14,10},{16,0},{1... | collective-permute-start | bytes 393224 | tf_op jit(solution)/shard_map/ppermute | solution.py:389
  22.7 18.2 %collective-permute-start.2 = (bf16[2,128,256]{2,1,0:T(8,128)(2,1)S(1)}, bf16[2,128,256]{2,1,0:T(8,128)(2,1)}, u32[]{:S(2)}, u32[]{:S(2)}) collective-permute-start(bf16[2,128,256]{2,1,0:T(8,128)(2,1)S(1)} %bitcast.123), channel_id=1, source_target_pairs={{0,32},{2,10},{4,36},{6,14},{8,40},{10,2},{12,44},{14,6},{16,48},{... | collective-permute-start | bytes 393224 | tf_op jit(solution)/shard_map/ppermute | solution.py:389
  96.1 19.8 %collective-permute-start.14 = (bf16[2,128,1536]{2,1,0:T(8,128)(2,1)S(1)}, bf16[2,128,1536]{2,1,0:T(8,128)(2,1)S(1)}, u32[]{:S(2)}, u32[]{:S(2)}) collective-permute-start(bf16[2,128,1536]{2,1,0:T(8,128)(2,1)S(1)} %pad_maximum_fusion.3.refs_0_), channel_id=1, source_target_pairs={{0,4},{2,18},{4,8},{6,22},{8,12},{10,26},{12,0},{14,30},{16,20},{1... | collective-permute-start | bytes 2359304 | tf_op jit(solution)/shard_map/ppermute | solution.py:389
  96.1 22.9 %collective-permute-start.15 = (bf16[2,128,1536]{2,1,0:T(8,128)(2,1)S(1)}, bf16[2,128,1536]{2,1,0:T(8,128)(2,1)S(1)}, u32[]{:S(2)}, u32[]{:S(2)}) collective-permute-start(bf16[2,128,1536]{2,1,0:T(8,128)(2,1)S(1)} %pad_maximum_fusion.3.refs_0_), channel_id=1, source_target_pairs={{0,2},{2,0},{4,6},{6,4},{8,10},{10,8},{12,14},{14,12},{16,18},{18,... | collective-permute-start | bytes 2359304 | tf_op jit(solution)/shard_map/ppermute | solution.py:370
  143.3 18.7 %collective-permute-start.23 = (bf16[2,128,1536]{2,1,0:T(8,128)(2,1)S(1)}, bf16[2,128,1536]{2,1,0:T(8,128)(2,1)S(1)}, u32[]{:S(2)}, u32[]{:S(2)}) collective-permute-start(bf16[2,128,1536]{2,1,0:T(8,128)(2,1)S(1)} %add_convert_fusion.17), channel_id=1, source_target_pairs={{0,8},{2,34},{4,12},{6,38},{8,0},{10,42},{12,4},{14,46},{16,24},{1... | collective-permute-start | bytes 2359304 | tf_op jit(solution)/shard_map/ppermute | solution.py:394
  144.6 19.4 %collective-permute-start.25 = (bf16[2,128,1536]{2,1,0:T(8,128)(2,1)S(1)}, bf16[2,128,1536]{2,1,0:T(8,128)(2,1)S(1)}, u32[]{:S(2)}, u32[]{:S(2)}) collective-permute-start(bf16[2,128,1536]{2,1,0:T(8,128)(2,1)S(1)} %add_convert_fusion.16), channel_id=1, source_target_pairs={{0,12},{2,50},{4,0},{6,54},{8,4},{10,58},{12,8},{14,62},{16,28},{1... | collective-permute-start | bytes 2359304 | tf_op jit(solution)/shard_map/ppermute | solution.py:394
  248.7 21.1 %collective-permute-start.45 = (bf16[2,128,1536]{2,1,0:T(8,128)(2,1)S(1)}, bf16[2,128,1536]{2,1,0:T(8,128)(2,1)S(1)}, u32[]{:S(2)}, u32[]{:S(2)}) collective-permute-start(bf16[2,128,1536]{2,1,0:T(8,128)(2,1)S(1)} %pad_maximum_fusion.5.refs_0_.refs_8_), channel_id=1, source_target_pairs={{0,4},{2,18},{4,8},{6,22},{8,12},{10,26},{12,0},{14,30},{16,20},{1... | collective-permute-start | bytes 2359304 | tf_op jit(solution)/shard_map/ppermute | solution.py:389
  249.9 23.5 %collective-permute-start.46 = (bf16[2,128,1536]{2,1,0:T(8,128)(2,1)S(1)}, bf16[2,128,1536]{2,1,0:T(8,128)(2,1)S(1)}, u32[]{:S(2)}, u32[]{:S(2)}) collective-permute-start(bf16[2,128,1536]{2,1,0:T(8,128)(2,1)S(1)} %pad_maximum_fusion.5.refs_0_.refs_8_), channel_id=1, source_target_pairs={{0,2},{2,0},{4,6},{6,4},{8,10},{10,8},{12,14},{14,12},{16,18},{18,... | collective-permute-start | bytes 2359304 | tf_op jit(solution)/shard_map/ppermute | solution.py:370
  292.1 18.9 %collective-permute-start.63 = (bf16[2,128,1536]{2,1,0:T(8,128)(2,1)}, bf16[2,128,1536]{2,1,0:T(8,128)(2,1)}, u32[]{:S(2)}, u32[]{:S(2)}) collective-permute-start(bf16[2,128,1536]{2,1,0:T(8,128)(2,1)} %get-tuple-element.217), channel_id=1, source_target_pairs={{0,2},{2,0},{4,6},{6,4},{8,10},{10,8},{12,14},{14,12},{16,18},{18,... | collective-permute-start | bytes 2359304 | tf_op jit(solution)/shard_map/ppermute | solution.py:370
  317.0 21.0 %collective-permute-start.52 = (bf16[2,128,1536]{2,1,0:T(8,128)(2,1)S(1)}, bf16[2,128,1536]{2,1,0:T(8,128)(2,1)S(1)}, u32[]{:S(2)}, u32[]{:S(2)}) collective-permute-start(bf16[2,128,1536]{2,1,0:T(8,128)(2,1)S(1)} %add_convert_fusion.13), channel_id=1, source_target_pairs={{0,4},{2,18},{4,8},{6,22},{8,12},{10,26},{12,0},{14,30},{16,20},{1... | collective-permute-start | bytes 2359304 | tf_op jit(solution)/shard_map/ppermute | solution.py:394
  318.1 19.8 %collective-permute-start.54 = (bf16[2,128,1536]{2,1,0:T(8,128)(2,1)S(1)}, bf16[2,128,1536]{2,1,0:T(8,128)(2,1)S(1)}, u32[]{:S(2)}, u32[]{:S(2)}) collective-permute-start(bf16[2,128,1536]{2,1,0:T(8,128)(2,1)S(1)} %add_convert_fusion.12), channel_id=1, source_target_pairs={{0,8},{2,34},{4,12},{6,38},{8,0},{10,42},{12,4},{14,46},{16,24},{1... | collective-permute-start | bytes 2359304 | tf_op jit(solution)/shard_map/ppermute | solution.py:394
  319.2 19.7 %collective-permute-start.56 = (bf16[2,128,1536]{2,1,0:T(8,128)(2,1)S(1)}, bf16[2,128,1536]{2,1,0:T(8,128)(2,1)S(1)}, u32[]{:S(2)}, u32[]{:S(2)}) collective-permute-start(bf16[2,128,1536]{2,1,0:T(8,128)(2,1)S(1)} %add_convert_fusion.11), channel_id=1, source_target_pairs={{0,12},{2,50},{4,0},{6,54},{8,4},{10,58},{12,8},{14,62},{16,28},{1... | collective-permute-start | bytes 2359304 | tf_op jit(solution)/shard_map/ppermute | solution.py:394
  320.6 21.5 %collective-permute-start.60 = (bf16[2,128,1536]{2,1,0:T(8,128)(2,1)S(1)}, bf16[2,128,1536]{2,1,0:T(8,128)(2,1)S(1)}, u32[]{:S(2)}, u32[]{:S(2)}) collective-permute-start(bf16[2,128,1536]{2,1,0:T(8,128)(2,1)S(1)} %get-tuple-element.211), channel_id=1, source_target_pairs={{0,2},{2,0},{4,6},{6,4},{8,10},{10,8},{12,14},{14,12},{16,18},{18,... | collective-permute-start | bytes 2359304 | tf_op jit(solution)/shard_map/ppermute | solution.py:370
  357.7 21.3 %collective-permute-start.67 = (bf16[2,128,1536]{2,1,0:T(8,128)(2,1)S(1)}, bf16[2,128,1536]{2,1,0:T(8,128)(2,1)S(1)}, u32[]{:S(2)}, u32[]{:S(2)}) collective-permute-start(bf16[2,128,1536]{2,1,0:T(8,128)(2,1)S(1)} %add_convert_fusion.7), channel_id=1, source_target_pairs={{0,8},{2,34},{4,12},{6,38},{8,0},{10,42},{12,4},{14,46},{16,24},{1... | collective-permute-start | bytes 2359304 | tf_op jit(solution)/shard_map/ppermute | solution.py:394
  360.9 18.2 %collective-permute-start.68 = (bf16[2,128,1536]{2,1,0:T(8,128)(2,1)S(1)}, bf16[2,128,1536]{2,1,0:T(8,128)(2,1)S(1)}, u32[]{:S(2)}, u32[]{:S(2)}) collective-permute-start(bf16[2,128,1536]{2,1,0:T(8,128)(2,1)S(1)} %add_convert_fusion.6), channel_id=1, source_target_pairs={{0,12},{2,50},{4,0},{6,54},{8,4},{10,58},{12,8},{14,62},{16,28},{1... | collective-permute-start | bytes 2359304 | tf_op jit(solution)/shard_map/ppermute | solution.py:394
  444.5 21.8 %collective-permute-start.86 = (bf16[2,128,1536]{2,1,0:T(8,128)(2,1)S(1)}, bf16[2,128,1536]{2,1,0:T(8,128)(2,1)S(1)}, u32[]{:S(2)}, u32[]{:S(2)}) collective-permute-start(bf16[2,128,1536]{2,1,0:T(8,128)(2,1)S(1)} %pad_maximum_fusion.7.refs_0_), channel_id=1, source_target_pairs={{0,12},{2,50},{4,0},{6,54},{8,4},{10,58},{12,8},{14,62},{16,28},{1... | collective-permute-start | bytes 2359304 | tf_op jit(solution)/shard_map/ppermute | solution.py:389
  449.0 20.8 %collective-permute-start.88 = (bf16[2,128,1536]{2,1,0:T(8,128)(2,1)S(1)}, bf16[2,128,1536]{2,1,0:T(8,128)(2,1)S(1)}, u32[]{:S(2)}, u32[]{:S(2)}) collective-permute-start(bf16[2,128,1536]{2,1,0:T(8,128)(2,1)S(1)} %pad_maximum_fusion.7.refs_0_), channel_id=1, source_target_pairs={{0,4},{2,18},{4,8},{6,22},{8,12},{10,26},{12,0},{14,30},{16,20},{1... | collective-permute-start | bytes 2359304 | tf_op jit(solution)/shard_map/ppermute | solution.py:389
  449.5 20.2 %collective-permute-start.89 = (bf16[2,128,1536]{2,1,0:T(8,128)(2,1)S(1)}, bf16[2,128,1536]{2,1,0:T(8,128)(2,1)S(1)}, u32[]{:S(2)}, u32[]{:S(2)}) collective-permute-start(bf16[2,128,1536]{2,1,0:T(8,128)(2,1)S(1)} %get-tuple-element.250), channel_id=1, source_target_pairs={{0,1},{1,0},{2,3},{3,2},{4,5},{5,4},{6,7},{7,6},{8,9},{9,8},{10,11... | collective-permute-start | bytes 2359304 | tf_op jit(solution)/shard_map/ppermute | solution.py:374
  474.9 22.8 %collective-permute-start.94 = (bf16[2,128,1536]{2,1,0:T(8,128)(2,1)S(1)}, bf16[2,128,1536]{2,1,0:T(8,128)(2,1)S(1)}, u32[]{:S(2)}, u32[]{:S(2)}) collective-permute-start(bf16[2,128,1536]{2,1,0:T(8,128)(2,1)S(1)} %get-tuple-element.267), channel_id=1, source_target_pairs={{0,1},{1,0},{2,3},{3,2},{4,5},{5,4},{6,7},{7,6},{8,9},{9,8},{10,11... | collective-permute-start | bytes 2359304 | tf_op jit(solution)/shard_map/ppermute | solution.py:374
  501.9 20.5 %collective-permute-start.99 = (bf16[2,128,1536]{2,1,0:T(8,128)(2,1)S(1)}, bf16[2,128,1536]{2,1,0:T(8,128)(2,1)S(1)}, u32[]{:S(2)}, u32[]{:S(2)}) collective-permute-start(bf16[2,128,1536]{2,1,0:T(8,128)(2,1)S(1)} %add_convert_fusion.2), channel_id=1, source_target_pairs={{0,8},{2,34},{4,12},{6,38},{8,0},{10,42},{12,4},{14,46},{16,24},{1... | collective-permute-start | bytes 2359304 | tf_op jit(solution)/shard_map/ppermute | solution.py:394
  505.2 18.2 %collective-permute-start.101 = (bf16[2,128,1536]{2,1,0:T(8,128)(2,1)S(1)}, bf16[2,128,1536]{2,1,0:T(8,128)(2,1)S(1)}, u32[]{:S(2)}, u32[]{:S(2)}) collective-permute-start(bf16[2,128,1536]{2,1,0:T(8,128)(2,1)S(1)} %add_convert_fusion.1), channel_id=1, source_target_pairs={{0,12},{2,50},{4,0},{6,54},{8,4},{10,58},{12,8},{14,62},{16,28},{1... | collective-permute-start | bytes 2359304 | tf_op jit(solution)/shard_map/ppermute | solution.py:394
  505.4 18.5 %collective-permute-start.102 = (bf16[2,128,1536]{2,1,0:T(8,128)(2,1)S(1)}, bf16[2,128,1536]{2,1,0:T(8,128)(2,1)S(1)}, u32[]{:S(2)}, u32[]{:S(2)}) collective-permute-start(bf16[2,128,1536]{2,1,0:T(8,128)(2,1)S(1)} %get-tuple-element.284), channel_id=1, source_target_pairs={{0,1},{1,0},{2,3},{3,2},{4,5},{5,4},{6,7},{7,6},{8,9},{9,8},{10,11... | collective-permute-start | bytes 2359304 | tf_op jit(solution)/shard_map/ppermute | solution.py:374
  543.8 34.6 %collective-permute-start.108 = (bf16[2,256,1280]{2,1,0:T(8,128)(2,1)}, bf16[2,256,1280]{2,1,0:T(8,128)(2,1)}, u32[]{:S(2)}, u32[]{:S(2)}) collective-permute-start(bf16[2,256,1280]{2,1,0:T(8,128)(2,1)} %get-tuple-element.293.g_own), channel_id=1, source_target_pairs={{0,1},{1,0},{2,3},{3,2},{4,5},{5,4},{6,7},{7,6},{8,9},{9,8},{10,11... | collective-permute-start | bytes 3932168 | tf_op jit(solution)/shard_map/ppermute | solution.py:374
  547.3 28.9 %all-to-all-start.1 = ((bf16[16,24,1536]{2,1,0:T(8,128)(2,1)}), bf16[16,24,1536]{2,1,0:T(8,128)(2,1)}, u32[]{:S(2)}, u32[]{:S(2)}) async-start(bf16[16,24,1536]{2,1,0:T(8,128)(2,1)} %bitcast.136), calls=%async_computation.1 | async-start | bytes 2359296 | tf_op jit(solution)/shard_map/all_to_all | solution.py:425
  553.2 94.6 %all-gather.3.cloned.1.call-start = ((), (), s32[]{:S(2)}) async-start(), calls=%async_computation.5 | async-start | bytes 2433024 | tf_op jit(solution)/shard_map/all_gather | solution.py:730
  581.2 37.1 %all-to-all-start.2 = ((bf16[16,96,384]{2,1,0:T(8,128)(2,1)}), bf16[16,96,384]{2,1,0:T(8,128)(2,1)}, u32[]{:S(2)}, u32[]{:S(2)}) async-start(bf16[16,96,384]{2,1,0:T(8,128)(2,1)} %bitcast.135), calls=%async_computation.2 | async-start | bytes 2359296 | tf_op jit(solution)/shard_map/all_to_all | solution.py:425
  587.8 23.4 %collective-permute-start.109 = (bf16[2,512,256]{2,1,0:T(8,128)(2,1)}, bf16[2,512,256]{2,1,0:T(8,128)(2,1)S(1)}, u32[]{:S(2)}, u32[]{:S(2)}) collective-permute-start(bf16[2,512,256]{2,1,0:T(8,128)(2,1)} %copy-done.49), channel_id=1, source_target_pairs={{0,4},{2,18},{4,8},{6,22},{8,12},{10,26},{12,0},{14,30},{16,20},{1... | collective-permute-start | bytes 1572872 | tf_op jit(solution)/shard_map/ppermute | solution.py:394
  589.1 28.0 %collective-permute-start.110 = (bf16[2,512,256]{2,1,0:T(8,128)(2,1)}, bf16[2,512,256]{2,1,0:T(8,128)(2,1)S(1)}, u32[]{:S(2)}, u32[]{:S(2)}) collective-permute-start(bf16[2,512,256]{2,1,0:T(8,128)(2,1)} %copy-done.48), channel_id=1, source_target_pairs={{0,8},{2,34},{4,12},{6,38},{8,0},{10,42},{12,4},{14,46},{16,24},{1... | collective-permute-start | bytes 1572872 | tf_op jit(solution)/shard_map/ppermute | solution.py:394
  591.5 25.6 %collective-permute-start.111 = (bf16[2,512,256]{2,1,0:T(8,128)(2,1)}, bf16[2,512,256]{2,1,0:T(8,128)(2,1)S(1)}, u32[]{:S(2)}, u32[]{:S(2)}) collective-permute-start(bf16[2,512,256]{2,1,0:T(8,128)(2,1)} %copy-done.47), channel_id=1, source_target_pairs={{0,12},{2,50},{4,0},{6,54},{8,4},{10,58},{12,8},{14,62},{16,28},{1... | collective-permute-start | bytes 1572872 | tf_op jit(solution)/shard_map/ppermute | solution.py:394
  638.9 45.2 %collective-permute-start.117 = (bf16[640,1536]{1,0:T(8,128)(2,1)}, bf16[640,1536]{1,0:T(8,128)(2,1)}, u32[]{:S(2)}, u32[]{:S(2)}) collective-permute-start(bf16[640,1536]{1,0:T(8,128)(2,1)} %convert_element_type.592), channel_id=1, source_target_pairs={{0,1},{1,0},{2,3},{3,2},{4,5},{5,4},{6,7},{7,6},{8,9},{9,8},{10,11... | collective-permute-start | bytes 5898248 | tf_op jit(solution)/shard_map/ppermute | solution.py:374
  655.7 33.6 %all-to-all-start.4 = ((bf16[16,103,640]{2,1,0:T(8,128)(2,1)}), bf16[16,103,640]{2,1,0:T(8,128)(2,1)S(1)}, u32[]{:S(2)}, u32[]{:S(2)}) async-start(bf16[16,103,640]{2,1,0:T(8,128)(2,1)} %broadcast_in_dim.42), calls=%async_computation.4 | async-start | bytes 4259840 | tf_op jit(solution)/shard_map/all_to_all | solution.py:425
  661.4 22.6 %collective-permute-start.116 = (bf16[2,32,1536]{2,1,0:T(8,128)(2,1)S(1)}, bf16[2,32,1536]{2,1,0:T(8,128)(2,1)S(1)}, u32[]{:S(2)}, u32[]{:S(2)}) collective-permute-start(bf16[2,32,1536]{2,1,0:T(8,128)(2,1)S(1)} %dynamic-slice_convert_fusion), channel_id=1, source_target_pairs={{0,1},{1,0},{2,3},{3,2},{4,5},{5,4},{6,7},{7,6},{8,9},{9,8},{10,11... | collective-permute-start | bytes 589832 | tf_op jit(solution)/shard_map/ppermute | solution.py:374
  (237 other events, 3452.7 us)
Sparse Core Ops, SparseCore 0:
  578.5 60.7 all-gather.2

commit v2 on v1

--- a/solution.py
+++ b/solution.py
@@ -44,9 +44,15 @@
     return pl.BlockSpec((None, *shape), lambda m: (m, *(0,) * len(shape)))
 
 
-def local_call(kernel, outs, operands, scratch=(), flops=0, smem=0, vmem=40, each=(), sums=(), micros=1):
-    each = list(each)
-    moved = sum(int(np.prod(v.shape)) * v.dtype.itemsize for v in [*operands, *each])
+def pair_spec(shape):
+    return pl.BlockSpec((shape[0], None, *shape[2:]), lambda m: (0, m, *(0,) * len(shape[2:])))
+
+
+def local_call(
+    kernel, outs, operands, scratch=(), flops=0, smem=0, vmem=40, each=(), pairs=(), sums=(), micros=1
+):
+    each, pairs = list(each), list(pairs)
+    moved = sum(int(np.prod(v.shape)) * v.dtype.itemsize for v in [*operands, *each, *pairs])
     moved += sum(micros * int(np.prod(s)) * jnp.dtype(d).itemsize for s, d in outs)
     params = dict(
         scratch_shapes=[pltpu.VMEM(s, d) for s, d in scratch],
@@ -69,10 +75,11 @@
         + [jax.ShapeDtypeStruct(s, d) for s, d in sums],
         in_specs=scalars
         + [whole_spec(v.shape, pipeline_mode=pl.Buffered(1)) for v in operands[smem:]]
-        + [micro_spec(v.shape[1:]) for v in each],
+        + [micro_spec(v.shape[1:]) for v in each]
+        + [pair_spec(v.shape) for v in pairs],
         out_specs=[micro_spec(s) for s, d in outs] + [whole_spec(s) for s, d in sums],
         **params,
-    )(*operands, *each)
+    )(*operands, *each, *pairs)
 
 
 def turn(values, cosine, sine):
@@ -272,10 +279,9 @@
 
 def experts_back_kernel(s_ref, router, wg, wu, wd, *refs):
     grads_in, refs = refs[: 2 * SIDE], refs[2 * SIDE :]
-    tokens_in, refs = refs[: 2 * SIDE], refs[2 * SIDE :]
     tgt, gates, g_ref, u_ref, *refs = refs
     grads_out, refs = refs[: 2 * SIDE], refs[2 * SIDE :]
-    dgu_ref, h_ref, dy, router_grad, inner, back = refs
+    dgu_ref, h_ref, dy, dz_ref, inner, back = refs
     chunks = SIDE
     rows = dy.shape[0] // 2
     for ch in range(chunks):
@@ -319,7 +325,7 @@
         dz = dz - table * (sums[0] + sums[1])
         high = dz.astype(bf16)
         lower = (dz - high.astype(f32)).astype(bf16)
-        both = jnp.concatenate([high, lower], axis=0)
+        dz_ref[:, span] = jnp.concatenate([high, lower], axis=0)
         at = ch * HALF
         moved = jnp.concatenate([back[at : at + HALF, :], back[rows + at : rows + at + HALF, :]], axis=0)
         value = tn(
@@ -327,32 +333,44 @@
             jnp.concatenate([moved.astype(bf16), router[...]], axis=0),
         )
         put_two(grads_out, ch, value.astype(bf16))
-        part = nn(both, two_of(tokens_in, ch))
-        part = part[: table.shape[0]] + part[table.shape[0] :]
-        if ch == 0:
-            begin = pl.program_id(0) == 0
-            router_grad[...] = part + jnp.where(begin, 0.0, router_grad[...])
-        else:
-            router_grad[...] += part
-
-
-def expert_weights_kernel(s_ref, b_own, o0, o1, o2, o3, g_own, g_other, h, dy, gate, up, down):
-    rows, size = h.shape[0], o0.shape[0]
+
+
+def router_kernel(dz_ref, *refs):
+    tokens_in, (router_grad,) = refs[: 2 * SIDE], refs[2 * SIDE :]
+    total = 0.0
+    for ch in range(SIDE):
+        total = total + nn(dz_ref[:, ch * CHUNK : (ch + 1) * CHUNK], two_of(tokens_in, ch))
+    rows = router_grad.shape[0]
+    total = total[:rows] + total[rows:]
+    router_grad[...] = total + jnp.where(pl.program_id(0) == 0, 0.0, router_grad[...])
+
+
+def expert_weights_kernel(
+    s_ref, b_own, o0, o1, o2, h, dy, dgu, gate, up, near, far, down
+):
+    rows, size = h.shape[0], o1.shape[0]
+    half = s_ref[2 + h.shape[1] // BLOCK]
     begin = pl.program_id(0) == 0
     for k in range(h.shape[1] // BLOCK):
         at = slice(k * BLOCK, (k + 1) * BLOCK)
         wide = slice(2 * k * BLOCK, 2 * (k + 1) * BLOCK)
         here = pl.ds(pl.multiple_of(s_ref[2 + k] * rows, rows), rows)
         first = s_ref[2 + k] == 0
-        theirs = [jnp.where(first, o0[...], o2[...]), jnp.where(first, o1[...], o3[...])]
+        theirs = [jnp.where(first, o0[:size], o1[...]), jnp.where(first, o0[size:], o2[...])]
         both = tn(
             jnp.concatenate([b_own[here, :], *theirs], axis=0),
-            jnp.concatenate([g_own[:, wide], g_other[:, wide]], axis=0),
+            jnp.concatenate([dgu[half, :, wide], dgu[1 - half, :, wide]], axis=0),
         )
         low = tn(h[:, at], dy[here, :])
         gate[:, at] = both[:, :BLOCK] + jnp.where(begin, 0.0, gate[:, at])
         up[:, at] = both[:, BLOCK:] + jnp.where(begin, 0.0, up[:, at])
-        down[at, :] = low + jnp.where(begin, 0.0, down[at, :])
+        low = low + jnp.where(begin, 0.0, down[at, :])
+        down[at, :] = low
+        cut = at.start - near.shape[0]
+        if cut < 0:
+            near[at, :] = low.astype(bf16)
+        else:
+            far[cut : cut + BLOCK, :] = low.astype(bf16)
 
 
 def ring(stage, steps):
@@ -480,7 +498,7 @@
     first_expert = rank * blocks // EXPERT_BLOCKS
     which = (rank * blocks + jnp.arange(blocks)) // EXPERT_BLOCKS - first_expert
     scalars = jnp.concatenate(
-        [jnp.stack([first_expert, first_expert + 1]), which]
+        [jnp.stack([first_expert, first_expert + 1]), which, half.reshape(1)]
     ).astype(jnp.int32)
 
     tokens = CHIPS * own_rows
@@ -545,7 +563,7 @@
             ],
             flops=20 * micros * length * 6 * chip_rows * LANES,
             smem=1,
-            vmem=32,
+            vmem=60,
             micros=micros,
         )
 
@@ -585,7 +603,7 @@
         )
         return result[: 2 * SIDE], result[2 * SIDE :]
 
-    def run_experts_back(grads, arrived, gates, g, u):
+    def run_experts_back(grads, gates, g, u):
         result = local_call(
             experts_back_kernel,
             [piece] * (2 * SIDE)
@@ -593,10 +611,10 @@
                 ((slot_rows // 2, 2 * hidden_width), bf16),
                 ((slot_rows // 2, hidden_width), bf16),
                 ((slot_rows, width), bf16),
+                ((2 * expert_rows, 2 * tokens), bf16),
             ],
             [scalars, router_t, gate_w, up_w, down_w],
-            each=[*grads, *arrived, targets, gates, g, u],
-            sums=[((expert_rows, width), f32)],
+            each=[*grads, targets, gates, g, u],
             scratch=[((slot_rows, LANES), f32), ((slot_rows, width), f32)],
             flops=10 * micros * slot_rows * hidden_width * width,
             smem=1,
@@ -614,10 +632,6 @@
         rows64 = in_order(rows32, other_half(rows32), half, 1)
         return in_order(rows64, other_core(rows64), core, 1)
 
-    def tokens_out(rows32):
-        arrived = everyone(rows32)
-        return arrived + [other_core(p) for p in arrived]
-
     def over_cores(parts):
         return [
             (own.astype(f32) + other_core(other).astype(f32)).astype(bf16)
@@ -638,33 +652,46 @@
     def forward(own, x128, sent=None):
         nonlocal targets, masks
         a, q, kv = project(x128)
-        if sent is not None:
-            kv, own_routes = pin(
-                kv, lax.dynamic_slice_in_dim(routes[0], half * own_rows, own_rows, 1)
-            )
-            targets, masks = prepare(own_routes)
         kv_all = everyone(kv)
-        if sent is not None:
-            *kv_all, targets, masks = pin(*kv_all, targets, masks)
         o, log_total, y = attend(q, kv_all)
         residual = own.astype(f32) + sum_four(y)
         mixed = (residual * inverse_root(residual) * gain_two).astype(bf16)
-        arrived = tokens_out(mixed if sent is None else jnp.where(section == 0, mixed, sent))
+        if sent is not None:
+            own_routes = lax.dynamic_slice_in_dim(routes[0], half * own_rows, own_rows, 1)
+            targets, masks = prepare(pin(own_routes, kv_all[0])[0])
+            mixed = jnp.where(section == 0, mixed, sent)
+        arrived = everyone(mixed)
+        if sent is not None:
+            *arrived, targets, masks = pin(*arrived, targets, masks)
+        arrived = arrived + [other_core(p) for p in arrived]
         parts, rest = run_experts(arrived)
         return parts, (own, x128, a, q, kv_all, o, log_total, residual, arrived, *rest)
 
-    def backward(grad_rows, grads, kept, first=(), second=()):
-        residual, arrived, gates, _, g, u = kept[7:]
-        parts, (dgu, h, dy, router_grad) = run_experts_back(grads, arrived, gates, g, u)
-        *parts, first = pin(*parts, first)
-        if second:
-            *parts, rows = pin(*parts, second[0])
-            second = [other_half(rows)]
-        mixed_grad, second = tokens_back(parts, second)
+    def backward(grad_rows, grads, kept, between=None):
+        residual, _, gates, _, g, u = kept[7:]
+        parts, rest = run_experts_back(grads, gates, g, u)
+        if between is None:
+            mixed_grad = tokens_back(parts)[0]
+        else:
+            parts = between(*between(*parts, finish=True), start=True)
+            (router_grad,) = local_call(
+                router_kernel,
+                [],
+                [],
+                each=[rest[3], *kept[8]],
+                sums=[((expert_rows, width), f32)],
+                flops=4 * micros * expert_rows * 2 * tokens * width,
+                vmem=20,
+                micros=micros,
+            )
+            pieces = to_ring(over_cores(parts), 1)
+            joined, router_grad = between(added(pieces).astype(bf16), router_grad, finish=True)
+            rest = (*rest[:3], router_grad)
+            mixed_grad = added(to_ring(pieces_of(joined), 0))
         root = inverse_root(residual)
         gain_two_grad = jnp.sum(mixed_grad * residual * root, axis=(0, 1))
         resid_grad = grad_rows.astype(f32) + norm_back(residual, root, mixed_grad, gain_two)
-        return resid_grad, (dgu, h, dy), router_grad, gain_two_grad, [first, *second]
+        return resid_grad, rest, gain_two_grad
 
     targets = masks = None
     own_x = lax.dynamic_slice_in_dim(x_in, half * own_rows, own_rows, 1)
@@ -684,10 +711,12 @@
     resid_grad, *_ = backward(cotangent, upper_grads, kept)
     low, *joined = pin(resid_grad.astype(bf16), *over_cores(last_parts))
     pieces = to_ring(joined, 1)
-    dq, *dkv = attend_back(q, kv_all, to_four(low), log_total, o)
+    out_grad, rows = pin(to_four(low), slots_in[:, : slot_rows // 2])
+    other_slots = [other_half(rows)]
+    dq, *dkv = attend_back(q, kv_all, out_grad, log_total, o)
     *dkv, joined = pin(*dkv, added(pieces).astype(bf16))
     dkv, _ = to_owners(dkv)
-    *dkv, joined = pin(*dkv, joined)
+    *dkv, joined, other_slots[0] = pin(*dkv, joined, other_slots[0])
     pieces = to_ring(pieces_of(joined), 0)
     _, y, _ = after_keys(dkv, dq, x128)
     normed_grad, out = pin(sum_four(y), (residual + added(pieces)).astype(bf16))
@@ -697,92 +726,91 @@
     coming, other_out = pin(jnp.where(section == 0, coming, cotangent), other_half(out))
     activations = in_order(out, other_out, half, 1)
 
-    size = slot_rows // SIDE
-    other_slots = []
-
-    def next_slots(*values):
-        at = len(other_slots) * size
-        *values, rows = pin(*values, slots_in[:, at : at + size])
-        other_slots.append(other_half(rows))
+    cuts = [0, slot_rows // 2, slot_rows * 3 // 4, slot_rows]
+
+    def between(*values, finish=False, start=False):
+        if finish:
+            *values, other_slots[-1] = pin(*values, other_slots[-1])
+        if start:
+            at, end = cuts[len(other_slots) :][:2]
+            *values, rows = pin(*values, slots_in[:, at:end])
+            other_slots.append(other_half(rows))
         return values
 
-    def slots_done(*values):
-        *values, other_slots[-1] = pin(*values, other_slots[-1])
-        return values
-
-    (coming,) = next_slots(coming)
-    arrived = from_ring(coming, 0)
-    (arrived,) = next_slots(*slots_done(jnp.concatenate(arrived, axis=1)))
-    arrived = next_slots(*slots_done(*from_ring(arrived, 1)))
+    arrived = between(*everyone(coming), start=True)
     grads = arrived + [other_core(p) for p in arrived]
-    resid_grad, (dgu, h, dy), router_grad, gain_two_grad, last_slots = backward(
-        coming, grads, kept, other_slots[2], [slots_in[:, 3 * size :]]
-    )
-    other_slots[2:] = last_slots
-    out_grad, dgu_sent = pin(to_four(resid_grad.astype(bf16)), dgu)
-    other_dgu = other_half(dgu_sent)
+    resid_grad, (dgu, h, dy, router_grad), gain_two_grad = backward(coming, grads, kept, between)
+    out_grad = to_four(resid_grad.astype(bf16))
+    all_dgu = lax.all_gather(dgu, "tp")
     out_w_grad = tn(o.reshape(both_rows, -1), out_grad.reshape(both_rows, width)).astype(bf16)
-    out_w_grad = jnp.sum(
-        exchange(out_w_grad.reshape(CHIPS, -1, width)).astype(f32), axis=0
-    ).astype(bf16)
+    out_w_grad = exchange(out_w_grad.reshape(CHIPS, -1, width))
     dq, *dkv = attend_back(q, kv_all, out_grad, log_total, o)
-    *dkv, out_w_grad, other_dgu = pin(*dkv, out_w_grad, other_dgu)
-    all_out = lax.all_gather(out_w_grad, "ep")
-    q_grad = tn(a, dq.reshape(both_rows, -1)).astype(bf16).reshape(CHIPS, -1, 3 * LANES)
-    q_grad = exchange(q_grad)
-    gate_grad, up_grad, down_part = local_call(
+    dq, out_w_grad = pin(dq, out_w_grad)
+    out_w_grad = jnp.sum(out_w_grad.astype(f32), axis=0).astype(bf16)
+    near_rows = 2 * BLOCK
+    gate_grad, up_grad, near, far = local_call(
         expert_weights_kernel,
         [],
         [scalars],
-        each=[slots_in, *other_slots, dgu, other_dgu, h, dy],
-        sums=[((width, hidden_width), f32), ((width, hidden_width), f32), ((hidden_width, width), f32)],
+        each=[slots_in, *other_slots, h, dy],
+        pairs=[all_dgu],
+        sums=[
+            ((width, hidden_width), f32),
+            ((width, hidden_width), f32),
+            ((near_rows, width), bf16),
+            ((hidden_width - near_rows, width), bf16),
+        ],
+        scratch=[((hidden_width, width), f32)],
         flops=10 * slot_rows * hidden_width * width,
         smem=1,
         vmem=56,
         micros=micros,
     )
-    down_part = down_part.astype(bf16)
-    arrived, (gate_grad, up_grad, down_part, q_grad) = to_owners(
-        dkv, (gate_grad, up_grad, down_part, q_grad)
-    )
-    other_down = other_half(down_part)
+    all_out = lax.all_gather(out_w_grad, "ep")
+    q_grad = tn(a, dq.reshape(both_rows, -1)).astype(bf16)
+    q_grad = exchange(q_grad.reshape(CHIPS, -1, 3 * LANES))
+    arrived, (gate_grad, up_grad, near, far, q_grad) = to_owners(
+        dkv, (gate_grad, up_grad, near, far, q_grad)
+    )
     q_grad = jnp.sum(q_grad.astype(f32), axis=0).astype(bf16)
     dqkv, y, gain_one_grad = after_keys(arrived, dq, x128)
+    near_down = other_half(near)
+
+    kv_width = 2 * LANES
     small = jnp.concatenate([router_grad[:experts], gain_one_grad, gain_two_grad[None]], axis=0)
-    kv_width, all_width = 2 * LANES, 5 * LANES
     small_count = small.size
-    per_chip = -(-small_count // (CHIPS * 8 * LANES)) * 8 * LANES
-    small = jnp.pad(small.reshape(-1), (0, CHIPS * per_chip - small_count)).astype(bf16)
-    kv_grad = tn(a, dqkv[:, 3 * LANES :]).astype(bf16).reshape(CHIPS, -1, kv_width)
-    lines = kv_grad.shape[1]
-    summed = exchange(
-        jnp.concatenate([kv_grad, small.reshape(CHIPS, -1, kv_width)], axis=1)
-    )
-    summed, all_out, q_grad, y = pin(summed, all_out, q_grad, y)
-    summed = jnp.sum(summed.astype(f32), axis=0).astype(bf16)
-    small = jnp.pad(
-        summed[lines:].reshape(-1, LANES), ((0, -per_chip // LANES % 5), (0, 0))
-    ).reshape(-1, all_width)
-    wide = jnp.concatenate(
-        [jnp.concatenate([q_grad, summed[:lines]], axis=1), small], axis=0
-    )
+    small_lines = -(-small_count // (CHIPS * kv_width))
+    small = jnp.pad(small.reshape(-1), (0, CHIPS * small_lines * kv_width - small_count))
+    small = small.reshape(CHIPS, small_lines, kv_width).astype(bf16)
+    wide = tn(a, dqkv[:, 3 * LANES :]).astype(bf16).reshape(CHIPS, -1, kv_width)
+    lines = wide.shape[1]
+    wide, near_down, all_out = pin(jnp.concatenate([wide, small], axis=1), near_down, all_out)
+    all_q = lax.all_gather(pin(q_grad, all_out)[0], "ep")
+    far_down = other_half(pin(far, near_down)[0])
+    wide, y, far_down = pin(exchange(wide), y, far_down)
     normed_grad = sum_four(y)
-    wide, normed_grad, other_down = pin(broadcast(wide), normed_grad, other_down)
+    wide, normed_grad, all_q = pin(
+        broadcast(jnp.sum(wide.astype(f32), axis=0).astype(bf16)), normed_grad, all_q
+    )
     input_grads = (resid_grad + norm_back(own, root, normed_grad, gain_one)).astype(bf16)
-    down_grad = down_part.astype(f32) + other_down.astype(f32)
-    small = wide[:, lines:].reshape(CHIPS, -1)[:, :per_chip].reshape(-1)[:small_count]
-    small = small.reshape(experts + 2, width)
+    down_grad = jnp.concatenate(
+        [near.astype(f32) + near_down.astype(f32), far.astype(f32) + far_down.astype(f32)], axis=0
+    )
+    small = wide[:, lines:].reshape(-1)[:small_count].reshape(experts + 2, width)
     small = small.astype(f32) + other_core(small).astype(f32)
     small = small + other_half(small.astype(bf16)).astype(f32)
-    wide = wide[:, :lines].reshape(width, all_width)
+    wide = wide[:, :lines].reshape(width, kv_width)
     other_wide = other_core(wide)
 
     def both_cores(start, end):
         return in_order(wide[:, start:end], other_wide[:, start:end], core, 1).astype(f32)
 
-    grad_q = both_cores(0, 3 * LANES)
-    grad_k = both_cores(3 * LANES, 4 * LANES)
-    grad_v = both_cores(4 * LANES, 5 * LANES)
+    grad_k = both_cores(0, LANES)
+    grad_v = both_cores(LANES, 2 * LANES)
+    all_q = all_q.reshape(CHIPS, 2, -1, 3 * LANES)
+    grad_q = jnp.concatenate(
+        [all_q[:, c].reshape(width, -1) for c in range(2)], axis=1
+    ).astype(f32)
     all_out = all_out.reshape(CHIPS, 2, -1, width)
     grad_out = jnp.concatenate(
         [all_out[:, c].reshape(-1, width) for c in range(2)], axis=0

time: 737 us -> 714 us (0.969)
  starting transfers between devices: 184 us -> 170 us
  waiting for transfers between devices: 288 us -> 280 us
  local copies, waits for them, and re-layouts: 48.3 us -> 40.7 us
    ppermute x14 -> x13, waiting for transfers between devices: 40.9 us -> 30 us  [other_half(): return lax.ppermute(value, 'tp', [(0, 1), (1, 0)])]
    ppermute x38, starting transfers between devices: 58.1 us -> 47.3 us  [other_core(): return lax.ppermute(value, 'ep', [(i, i ^ 1) for i in range(2 * CHIPS)])]
    ppermute x30, waiting for transfers between devices: 86.7 us -> 96.5 us  [from_ring(): lax.ppermute(value, 'ep', ring(stage, -d))]
    unnamed x288 -> x306, local copies, waits for them, and re-layouts: 27.5 us -> 19.2 us
    pallas_call x9 -> x10, Pallas kernels: 120 us -> 123 us  [local_call(): pl.pallas_call(kernel, grid=(micros,), out_shape=[jax.ShapeDtypeStruct((m...]
    ppermute x14 -> x13, starting transfers between devices: 14.8 us -> 15 us  [other_half(): return lax.ppermute(value, 'tp', [(0, 1), (1, 0)])]
  transfers between devices with their start and end apart: 127 -> 128, of which waited for: 77 -> 80; matrix products, arithmetic and copies ran while one was open for 8% -> 11% of each run, Pallas kernels for 10% -> 11%
where the time goes in v2:
time: 714 us; the launch traced here: 703 us
  waiting for transfers between devices  280 us (39%)
  starting transfers between devices  170 us (24%)
  Pallas kernels  130 us (18%)
  other arithmetic  59.9 us (8%)
  local copies, waits for them, and re-layouts  40.7 us (6%)
  between operations  16.4 us (2%)
    pallas_call x10, Pallas kernels, local_call(): pl.pallas_call(kernel, grid=(micros,), out_shape=[jax.ShapeDtypeStruct((m...  123 us
    ppermute x36, waiting for transfers between devices, to_ring(): lax.ppermute(pieces[d], 'ep', ring(stage, d))  98.2 us
    ppermute x30, waiting for transfers between devices, from_ring(): lax.ppermute(value, 'ep', ring(stage, -d))  96.5 us
    ppermute x38, starting transfers between devices, other_core(): return lax.ppermute(value, 'ep', [(i, i ^ 1) for i in range(2 * CHIPS)])  47.3 us
    ppermute x36, starting transfers between devices, to_ring(): lax.ppermute(pieces[d], 'ep', ring(stage, d))  41.7 us
    ppermute x30, starting transfers between devices, from_ring(): lax.ppermute(value, 'ep', ring(stage, -d))  32 us
    ppermute x13, waiting for transfers between devices, other_half(): return lax.ppermute(value, 'tp', [(0, 1), (1, 0)])  30 us
    all_to_all x5, starting transfers between devices, exchange(): lax.all_to_all(pieces, 'ep', 0, 0, tiled=True, axis_index_groups=groups)  26 us
  transfers between devices with their start and end apart: 128, of which 80 were waited for; matrix products, arithmetic and copies ran while one was open for 11% of the time, Pallas kernels for 11%

profile of v2, /device:TPU:1, one launch (start us, length us, event | category | flops | bytes accessed | tf_op | source)
XLA Modules:
  0.0 703.4 jit_solution(859299759076364607)
XLA Ops:
  33.5 7.7 %collective-permute-done.4.kv1 = bf16[2,512,256]{2,1,0:T(8,128)(2,1)} collective-permute-done((bf16[2,512,256]{2,1,0:T(8,128)(2,1)S(1)}, bf16[2,512,256]{2,1,0:T(8,128)(2,1)}, u32[]{:S(2)}, u32[]{:S(2)}) %collective-permute-start.4) | collective-permute-done | bytes 524320 | tf_op jit(solution)/shard_map/ppermute | solution.py:407
  46.9 8.5 %shard_map.221 = (bf16[2,128,384]{2,1,0:T(8,128)(2,1)}, f32[2,8,768]{2,1,0:T(8,128)}, bf16[2,128,1536]{2,1,0:T(8,128)(2,1)S(1)}) custom-call(s32[17]{0:T(128)S(1)} %pad_add_fusion.row_ref, bf16[384,1536]{1,0:T(8,128)(2,1)S(1)} %dynamic-slice_bitcast_fusion.1.wo_ref, bf16[2,128,384]{2,1,0:T(8,128)(2,1)S(1)} %bitcast.134, bf16[2,512,256]{2,1,0:T(8,128)(2,1)S(1)} %copy-done.33, ...), custom_call_target="tpu_custom_call" | custom-call | flops 3221225472 | bytes 4505668 | tf_op jit(solution)/shard_map/pallas_call | solution.py:71
  70.1 6.0 all-to-all-start
  88.8 9.8 %collective-permute-done.12.refs_1_ = bf16[2,128,1536]{2,1,0:T(8,128)(2,1)} collective-permute-done((bf16[2,128,1536]{2,1,0:T(8,128)(2,1)}, bf16[2,128,1536]{2,1,0:T(8,128)(2,1)}, u32[]{:S(2)}, u32[]{:S(2)}) %collective-permute-start.12) | collective-permute-done | bytes 786464 | tf_op jit(solution)/shard_map/ppermute | solution.py:407
  110.1 16.8 %shard_map.222 = (bf16[2,128,1536]{2,1,0:T(8,128)(2,1)S(1)}, bf16[2,128,1536]{2,1,0:T(8,128)(2,1)S(1)}, bf16[2,128,1536]{2,1,0:T(8,128)(2,1)S(1)}, bf16[2,128,15...) custom-call(s32[8]{0:T(128)S(1)} %pad_add_fusion.1.s_ref, ...), custom_call_target="tpu_custom_call" | custom-call | flops 10066329600 | bytes 25198624 | tf_op jit(solution)/shard_map/pallas_call | solution.py:71
  135.9 6.0 collective-permute-done.21
  141.9 9.2 %collective-permute-done.23 = bf16[2,128,1536]{2,1,0:T(8,128)(2,1)S(1)} collective-permute-done((bf16[2,128,1536]{2,1,0:T(8,128)(2,1)S(1)}, bf16[2,128,1536]{2,1,0:T(8,128)(2,1)S(1)}, u32[]{:S(2)}, u32[]{:S(2)}) %collective-permute-start.23) | collective-permute-done | bytes 786464 | tf_op jit(solution)/shard_map/ppermute | solution.py:412
  170.5 5.7 collective-permute-done.30
  193.0 11.1 %collective-permute-done.35.kv1 = bf16[2,512,256]{2,1,0:T(8,128)(2,1)S(1)} collective-permute-done((bf16[2,512,256]{2,1,0:T(8,128)(2,1)S(1)}, bf16[2,512,256]{2,1,0:T(8,128)(2,1)S(1)}, u32[]{:S(2)}, u32[]{:S(2)}) %collective-permute-start.35) | collective-permute-done | bytes 524320 | tf_op jit(solution)/shard_map/ppermute | solution.py:407
  207.8 7.7 %shard_map.224 = (bf16[2,128,384]{2,1,0:T(8,128)(2,1)S(1)}, f32[2,8,768]{2,1,0:T(8,128)S(1)}, bf16[2,128,1536]{2,1,0:T(8,128)(2,1)S(1)}) custom-call(s32[17]{0:T(128)S(1)} %pad_add_fusion.row_ref, bf16[384,1536]{1,0:T(8,128)(2,1)S(1)} %copy-done.12, bf16[2,128,384]{2,1,0:T(8,128)(2,1)S(1)} %bitcast.131, bf16[2,512,256]{2,1,0:T(8,128)(2,1)S(1)} %pad_maximum_fusion.9.kv0, ...), custom_call_target="tpu_custom_call" | custom-call | flops 3221225472 | bytes 4505668 | tf_op jit(solution)/shard_map/pallas_call | solution.py:71
  240.6 7.1 %collective-permute-done.43.refs_1_ = bf16[2,128,1536]{2,1,0:T(8,128)(2,1)S(1)} collective-permute-done((bf16[2,128,1536]{2,1,0:T(8,128)(2,1)S(1)}, bf16[2,128,1536]{2,1,0:T(8,128)(2,1)S(1)}, u32[]{:S(2)}, u32[]{:S(2)}) %collective-permute-start.43) | collective-permute-done | bytes 786464 | tf_op jit(solution)/shard_map/ppermute | solution.py:407
  264.4 16.7 %shard_map.225 = (bf16[2,128,1536]{2,1,0:T(8,128)(2,1)S(1)}, bf16[2,128,1536]{2,1,0:T(8,128)(2,1)S(1)}, bf16[2,128,1536]{2,1,0:T(8,128)(2,1)S(1)}, bf16[2,128,15...) custom-call(s32[8]{0:T(128)S(1)} %pad_add_fusion.1.s_ref, ...), custom_call_target="tpu_custom_call" | custom-call | flops 10066329600 | bytes 25198624 | tf_op jit(solution)/shard_map/pallas_call | solution.py:71
  283.2 16.2 %shard_map.226 = (bf16[2,128,1536]{2,1,0:T(8,128)(2,1)}, bf16[2,128,1536]{2,1,0:T(8,128)(2,1)}, bf16[2,128,1536]{2,1,0:T(8,128)(2,1)}, bf16[2,128,1536]{2,1,0:T(...) custom-call(s32[8]{0:T(128)S(1)} %pad_add_fusion.1.s_ref, ...), custom_call_target="tpu_custom_call" | custom-call | flops 10066329600 | bytes 27164704 | tf_op jit(solution)/shard_map/pallas_call | solution.py:71
  310.7 14.4 %collective-permute-done.52 = bf16[2,128,1536]{2,1,0:T(8,128)(2,1)S(1)} collective-permute-done((bf16[2,128,1536]{2,1,0:T(8,128)(2,1)S(1)}, bf16[2,128,1536]{2,1,0:T(8,128)(2,1)S(1)}, u32[]{:S(2)}, u32[]{:S(2)}) %collective-permute-start.52) | collective-permute-done | bytes 786464 | tf_op jit(solution)/shard_map/ppermute | solution.py:412
  352.0 13.6 %shard_map.227 = (bf16[2,128,384]{2,1,0:T(8,128)(2,1)}, bf16[2,512,256]{2,1,0:T(8,128)(2,1)}, bf16[2,512,256]{2,1,0:T(8,128)(2,1)}, bf16[2,512,256]{2,1,0:T(8,128)(2,1)}, bf16[2,512,256]{2,1,0:T(8,128)(2,1)}) custom-call(s32[17]{0:T(128)} %copy-done.61, bf16[384,1536]{1,0:T(8,128)(2,1)} %copy-done.11, f32[128,128]{1,0:T(8,128)} %copy.68.cos_ref, ...), custom_call_target="tpu_custom_call" | custom-call | flops 8053063680 | bytes 6930500 | tf_op jit(solution)/shard_map/pallas_call | solution.py:71
  374.9 5.8 collective-permute-done.69
  380.8 6.2 collective-permute-done.70
  417.1 5.5 collective-permute-done.81
  437.4 8.8 %collective-permute-done.86.refs_1_ = bf16[2,128,1536]{2,1,0:T(8,128)(2,1)S(1)} collective-permute-done((bf16[2,128,1536]{2,1,0:T(8,128)(2,1)S(1)}, bf16[2,128,1536]{2,1,0:T(8,128)(2,1)S(1)}, u32[]{:S(2)}, u32[]{:S(2)}) %collective-permute-start.86) | collective-permute-done | bytes 786464 | tf_op jit(solution)/shard_map/ppermute | solution.py:407
  448.2 8.4 %collective-permute-done.88.refs_3_ = bf16[2,128,1536]{2,1,0:T(8,128)(2,1)S(1)} collective-permute-done((bf16[2,128,1536]{2,1,0:T(8,128)(2,1)S(1)}, bf16[2,128,1536]{2,1,0:T(8,128)(2,1)S(1)}, u32[]{:S(2)}, u32[]{:S(2)}) %collective-permute-start.88) | collective-permute-done | bytes 786464 | tf_op jit(solution)/shard_map/ppermute | solution.py:407
  456.6 6.5 collective-permute-start.89
  469.4 15.9 %shard_map.229 = (bf16[2,128,1536]{2,1,0:T(8,128)(2,1)}, bf16[2,128,1536]{2,1,0:T(8,128)(2,1)}, bf16[2,128,1536]{2,1,0:T(8,128)(2,1)}, bf16[2,128,1536]{2,1,0:T(...) custom-call(s32[8]{0:T(128)S(1)} %pad_add_fusion.1.s_ref, ...), custom_call_target="tpu_custom_call" | custom-call | flops 10066329600 | bytes 27164704 | tf_op jit(solution)/shard_map/pallas_call | solution.py:71
  496.5 13.7 %collective-permute-done.96 = bf16[2,128,1536]{2,1,0:T(8,128)(2,1)S(1)} collective-permute-done((bf16[2,128,1536]{2,1,0:T(8,128)(2,1)S(1)}, bf16[2,128,1536]{2,1,0:T(8,128)(2,1)S(1)}, u32[]{:S(2)}, u32[]{:S(2)}) %collective-permute-start.96) | collective-permute-done | bytes 786464 | tf_op jit(solution)/shard_map/ppermute | solution.py:412
  515.9 5.5 collective-permute-done.102
  535.8 5.7 all-to-all-start.1
  543.8 13.5 %shard_map.231 = (bf16[2,128,384]{2,1,0:T(8,128)(2,1)}, bf16[2,512,256]{2,1,0:T(8,128)(2,1)}, bf16[2,512,256]{2,1,0:T(8,128)(2,1)}, bf16[2,512,256]{2,1,0:T(8,128)(2,1)}, bf16[2,512,256]{2,1,0:T(8,128)(2,1)}) custom-call(s32[17]{0:T(128)} %copy-done.61, bf16[384,1536]{1,0:T(8,128)(2,1)} %copy-done.11, f32[128,128]{1,0:T(8,128)} %copy.68.cos_ref, ...), custom_call_target="tpu_custom_call" | custom-call | flops 8053063680 | bytes 6930500 | tf_op jit(solution)/shard_map/pallas_call | solution.py:71
  563.5 5.3 all-to-all-start.2
  573.8 13.3 %shard_map.232 = (f32[1536,640]{1,0:T(8,128)}, f32[1536,640]{1,0:T(8,128)}, bf16[256,1536]{1,0:T(8,128)(2,1)}, bf16[384,1536]{1,0:T(8,128)(2,1)}) custom-call(s32[8]{0:T(128)} %copy-done.54, bf16[2,512,1536]{2,1,0:T(8,128)(2,1)} %get-tuple-element.194.b_own, bf16[2,256,1536]{2,1,0:T(8,128)(2,1)} %collective-permute-done.75.o0, ...), custom_call_target="tpu_custom_call" | custom-call | flops 5033164800 | bytes 12714016 | tf_op jit(solution)/shard_map/pallas_call | solution.py:71
  592.0 6.3 collective-permute-done.108
  639.1 6.9 all-to-all-done.3
  646.1 5.6 collective-permute-done.114
  671.0 7.0 all-to-all-done.4
  (713 shorter events, 390.7 us)
Async XLA Ops:
  76.1 497.8 %all-gather.7.cloned.1.call-start = ((), (), s32[]{:S(2)}) async-start(), calls=%async_computation.5 | async-start | bytes 3932160 | tf_op jit(solution)/shard_map/all_gather | solution.py:744
  78.2 20.4 %collective-permute-start.12 = (bf16[2,128,1536]{2,1,0:T(8,128)(2,1)}, bf16[2,128,1536]{2,1,0:T(8,128)(2,1)}, u32[]{:S(2)}, u32[]{:S(2)}) collective-permute-start(bf16[2,128,1536]{2,1,0:T(8,128)(2,1)} %pad_maximum_fusion.3.refs_0_), channel_id=1, source_target_pairs={{0,12},{2,50},{4,0},{6,54},{8,4},{10,58},{12,8},{14,62},{16,28},{1... | collective-permute-start | bytes 2359304 | tf_op jit(solution)/shard_map/ppermute | solution.py:407
  81.4 20.9 %collective-permute-start.14 = (bf16[2,128,1536]{2,1,0:T(8,128)(2,1)}, bf16[2,128,1536]{2,1,0:T(8,128)(2,1)}, u32[]{:S(2)}, u32[]{:S(2)}) collective-permute-start(bf16[2,128,1536]{2,1,0:T(8,128)(2,1)} %pad_maximum_fusion.3.refs_0_), channel_id=1, source_target_pairs={{0,4},{2,18},{4,8},{6,22},{8,12},{10,26},{12,0},{14,30},{16,20},{1... | collective-permute-start | bytes 2359304 | tf_op jit(solution)/shard_map/ppermute | solution.py:407
  131.9 19.1 %collective-permute-start.23 = (bf16[2,128,1536]{2,1,0:T(8,128)(2,1)S(1)}, bf16[2,128,1536]{2,1,0:T(8,128)(2,1)S(1)}, u32[]{:S(2)}, u32[]{:S(2)}) collective-permute-start(bf16[2,128,1536]{2,1,0:T(8,128)(2,1)S(1)} %add_convert_fusion.17), channel_id=1, source_target_pairs={{0,8},{2,34},{4,12},{6,38},{8,0},{10,42},{12,4},{14,46},{16,24},{1... | collective-permute-start | bytes 2359304 | tf_op jit(solution)/shard_map/ppermute | solution.py:412
  237.1 20.8 %collective-permute-start.45 = (bf16[2,128,1536]{2,1,0:T(8,128)(2,1)S(1)}, bf16[2,128,1536]{2,1,0:T(8,128)(2,1)S(1)}, u32[]{:S(2)}, u32[]{:S(2)}) collective-permute-start(bf16[2,128,1536]{2,1,0:T(8,128)(2,1)S(1)} %pad_maximum_fusion.5.refs_0_), channel_id=1, source_target_pairs={{0,4},{2,18},{4,8},{6,22},{8,12},{10,26},{12,0},{14,30},{16,20},{1... | collective-permute-start | bytes 2359304 | tf_op jit(solution)/shard_map/ppermute | solution.py:407
  238.0 23.5 %collective-permute-start.46 = (bf16[2,128,1536]{2,1,0:T(8,128)(2,1)S(1)}, bf16[2,128,1536]{2,1,0:T(8,128)(2,1)S(1)}, u32[]{:S(2)}, u32[]{:S(2)}) collective-permute-start(bf16[2,128,1536]{2,1,0:T(8,128)(2,1)S(1)} %pad_maximum_fusion.5.refs_0_), channel_id=1, source_target_pairs={{0,2},{2,0},{4,6},{6,4},{8,10},{10,8},{12,14},{14,12},{16,18},{18,... | collective-permute-start | bytes 2359304 | tf_op jit(solution)/shard_map/ppermute | solution.py:388
  281.9 18.7 %collective-permute-start.63 = (bf16[2,128,1536]{2,1,0:T(8,128)(2,1)}, bf16[2,128,1536]{2,1,0:T(8,128)(2,1)S(1)}, u32[]{:S(2)}, u32[]{:S(2)}) collective-permute-start(bf16[2,128,1536]{2,1,0:T(8,128)(2,1)} %get-tuple-element.192), channel_id=1, source_target_pairs={{0,2},{2,0},{4,6},{6,4},{8,10},{10,8},{12,14},{14,12},{16,18},{18,... | collective-permute-start | bytes 2359304 | tf_op jit(solution)/shard_map/ppermute | solution.py:388
  304.3 20.8 %collective-permute-start.52 = (bf16[2,128,1536]{2,1,0:T(8,128)(2,1)S(1)}, bf16[2,128,1536]{2,1,0:T(8,128)(2,1)S(1)}, u32[]{:S(2)}, u32[]{:S(2)}) collective-permute-start(bf16[2,128,1536]{2,1,0:T(8,128)(2,1)S(1)} %add_convert_fusion.13), channel_id=1, source_target_pairs={{0,4},{2,18},{4,8},{6,22},{8,12},{10,26},{12,0},{14,30},{16,20},{1... | collective-permute-start | bytes 2359304 | tf_op jit(solution)/shard_map/ppermute | solution.py:412
  306.5 18.5 %collective-permute-start.54 = (bf16[2,128,1536]{2,1,0:T(8,128)(2,1)S(1)}, bf16[2,128,1536]{2,1,0:T(8,128)(2,1)S(1)}, u32[]{:S(2)}, u32[]{:S(2)}) collective-permute-start(bf16[2,128,1536]{2,1,0:T(8,128)(2,1)S(1)} %add_convert_fusion.12), channel_id=1, source_target_pairs={{0,8},{2,34},{4,12},{6,38},{8,0},{10,42},{12,4},{14,46},{16,24},{1... | collective-permute-start | bytes 2359304 | tf_op jit(solution)/shard_map/ppermute | solution.py:412
  307.4 18.8 %collective-permute-start.56 = (bf16[2,128,1536]{2,1,0:T(8,128)(2,1)S(1)}, bf16[2,128,1536]{2,1,0:T(8,128)(2,1)S(1)}, u32[]{:S(2)}, u32[]{:S(2)}) collective-permute-start(bf16[2,128,1536]{2,1,0:T(8,128)(2,1)S(1)} %add_convert_fusion.11), channel_id=1, source_target_pairs={{0,12},{2,50},{4,0},{6,54},{8,4},{10,58},{12,8},{14,62},{16,28},{1... | collective-permute-start | bytes 2359304 | tf_op jit(solution)/shard_map/ppermute | solution.py:412
  309.6 19.9 %collective-permute-start.60 = (bf16[2,128,1536]{2,1,0:T(8,128)(2,1)S(1)}, bf16[2,128,1536]{2,1,0:T(8,128)(2,1)S(1)}, u32[]{:S(2)}, u32[]{:S(2)}) collective-permute-start(bf16[2,128,1536]{2,1,0:T(8,128)(2,1)S(1)} %get-tuple-element.186), channel_id=1, source_target_pairs={{0,2},{2,0},{4,6},{6,4},{8,10},{10,8},{12,14},{14,12},{16,18},{18,... | collective-permute-start | bytes 2359304 | tf_op jit(solution)/shard_map/ppermute | solution.py:388
  346.3 19.3 %collective-permute-start.66 = (bf16[2,128,1536]{2,1,0:T(8,128)(2,1)}, bf16[2,128,1536]{2,1,0:T(8,128)(2,1)}, u32[]{:S(2)}, u32[]{:S(2)}) collective-permute-start(bf16[2,128,1536]{2,1,0:T(8,128)(2,1)} %add_convert_fusion.8), channel_id=1, source_target_pairs={{0,4},{2,18},{4,8},{6,22},{8,12},{10,26},{12,0},{14,30},{16,20},{1... | collective-permute-start | bytes 2359304 | tf_op jit(solution)/shard_map/ppermute | solution.py:412
  346.3 21.9 %collective-permute-start.67 = (bf16[2,128,1536]{2,1,0:T(8,128)(2,1)}, bf16[2,128,1536]{2,1,0:T(8,128)(2,1)}, u32[]{:S(2)}, u32[]{:S(2)}) collective-permute-start(bf16[2,128,1536]{2,1,0:T(8,128)(2,1)} %add_convert_fusion.7), channel_id=1, source_target_pairs={{0,8},{2,34},{4,12},{6,38},{8,0},{10,42},{12,4},{14,46},{16,24},{1... | collective-permute-start | bytes 2359304 | tf_op jit(solution)/shard_map/ppermute | solution.py:412
  349.8 18.4 %collective-permute-start.68 = (bf16[2,128,1536]{2,1,0:T(8,128)(2,1)}, bf16[2,128,1536]{2,1,0:T(8,128)(2,1)}, u32[]{:S(2)}, u32[]{:S(2)}) collective-permute-start(bf16[2,128,1536]{2,1,0:T(8,128)(2,1)} %add_convert_fusion.6), channel_id=1, source_target_pairs={{0,12},{2,50},{4,0},{6,54},{8,4},{10,58},{12,8},{14,62},{16,28},{1... | collective-permute-start | bytes 2359304 | tf_op jit(solution)/shard_map/ppermute | solution.py:412
  350.9 45.1 %collective-permute-start.75 = (bf16[2,256,1536]{2,1,0:T(8,128)(2,1)}, bf16[2,256,1536]{2,1,0:T(8,128)(2,1)}, u32[]{:S(2)}, u32[]{:S(2)}) collective-permute-start(bf16[2,256,1536]{2,1,0:T(8,128)(2,1)} %slice.142), channel_id=1, source_target_pairs={{0,1},{1,0},{2,3},{3,2},{4,5},{5,4},{6,7},{7,6},{8,9},{9,8},{10,11... | collective-permute-start | bytes 4718600 | tf_op jit(solution)/shard_map/ppermute | solution.py:392
  436.5 20.1 %collective-permute-start.88 = (bf16[2,128,1536]{2,1,0:T(8,128)(2,1)S(1)}, bf16[2,128,1536]{2,1,0:T(8,128)(2,1)S(1)}, u32[]{:S(2)}, u32[]{:S(2)}) collective-permute-start(bf16[2,128,1536]{2,1,0:T(8,128)(2,1)S(1)} %constant_dynamic-update-slice_fusion.refs_0_), channel_id=1, source_target_pairs={{0,4},{2,18},{4,8},{6,22},{8,12},{10,26},{12,0},{14,30},{16,20},{1... | collective-permute-start | bytes 2359304 | tf_op jit(solution)/shard_map/ppermute | solution.py:407
  463.7 21.6 %collective-permute-start.93 = (bf16[2,128,1536]{2,1,0:T(8,128)(2,1)S(1)}, bf16[2,128,1536]{2,1,0:T(8,128)(2,1)S(1)}, u32[]{:S(2)}, u32[]{:S(2)}) collective-permute-start(bf16[2,128,1536]{2,1,0:T(8,128)(2,1)S(1)} %get-tuple-element.235), channel_id=1, source_target_pairs={{0,1},{1,0},{2,3},{3,2},{4,5},{5,4},{6,7},{7,6},{8,9},{9,8},{10,11... | collective-permute-start | bytes 2359304 | tf_op jit(solution)/shard_map/ppermute | solution.py:392
  489.4 20.8 %collective-permute-start.96 = (bf16[2,128,1536]{2,1,0:T(8,128)(2,1)S(1)}, bf16[2,128,1536]{2,1,0:T(8,128)(2,1)S(1)}, u32[]{:S(2)}, u32[]{:S(2)}) collective-permute-start(bf16[2,128,1536]{2,1,0:T(8,128)(2,1)S(1)} %add_convert_fusion.3), channel_id=1, source_target_pairs={{0,4},{2,18},{4,8},{6,22},{8,12},{10,26},{12,0},{14,30},{16,20},{1... | collective-permute-start | bytes 2359304 | tf_op jit(solution)/shard_map/ppermute | solution.py:412
  491.1 19.2 %collective-permute-start.98 = (bf16[2,128,1536]{2,1,0:T(8,128)(2,1)S(1)}, bf16[2,128,1536]{2,1,0:T(8,128)(2,1)S(1)}, u32[]{:S(2)}, u32[]{:S(2)}) collective-permute-start(bf16[2,128,1536]{2,1,0:T(8,128)(2,1)S(1)} %add_convert_fusion.2), channel_id=1, source_target_pairs={{0,8},{2,34},{4,12},{6,38},{8,0},{10,42},{12,4},{14,46},{16,24},{1... | collective-permute-start | bytes 2359304 | tf_op jit(solution)/shard_map/ppermute | solution.py:412
  493.4 19.2 %collective-permute-start.100 = (bf16[2,128,1536]{2,1,0:T(8,128)(2,1)S(1)}, bf16[2,128,1536]{2,1,0:T(8,128)(2,1)S(1)}, u32[]{:S(2)}, u32[]{:S(2)}) collective-permute-start(bf16[2,128,1536]{2,1,0:T(8,128)(2,1)S(1)} %add_convert_fusion.1), channel_id=1, source_target_pairs={{0,12},{2,50},{4,0},{6,54},{8,4},{10,58},{12,8},{14,62},{16,28},{1... | collective-permute-start | bytes 2359304 | tf_op jit(solution)/shard_map/ppermute | solution.py:412
  494.1 18.9 %collective-permute-start.101 = (bf16[2,128,1536]{2,1,0:T(8,128)(2,1)S(1)}, bf16[2,128,1536]{2,1,0:T(8,128)(2,1)S(1)}, u32[]{:S(2)}, u32[]{:S(2)}) collective-permute-start(bf16[2,128,1536]{2,1,0:T(8,128)(2,1)S(1)} %get-tuple-element.253), channel_id=1, source_target_pairs={{0,1},{1,0},{2,3},{3,2},{4,5},{5,4},{6,7},{7,6},{8,9},{9,8},{10,11... | collective-permute-start | bytes 2359304 | tf_op jit(solution)/shard_map/ppermute | solution.py:392
  535.8 22.8 %all-to-all-start.1 = ((bf16[16,24,1536]{2,1,0:T(8,128)(2,1)}), bf16[16,24,1536]{2,1,0:T(8,128)(2,1)}, u32[]{:S(2)}, u32[]{:S(2)}) async-start(bf16[16,24,1536]{2,1,0:T(8,128)(2,1)} %bitcast.145), calls=%async_computation.1 | async-start | bytes 2359296 | tf_op jit(solution)/shard_map/all_to_all | solution.py:443
  541.6 83.9 %all-gather.9.cloned.1.call-start = ((), (), s32[]{:S(2)}) async-start(), calls=%async_computation.6 | async-start | bytes 2433024 | tf_op jit(solution)/shard_map/all_gather | solution.py:769
  563.5 37.2 %all-to-all-start.2 = ((bf16[16,96,384]{2,1,0:T(8,128)(2,1)}), bf16[16,96,384]{2,1,0:T(8,128)(2,1)}, u32[]{:S(2)}, u32[]{:S(2)}) async-start(bf16[16,96,384]{2,1,0:T(8,128)(2,1)} %bitcast.135), calls=%async_computation.2 | async-start | bytes 2359296 | tf_op jit(solution)/shard_map/all_to_all | solution.py:443
  568.8 112.4 %all-gather.11.cloned.1.call-start = ((), (), s32[]{:S(2)}) async-start(), calls=%async_computation.7 | async-start | bytes 2433024 | tf_op jit(solution)/shard_map/all_gather | solution.py:788
  568.9 23.2 %collective-permute-start.107 = (bf16[2,512,256]{2,1,0:T(8,128)(2,1)}, bf16[2,512,256]{2,1,0:T(8,128)(2,1)}, u32[]{:S(2)}, u32[]{:S(2)}) collective-permute-start(bf16[2,512,256]{2,1,0:T(8,128)(2,1)} %get-tuple-element.257), channel_id=1, source_target_pairs={{0,4},{2,18},{4,8},{6,22},{8,12},{10,26},{12,0},{14,30},{16,20},{1... | collective-permute-start | bytes 1572872 | tf_op jit(solution)/shard_map/ppermute | solution.py:412
  570.2 28.1 %collective-permute-start.108 = (bf16[2,512,256]{2,1,0:T(8,128)(2,1)}, bf16[2,512,256]{2,1,0:T(8,128)(2,1)}, u32[]{:S(2)}, u32[]{:S(2)}) collective-permute-start(bf16[2,512,256]{2,1,0:T(8,128)(2,1)} %get-tuple-element.258), channel_id=1, source_target_pairs={{0,8},{2,34},{4,12},{6,38},{8,0},{10,42},{12,4},{14,46},{16,24},{1... | collective-permute-start | bytes 1572872 | tf_op jit(solution)/shard_map/ppermute | solution.py:412
  572.6 25.7 %collective-permute-start.109 = (bf16[2,512,256]{2,1,0:T(8,128)(2,1)}, bf16[2,512,256]{2,1,0:T(8,128)(2,1)}, u32[]{:S(2)}, u32[]{:S(2)}) collective-permute-start(bf16[2,512,256]{2,1,0:T(8,128)(2,1)} %get-tuple-element.259), channel_id=1, source_target_pairs={{0,12},{2,50},{4,0},{6,54},{8,4},{10,58},{12,8},{14,62},{16,28},{1... | collective-permute-start | bytes 1572872 | tf_op jit(solution)/shard_map/ppermute | solution.py:412
  607.3 18.1 %collective-permute-start.113 = (bf16[256,1536]{1,0:T(8,128)(2,1)}, bf16[256,1536]{1,0:T(8,128)(2,1)}, u32[]{:S(2)}, u32[]{:S(2)}) collective-permute-start(bf16[256,1536]{1,0:T(8,128)(2,1)} %get-tuple-element.276), channel_id=1, source_target_pairs={{0,1},{1,0},{2,3},{3,2},{4,5},{5,4},{6,7},{7,6},{8,9},{9,8},{10,11... | collective-permute-start | bytes 2359304 | tf_op jit(solution)/shard_map/ppermute | solution.py:392
  626.3 25.4 %collective-permute-start.114 = (bf16[384,1536]{1,0:T(8,128)(2,1)}, bf16[384,1536]{1,0:T(8,128)(2,1)}, u32[]{:S(2)}, u32[]{:S(2)}) collective-permute-start(bf16[384,1536]{1,0:T(8,128)(2,1)} %get-tuple-element.282), channel_id=1, source_target_pairs={{0,1},{1,0},{2,3},{3,2},{4,5},{5,4},{6,7},{7,6},{8,9},{9,8},{10,11... | collective-permute-start | bytes 3538952 | tf_op jit(solution)/shard_map/ppermute | solution.py:392
  627.3 18.8 %all-to-all-start.3 = ((bf16[16,112,256]{2,1,0:T(8,128)(2,1)}), bf16[16,112,256]{2,1,0:T(8,128)(2,1)S(1)}, u32[]{:S(2)}, u32[]{:S(2)}) async-start(bf16[16,112,256]{2,1,0:T(8,128)(2,1)} %pad_maximum_fusion.1), calls=%async_computation.3 | async-start | bytes 1835008 | tf_op jit(solution)/shard_map/all_to_all | solution.py:443
  656.9 21.1 %all-to-all-start.4 = ((bf16[16,112,256]{2,1,0:T(8,128)(2,1)}), bf16[16,112,256]{2,1,0:T(8,128)(2,1)}, u32[]{:S(2)}, u32[]{:S(2)}) async-start(bf16[16,112,256]{2,1,0:T(8,128)(2,1)} %broadcast_in_dim.42), calls=%async_computation.4 | async-start | bytes 1835008 | tf_op jit(solution)/shard_map/all_to_all | solution.py:443
  (247 other events, 2968.5 us)
Sparse Core Ops, SparseCore 0:
  524.2 44.1 all-gather.6
  570.6 54.4 all-gather.8
  627.4 53.7 all-gather.10

commit v3 on v2

--- a/solution.py
+++ b/solution.py
@@ -745,7 +745,7 @@
     out_w_grad = tn(o.reshape(both_rows, -1), out_grad.reshape(both_rows, width)).astype(bf16)
     out_w_grad = exchange(out_w_grad.reshape(CHIPS, -1, width))
     dq, *dkv = attend_back(q, kv_all, out_grad, log_total, o)
-    dq, out_w_grad = pin(dq, out_w_grad)
+    dq, out_w_grad, h = pin(dq, out_w_grad, h)
     out_w_grad = jnp.sum(out_w_grad.astype(f32), axis=0).astype(bf16)
     near_rows = 2 * BLOCK
     gate_grad, up_grad, near, far = local_call(
@@ -767,14 +767,12 @@
         micros=micros,
     )
     all_out = lax.all_gather(out_w_grad, "ep")
-    q_grad = tn(a, dq.reshape(both_rows, -1)).astype(bf16)
+    near_down = other_half(near)
+    arrived, (gate_grad, up_grad, late_dq) = to_owners(dkv, (gate_grad, up_grad, dq))
+    q_grad = tn(a, late_dq.reshape(both_rows, -1)).astype(bf16)
     q_grad = exchange(q_grad.reshape(CHIPS, -1, 3 * LANES))
-    arrived, (gate_grad, up_grad, near, far, q_grad) = to_owners(
-        dkv, (gate_grad, up_grad, near, far, q_grad)
-    )
-    q_grad = jnp.sum(q_grad.astype(f32), axis=0).astype(bf16)
+    *arrived, near_down = pin(*arrived, near_down)
     dqkv, y, gain_one_grad = after_keys(arrived, dq, x128)
-    near_down = other_half(near)
 
     kv_width = 2 * LANES
     small = jnp.concatenate([router_grad[:experts], gain_one_grad, gain_two_grad[None]], axis=0)
@@ -784,33 +782,38 @@
     small = small.reshape(CHIPS, small_lines, kv_width).astype(bf16)
     wide = tn(a, dqkv[:, 3 * LANES :]).astype(bf16).reshape(CHIPS, -1, kv_width)
     lines = wide.shape[1]
-    wide, near_down, all_out = pin(jnp.concatenate([wide, small], axis=1), near_down, all_out)
-    all_q = lax.all_gather(pin(q_grad, all_out)[0], "ep")
     far_down = other_half(pin(far, near_down)[0])
-    wide, y, far_down = pin(exchange(wide), y, far_down)
+    wide, y, far_down, all_out, q_grad = pin(
+        exchange(jnp.concatenate([wide, small], axis=1)), y, far_down, all_out, q_grad
+    )
+    wide = jnp.sum(wide.astype(f32), axis=0).astype(bf16)
+    q_grad = jnp.sum(q_grad.astype(f32), axis=0).astype(bf16)
+    all_width = 5 * LANES
+    per_chip = small_lines * kv_width
+    small = wide[lines:].reshape(-1, LANES)
+    small = jnp.pad(small, ((0, -small.shape[0] % 5), (0, 0))).reshape(-1, all_width)
+    wide = jnp.concatenate(
+        [jnp.concatenate([q_grad, wide[:lines]], axis=1), small], axis=0
+    )
     normed_grad = sum_four(y)
-    wide, normed_grad, all_q = pin(
-        broadcast(jnp.sum(wide.astype(f32), axis=0).astype(bf16)), normed_grad, all_q
-    )
+    wide, normed_grad = pin(broadcast(wide), normed_grad)
     input_grads = (resid_grad + norm_back(own, root, normed_grad, gain_one)).astype(bf16)
     down_grad = jnp.concatenate(
         [near.astype(f32) + near_down.astype(f32), far.astype(f32) + far_down.astype(f32)], axis=0
     )
-    small = wide[:, lines:].reshape(-1)[:small_count].reshape(experts + 2, width)
+    small = wide[:, lines:].reshape(CHIPS, -1)[:, :per_chip].reshape(-1)[:small_count]
+    small = small.reshape(experts + 2, width)
     small = small.astype(f32) + other_core(small).astype(f32)
     small = small + other_half(small.astype(bf16)).astype(f32)
-    wide = wide[:, :lines].reshape(width, kv_width)
+    wide = wide[:, :lines].reshape(width, all_width)
     other_wide = other_core(wide)
 
     def both_cores(start, end):
         return in_order(wide[:, start:end], other_wide[:, start:end], core, 1).astype(f32)
 
-    grad_k = both_cores(0, LANES)
-    grad_v = both_cores(LANES, 2 * LANES)
-    all_q = all_q.reshape(CHIPS, 2, -1, 3 * LANES)
-    grad_q = jnp.concatenate(
-        [all_q[:, c].reshape(width, -1) for c in range(2)], axis=1
-    ).astype(f32)
+    grad_q = both_cores(0, 3 * LANES)
+    grad_k = both_cores(3 * LANES, 4 * LANES)
+    grad_v = both_cores(4 * LANES, 5 * LANES)
     all_out = all_out.reshape(CHIPS, 2, -1, width)
     grad_out = jnp.concatenate(
         [all_out[:, c].reshape(-1, width) for c in range(2)], axis=0

time: 714 us -> 729 us (1.021)
  waiting for transfers between devices: 280 us -> 301 us
    all_to_all x5, waiting for transfers between devices: 16.5 us -> 32.6 us  [exchange(): lax.all_to_all(pieces, 'ep', 0, 0, tiled=True, axis_index_groups=groups)]
    unnamed x306 -> x264, local copies, waits for them, and re-layouts: 19.2 us -> 10.9 us
  transfers between devices with their start and end apart: 128 -> 127, of which waited for: 80 -> 81; matrix products, arithmetic and copies ran while one was open for 11% -> 10% of each run, Pallas kernels for 11% -> 10%
where the time goes in v3:
time: 729 us; the launch traced here: 719 us
  waiting for transfers between devices  301 us (41%)
  starting transfers between devices  171 us (23%)
  Pallas kernels  128 us (18%)
  other arithmetic  63.1 us (9%)
  local copies, waits for them, and re-layouts  35.1 us (5%)
  between operations  16.6 us (2%)
    pallas_call x10, Pallas kernels, local_call(): pl.pallas_call(kernel, grid=(micros,), out_shape=[jax.ShapeDtypeStruct((m...  122 us
    ppermute x36, waiting for transfers between devices, to_ring(): lax.ppermute(pieces[d], 'ep', ring(stage, d))  105 us
    ppermute x30, waiting for transfers between devices, from_ring(): lax.ppermute(value, 'ep', ring(stage, -d))  97.1 us
    ppermute x38, starting transfers between devices, other_core(): return lax.ppermute(value, 'ep', [(i, i ^ 1) for i in range(2 * CHIPS)])  47.6 us
    ppermute x36, starting transfers between devices, to_ring(): lax.ppermute(pieces[d], 'ep', ring(stage, d))  41.4 us
    all_to_all x5, waiting for transfers between devices, exchange(): lax.all_to_all(pieces, 'ep', 0, 0, tiled=True, axis_index_groups=groups)  32.6 us
    ppermute x30, starting transfers between devices, from_ring(): lax.ppermute(value, 'ep', ring(stage, -d))  30.7 us
    all_to_all x5, starting transfers between devices, exchange(): lax.all_to_all(pieces, 'ep', 0, 0, tiled=True, axis_index_groups=groups)  28.3 us
  transfers between devices with their start and end apart: 127, of which 81 were waited for; matrix products, arithmetic and copies ran while one was open for 10% of the time, Pallas kernels for 10%

profile of v3, /device:TPU:1, one launch (start us, length us, event | category | flops | bytes accessed | tf_op | source)
XLA Modules:
  0.0 718.6 jit_solution(10337990535755053434)
XLA Ops:
  33.5 7.7 %collective-permute-done.4.kv1 = bf16[2,512,256]{2,1,0:T(8,128)(2,1)} collective-permute-done((bf16[2,512,256]{2,1,0:T(8,128)(2,1)S(1)}, bf16[2,512,256]{2,1,0:T(8,128)(2,1)}, u32[]{:S(2)}, u32[]{:S(2)}) %collective-permute-start.4) | collective-permute-done | bytes 524320 | tf_op jit(solution)/shard_map/ppermute | solution.py:407
  46.9 8.5 %shard_map.221 = (bf16[2,128,384]{2,1,0:T(8,128)(2,1)}, f32[2,8,768]{2,1,0:T(8,128)}, bf16[2,128,1536]{2,1,0:T(8,128)(2,1)S(1)}) custom-call(s32[17]{0:T(128)S(1)} %pad_add_fusion.row_ref, bf16[384,1536]{1,0:T(8,128)(2,1)S(1)} %dynamic-slice_bitcast_fusion.1.wo_ref, bf16[2,128,384]{2,1,0:T(8,128)(2,1)S(1)} %bitcast.137, bf16[2,512,256]{2,1,0:T(8,128)(2,1)S(1)} %copy-done.33, ...), custom_call_target="tpu_custom_call" | custom-call | flops 3221225472 | bytes 4505668 | tf_op jit(solution)/shard_map/pallas_call | solution.py:71
  70.1 6.0 all-to-all-start
  88.8 9.8 %collective-permute-done.12.refs_1_ = bf16[2,128,1536]{2,1,0:T(8,128)(2,1)} collective-permute-done((bf16[2,128,1536]{2,1,0:T(8,128)(2,1)}, bf16[2,128,1536]{2,1,0:T(8,128)(2,1)}, u32[]{:S(2)}, u32[]{:S(2)}) %collective-permute-start.12) | collective-permute-done | bytes 786464 | tf_op jit(solution)/shard_map/ppermute | solution.py:407
  110.1 16.6 %shard_map.222 = (bf16[2,128,1536]{2,1,0:T(8,128)(2,1)S(1)}, bf16[2,128,1536]{2,1,0:T(8,128)(2,1)S(1)}, bf16[2,128,1536]{2,1,0:T(8,128)(2,1)S(1)}, bf16[2,128,15...) custom-call(s32[8]{0:T(128)S(1)} %pad_add_fusion.1.s_ref, ...), custom_call_target="tpu_custom_call" | custom-call | flops 10066329600 | bytes 25198624 | tf_op jit(solution)/shard_map/pallas_call | solution.py:71
  135.7 6.0 collective-permute-done.21
  141.7 9.2 %collective-permute-done.23 = bf16[2,128,1536]{2,1,0:T(8,128)(2,1)S(1)} collective-permute-done((bf16[2,128,1536]{2,1,0:T(8,128)(2,1)S(1)}, bf16[2,128,1536]{2,1,0:T(8,128)(2,1)S(1)}, u32[]{:S(2)}, u32[]{:S(2)}) %collective-permute-start.23) | collective-permute-done | bytes 786464 | tf_op jit(solution)/shard_map/ppermute | solution.py:412
  171.3 5.7 collective-permute-done.30
  193.8 11.1 %collective-permute-done.35.kv1 = bf16[2,512,256]{2,1,0:T(8,128)(2,1)S(1)} collective-permute-done((bf16[2,512,256]{2,1,0:T(8,128)(2,1)S(1)}, bf16[2,512,256]{2,1,0:T(8,128)(2,1)S(1)}, u32[]{:S(2)}, u32[]{:S(2)}) %collective-permute-start.35) | collective-permute-done | bytes 524320 | tf_op jit(solution)/shard_map/ppermute | solution.py:407
  208.5 7.7 %shard_map.224 = (bf16[2,128,384]{2,1,0:T(8,128)(2,1)S(1)}, f32[2,8,768]{2,1,0:T(8,128)S(1)}, bf16[2,128,1536]{2,1,0:T(8,128)(2,1)S(1)}) custom-call(s32[17]{0:T(128)S(1)} %pad_add_fusion.row_ref, bf16[384,1536]{1,0:T(8,128)(2,1)S(1)} %copy-done.13, bf16[2,128,384]{2,1,0:T(8,128)(2,1)S(1)} %bitcast.134, bf16[2,512,256]{2,1,0:T(8,128)(2,1)S(1)} %pad_maximum_fusion.9.kv0, ...), custom_call_target="tpu_custom_call" | custom-call | flops 3221225472 | bytes 4505668 | tf_op jit(solution)/shard_map/pallas_call | solution.py:71
  241.4 7.1 collective-permute-done.43.refs_1_
  265.1 16.6 %shard_map.225 = (bf16[2,128,1536]{2,1,0:T(8,128)(2,1)S(1)}, bf16[2,128,1536]{2,1,0:T(8,128)(2,1)S(1)}, bf16[2,128,1536]{2,1,0:T(8,128)(2,1)S(1)}, bf16[2,128,15...) custom-call(s32[8]{0:T(128)S(1)} %pad_add_fusion.1.s_ref, ...), custom_call_target="tpu_custom_call" | custom-call | flops 10066329600 | bytes 25198624 | tf_op jit(solution)/shard_map/pallas_call | solution.py:71
  283.0 15.8 %shard_map.226 = (bf16[2,128,1536]{2,1,0:T(8,128)(2,1)}, bf16[2,128,1536]{2,1,0:T(8,128)(2,1)}, bf16[2,128,1536]{2,1,0:T(8,128)(2,1)}, bf16[2,128,1536]{2,1,0:T(...) custom-call(s32[8]{0:T(128)S(1)} %pad_add_fusion.1.s_ref, ...), custom_call_target="tpu_custom_call" | custom-call | flops 10066329600 | bytes 27164704 | tf_op jit(solution)/shard_map/pallas_call | solution.py:71
  312.3 14.5 %collective-permute-done.52 = bf16[2,128,1536]{2,1,0:T(8,128)(2,1)S(1)} collective-permute-done((bf16[2,128,1536]{2,1,0:T(8,128)(2,1)S(1)}, bf16[2,128,1536]{2,1,0:T(8,128)(2,1)S(1)}, u32[]{:S(2)}, u32[]{:S(2)}) %collective-permute-start.52) | collective-permute-done | bytes 786464 | tf_op jit(solution)/shard_map/ppermute | solution.py:412
  353.4 13.5 %shard_map.227 = (bf16[2,128,384]{2,1,0:T(8,128)(2,1)}, bf16[2,512,256]{2,1,0:T(8,128)(2,1)}, bf16[2,512,256]{2,1,0:T(8,128)(2,1)}, bf16[2,512,256]{2,1,0:T(8,128)(2,1)}, bf16[2,512,256]{2,1,0:T(8,128)(2,1)}) custom-call(s32[17]{0:T(128)} %copy-done.51, bf16[384,1536]{1,0:T(8,128)(2,1)} %copy-done.12, f32[128,128]{1,0:T(8,128)} %copy.68.cos_ref, ...), custom_call_target="tpu_custom_call" | custom-call | flops 8053063680 | bytes 6930500 | tf_op jit(solution)/shard_map/pallas_call | solution.py:71
  376.8 5.6 collective-permute-done.69
  382.4 6.4 collective-permute-done.70
  416.6 5.8 collective-permute-done.81
  436.0 8.9 %collective-permute-done.86.refs_1_ = bf16[2,128,1536]{2,1,0:T(8,128)(2,1)S(1)} collective-permute-done((bf16[2,128,1536]{2,1,0:T(8,128)(2,1)S(1)}, bf16[2,128,1536]{2,1,0:T(8,128)(2,1)S(1)}, u32[]{:S(2)}, u32[]{:S(2)}) %collective-permute-start.86) | collective-permute-done | bytes 786464 | tf_op jit(solution)/shard_map/ppermute | solution.py:407
  447.4 8.4 %collective-permute-done.88.refs_3_ = bf16[2,128,1536]{2,1,0:T(8,128)(2,1)S(1)} collective-permute-done((bf16[2,128,1536]{2,1,0:T(8,128)(2,1)S(1)}, bf16[2,128,1536]{2,1,0:T(8,128)(2,1)S(1)}, u32[]{:S(2)}, u32[]{:S(2)}) %collective-permute-start.88) | collective-permute-done | bytes 786464 | tf_op jit(solution)/shard_map/ppermute | solution.py:407
  455.8 7.5 %collective-permute-start.89 = (bf16[2,128,1536]{2,1,0:T(8,128)(2,1)S(1)}, bf16[2,128,1536]{2,1,0:T(8,128)(2,1)S(1)}, u32[]{:S(2)}, u32[]{:S(2)}) collective-permute-start(bf16[2,128,1536]{2,1,0:T(8,128)(2,1)S(1)} %constant_dynamic-update-slice_fusion.refs_0_), channel_id=1, source_target_pairs={{0,2},{2,0},{4,6},{6,4},{8,10},{10,8},{12,14},{14,12},{16,18},{18,... | collective-permute-start | bytes 2359304 | tf_op jit(solution)/shard_map/ppermute | solution.py:388
  469.5 15.5 %shard_map.229 = (bf16[2,128,1536]{2,1,0:T(8,128)(2,1)}, bf16[2,128,1536]{2,1,0:T(8,128)(2,1)}, bf16[2,128,1536]{2,1,0:T(8,128)(2,1)}, bf16[2,128,1536]{2,1,0:T(...) custom-call(s32[8]{0:T(128)S(1)} %pad_add_fusion.1.s_ref, ...), custom_call_target="tpu_custom_call" | custom-call | flops 10066329600 | bytes 27164704 | tf_op jit(solution)/shard_map/pallas_call | solution.py:71
  497.0 13.7 %collective-permute-done.96 = bf16[2,128,1536]{2,1,0:T(8,128)(2,1)S(1)} collective-permute-done((bf16[2,128,1536]{2,1,0:T(8,128)(2,1)S(1)}, bf16[2,128,1536]{2,1,0:T(8,128)(2,1)S(1)}, u32[]{:S(2)}, u32[]{:S(2)}) %collective-permute-start.96) | collective-permute-done | bytes 786464 | tf_op jit(solution)/shard_map/ppermute | solution.py:412
  516.3 5.5 collective-permute-done.102
  536.3 5.6 all-to-all-start.1
  544.2 13.5 %shard_map.231 = (bf16[2,128,384]{2,1,0:T(8,128)(2,1)}, bf16[2,512,256]{2,1,0:T(8,128)(2,1)}, bf16[2,512,256]{2,1,0:T(8,128)(2,1)}, bf16[2,512,256]{2,1,0:T(8,128)(2,1)}, bf16[2,512,256]{2,1,0:T(8,128)(2,1)}) custom-call(s32[17]{0:T(128)} %copy-done.51, bf16[384,1536]{1,0:T(8,128)(2,1)} %copy-done.12, f32[128,128]{1,0:T(8,128)} %copy.68.cos_ref, ...), custom_call_target="tpu_custom_call" | custom-call | flops 8053063680 | bytes 6930500 | tf_op jit(solution)/shard_map/pallas_call | solution.py:71
  567.8 12.8 %shard_map.232 = (f32[1536,640]{1,0:T(8,128)}, f32[1536,640]{1,0:T(8,128)}, bf16[256,1536]{1,0:T(8,128)(2,1)}, bf16[384,1536]{1,0:T(8,128)(2,1)}) custom-call(s32[8]{0:T(128)} %copy-done.42, bf16[2,512,1536]{2,1,0:T(8,128)(2,1)} %get-tuple-element.195.b_own, bf16[2,256,1536]{2,1,0:T(8,128)(2,1)} %collective-permute-done.75.o0, ...), custom_call_target="tpu_custom_call" | custom-call | flops 5033164800 | bytes 12714016 | tf_op jit(solution)/shard_map/pallas_call | solution.py:71
  584.9 6.8 all-to-all-start.3
  597.9 10.1 %collective-permute-done.110 = bf16[2,128,256]{2,1,0:T(8,128)(2,1)S(1)} collective-permute-done((bf16[2,128,256]{2,1,0:T(8,128)(2,1)S(1)}, bf16[2,128,256]{2,1,0:T(8,128)(2,1)S(1)}, u32[]{:S(2)}, u32[]{:S(2)}) %collective-permute-start.110) | collective-permute-done | bytes 131104 | tf_op jit(solution)/shard_map/ppermute | solution.py:412
  608.0 6.4 collective-permute-done.111
  628.9 11.6 %all-to-all-done.2 = bf16[16,112,256]{2,1,0:T(8,128)(2,1)S(1)} async-done(((bf16[16,112,256]{2,1,0:T(8,128)(2,1)}), bf16[16,112,256]{2,1,0:T(8,128)(2,1)S(1)}, u32[]{:S(2)}, u32[]{:S(2)}) %all-to-all-start.2) | async-done | bytes 917536 | tf_op jit(solution)/shard_map/all_to_all | solution.py:443
  668.7 18.5 %all-to-all-done.4 = bf16[16,103,640]{2,1,0:T(8,128)(2,1)} async-done(((bf16[16,103,640]{2,1,0:T(8,128)(2,1)}), bf16[16,103,640]{2,1,0:T(8,128)(2,1)}, u32[]{:S(2)}, u32[]{:S(2)}) %all-to-all-start.4) | async-done | bytes 2109472 | tf_op jit(solution)/shard_map/all_to_all | solution.py:443
  (675 shorter events, 383.7 us)
Async XLA Ops:
  76.0 491.8 %all-gather.5.cloned.1.call-start = ((), (), s32[]{:S(2)}) async-start(), calls=%async_computation.5 | async-start | bytes 3932160 | tf_op jit(solution)/shard_map/all_gather | solution.py:744
  78.2 20.4 %collective-permute-start.12 = (bf16[2,128,1536]{2,1,0:T(8,128)(2,1)}, bf16[2,128,1536]{2,1,0:T(8,128)(2,1)}, u32[]{:S(2)}, u32[]{:S(2)}) collective-permute-start(bf16[2,128,1536]{2,1,0:T(8,128)(2,1)} %pad_maximum_fusion.3.refs_0_), channel_id=1, source_target_pairs={{0,12},{2,50},{4,0},{6,54},{8,4},{10,58},{12,8},{14,62},{16,28},{1... | collective-permute-start | bytes 2359304 | tf_op jit(solution)/shard_map/ppermute | solution.py:407
  81.4 20.9 %collective-permute-start.14 = (bf16[2,128,1536]{2,1,0:T(8,128)(2,1)}, bf16[2,128,1536]{2,1,0:T(8,128)(2,1)}, u32[]{:S(2)}, u32[]{:S(2)}) collective-permute-start(bf16[2,128,1536]{2,1,0:T(8,128)(2,1)} %pad_maximum_fusion.3.refs_0_), channel_id=1, source_target_pairs={{0,4},{2,18},{4,8},{6,22},{8,12},{10,26},{12,0},{14,30},{16,20},{1... | collective-permute-start | bytes 2359304 | tf_op jit(solution)/shard_map/ppermute | solution.py:407
  131.7 19.1 %collective-permute-start.23 = (bf16[2,128,1536]{2,1,0:T(8,128)(2,1)S(1)}, bf16[2,128,1536]{2,1,0:T(8,128)(2,1)S(1)}, u32[]{:S(2)}, u32[]{:S(2)}) collective-permute-start(bf16[2,128,1536]{2,1,0:T(8,128)(2,1)S(1)} %add_convert_fusion.17), channel_id=1, source_target_pairs={{0,8},{2,34},{4,12},{6,38},{8,0},{10,42},{12,4},{14,46},{16,24},{1... | collective-permute-start | bytes 2359304 | tf_op jit(solution)/shard_map/ppermute | solution.py:412
  134.8 18.0 %collective-permute-start.25 = (bf16[2,128,1536]{2,1,0:T(8,128)(2,1)S(1)}, bf16[2,128,1536]{2,1,0:T(8,128)(2,1)S(1)}, u32[]{:S(2)}, u32[]{:S(2)}) collective-permute-start(bf16[2,128,1536]{2,1,0:T(8,128)(2,1)S(1)} %add_convert_fusion.16), channel_id=1, source_target_pairs={{0,12},{2,50},{4,0},{6,54},{8,4},{10,58},{12,8},{14,62},{16,28},{1... | collective-permute-start | bytes 2359304 | tf_op jit(solution)/shard_map/ppermute | solution.py:412
  237.9 20.8 %collective-permute-start.45 = (bf16[2,128,1536]{2,1,0:T(8,128)(2,1)S(1)}, bf16[2,128,1536]{2,1,0:T(8,128)(2,1)S(1)}, u32[]{:S(2)}, u32[]{:S(2)}) collective-permute-start(bf16[2,128,1536]{2,1,0:T(8,128)(2,1)S(1)} %pad_maximum_fusion.5.refs_0_), channel_id=1, source_target_pairs={{0,4},{2,18},{4,8},{6,22},{8,12},{10,26},{12,0},{14,30},{16,20},{1... | collective-permute-start | bytes 2359304 | tf_op jit(solution)/shard_map/ppermute | solution.py:407
  238.8 23.5 %collective-permute-start.46 = (bf16[2,128,1536]{2,1,0:T(8,128)(2,1)S(1)}, bf16[2,128,1536]{2,1,0:T(8,128)(2,1)S(1)}, u32[]{:S(2)}, u32[]{:S(2)}) collective-permute-start(bf16[2,128,1536]{2,1,0:T(8,128)(2,1)S(1)} %pad_maximum_fusion.5.refs_0_), channel_id=1, source_target_pairs={{0,2},{2,0},{4,6},{6,4},{8,10},{10,8},{12,14},{14,12},{16,18},{18,... | collective-permute-start | bytes 2359304 | tf_op jit(solution)/shard_map/ppermute | solution.py:388
  306.0 20.8 %collective-permute-start.52 = (bf16[2,128,1536]{2,1,0:T(8,128)(2,1)S(1)}, bf16[2,128,1536]{2,1,0:T(8,128)(2,1)S(1)}, u32[]{:S(2)}, u32[]{:S(2)}) collective-permute-start(bf16[2,128,1536]{2,1,0:T(8,128)(2,1)S(1)} %add_convert_fusion.13), channel_id=1, source_target_pairs={{0,4},{2,18},{4,8},{6,22},{8,12},{10,26},{12,0},{14,30},{16,20},{1... | collective-permute-start | bytes 2359304 | tf_op jit(solution)/shard_map/ppermute | solution.py:412
  307.1 19.7 %collective-permute-start.54 = (bf16[2,128,1536]{2,1,0:T(8,128)(2,1)S(1)}, bf16[2,128,1536]{2,1,0:T(8,128)(2,1)S(1)}, u32[]{:S(2)}, u32[]{:S(2)}) collective-permute-start(bf16[2,128,1536]{2,1,0:T(8,128)(2,1)S(1)} %add_convert_fusion.12), channel_id=1, source_target_pairs={{0,8},{2,34},{4,12},{6,38},{8,0},{10,42},{12,4},{14,46},{16,24},{1... | collective-permute-start | bytes 2359304 | tf_op jit(solution)/shard_map/ppermute | solution.py:412
  308.2 19.7 %collective-permute-start.56 = (bf16[2,128,1536]{2,1,0:T(8,128)(2,1)S(1)}, bf16[2,128,1536]{2,1,0:T(8,128)(2,1)S(1)}, u32[]{:S(2)}, u32[]{:S(2)}) collective-permute-start(bf16[2,128,1536]{2,1,0:T(8,128)(2,1)S(1)} %add_convert_fusion.11), channel_id=1, source_target_pairs={{0,12},{2,50},{4,0},{6,54},{8,4},{10,58},{12,8},{14,62},{16,28},{1... | collective-permute-start | bytes 2359304 | tf_op jit(solution)/shard_map/ppermute | solution.py:412
  310.5 20.6 %collective-permute-start.60 = (bf16[2,128,1536]{2,1,0:T(8,128)(2,1)S(1)}, bf16[2,128,1536]{2,1,0:T(8,128)(2,1)S(1)}, u32[]{:S(2)}, u32[]{:S(2)}) collective-permute-start(bf16[2,128,1536]{2,1,0:T(8,128)(2,1)S(1)} %get-tuple-element.187), channel_id=1, source_target_pairs={{0,2},{2,0},{4,6},{6,4},{8,10},{10,8},{12,14},{14,12},{16,18},{18,... | collective-permute-start | bytes 2359304 | tf_op jit(solution)/shard_map/ppermute | solution.py:388
  347.9 19.0 %collective-permute-start.66 = (bf16[2,128,1536]{2,1,0:T(8,128)(2,1)}, bf16[2,128,1536]{2,1,0:T(8,128)(2,1)}, u32[]{:S(2)}, u32[]{:S(2)}) collective-permute-start(bf16[2,128,1536]{2,1,0:T(8,128)(2,1)} %add_convert_fusion.8), channel_id=1, source_target_pairs={{0,4},{2,18},{4,8},{6,22},{8,12},{10,26},{12,0},{14,30},{16,20},{1... | collective-permute-start | bytes 2359304 | tf_op jit(solution)/shard_map/ppermute | solution.py:412
  347.9 21.7 %collective-permute-start.67 = (bf16[2,128,1536]{2,1,0:T(8,128)(2,1)}, bf16[2,128,1536]{2,1,0:T(8,128)(2,1)}, u32[]{:S(2)}, u32[]{:S(2)}) collective-permute-start(bf16[2,128,1536]{2,1,0:T(8,128)(2,1)} %add_convert_fusion.7), channel_id=1, source_target_pairs={{0,8},{2,34},{4,12},{6,38},{8,0},{10,42},{12,4},{14,46},{16,24},{1... | collective-permute-start | bytes 2359304 | tf_op jit(solution)/shard_map/ppermute | solution.py:412
  351.2 18.4 %collective-permute-start.68 = (bf16[2,128,1536]{2,1,0:T(8,128)(2,1)}, bf16[2,128,1536]{2,1,0:T(8,128)(2,1)}, u32[]{:S(2)}, u32[]{:S(2)}) collective-permute-start(bf16[2,128,1536]{2,1,0:T(8,128)(2,1)} %add_convert_fusion.6), channel_id=1, source_target_pairs={{0,12},{2,50},{4,0},{6,54},{8,4},{10,58},{12,8},{14,62},{16,28},{1... | collective-permute-start | bytes 2359304 | tf_op jit(solution)/shard_map/ppermute | solution.py:412
  352.3 45.3 %collective-permute-start.75 = (bf16[2,256,1536]{2,1,0:T(8,128)(2,1)}, bf16[2,256,1536]{2,1,0:T(8,128)(2,1)}, u32[]{:S(2)}, u32[]{:S(2)}) collective-permute-start(bf16[2,256,1536]{2,1,0:T(8,128)(2,1)} %slice.151), channel_id=1, source_target_pairs={{0,1},{1,0},{2,3},{3,2},{4,5},{5,4},{6,7},{7,6},{8,9},{9,8},{10,11... | collective-permute-start | bytes 4718600 | tf_op jit(solution)/shard_map/ppermute | solution.py:392
  435.1 20.7 %collective-permute-start.88 = (bf16[2,128,1536]{2,1,0:T(8,128)(2,1)S(1)}, bf16[2,128,1536]{2,1,0:T(8,128)(2,1)S(1)}, u32[]{:S(2)}, u32[]{:S(2)}) collective-permute-start(bf16[2,128,1536]{2,1,0:T(8,128)(2,1)S(1)} %constant_dynamic-update-slice_fusion.refs_0_), channel_id=1, source_target_pairs={{0,4},{2,18},{4,8},{6,22},{8,12},{10,26},{12,0},{14,30},{16,20},{1... | collective-permute-start | bytes 2359304 | tf_op jit(solution)/shard_map/ppermute | solution.py:407
  463.9 21.1 %collective-permute-start.93 = (bf16[2,128,1536]{2,1,0:T(8,128)(2,1)S(1)}, bf16[2,128,1536]{2,1,0:T(8,128)(2,1)S(1)}, u32[]{:S(2)}, u32[]{:S(2)}) collective-permute-start(bf16[2,128,1536]{2,1,0:T(8,128)(2,1)S(1)} %get-tuple-element.236), channel_id=1, source_target_pairs={{0,1},{1,0},{2,3},{3,2},{4,5},{5,4},{6,7},{7,6},{8,9},{9,8},{10,11... | collective-permute-start | bytes 2359304 | tf_op jit(solution)/shard_map/ppermute | solution.py:392
  489.9 20.8 %collective-permute-start.96 = (bf16[2,128,1536]{2,1,0:T(8,128)(2,1)S(1)}, bf16[2,128,1536]{2,1,0:T(8,128)(2,1)S(1)}, u32[]{:S(2)}, u32[]{:S(2)}) collective-permute-start(bf16[2,128,1536]{2,1,0:T(8,128)(2,1)S(1)} %add_convert_fusion.3), channel_id=1, source_target_pairs={{0,4},{2,18},{4,8},{6,22},{8,12},{10,26},{12,0},{14,30},{16,20},{1... | collective-permute-start | bytes 2359304 | tf_op jit(solution)/shard_map/ppermute | solution.py:412
  491.5 19.2 %collective-permute-start.98 = (bf16[2,128,1536]{2,1,0:T(8,128)(2,1)S(1)}, bf16[2,128,1536]{2,1,0:T(8,128)(2,1)S(1)}, u32[]{:S(2)}, u32[]{:S(2)}) collective-permute-start(bf16[2,128,1536]{2,1,0:T(8,128)(2,1)S(1)} %add_convert_fusion.2), channel_id=1, source_target_pairs={{0,8},{2,34},{4,12},{6,38},{8,0},{10,42},{12,4},{14,46},{16,24},{1... | collective-permute-start | bytes 2359304 | tf_op jit(solution)/shard_map/ppermute | solution.py:412
  493.2 19.8 %collective-permute-start.100 = (bf16[2,128,1536]{2,1,0:T(8,128)(2,1)S(1)}, bf16[2,128,1536]{2,1,0:T(8,128)(2,1)S(1)}, u32[]{:S(2)}, u32[]{:S(2)}) collective-permute-start(bf16[2,128,1536]{2,1,0:T(8,128)(2,1)S(1)} %add_convert_fusion.1), channel_id=1, source_target_pairs={{0,12},{2,50},{4,0},{6,54},{8,4},{10,58},{12,8},{14,62},{16,28},{1... | collective-permute-start | bytes 2359304 | tf_op jit(solution)/shard_map/ppermute | solution.py:412
  494.6 18.9 %collective-permute-start.101 = (bf16[2,128,1536]{2,1,0:T(8,128)(2,1)S(1)}, bf16[2,128,1536]{2,1,0:T(8,128)(2,1)S(1)}, u32[]{:S(2)}, u32[]{:S(2)}) collective-permute-start(bf16[2,128,1536]{2,1,0:T(8,128)(2,1)S(1)} %get-tuple-element.254), channel_id=1, source_target_pairs={{0,1},{1,0},{2,3},{3,2},{4,5},{5,4},{6,7},{7,6},{8,9},{9,8},{10,11... | collective-permute-start | bytes 2359304 | tf_op jit(solution)/shard_map/ppermute | solution.py:392
  536.3 22.7 %all-to-all-start.1 = ((bf16[16,24,1536]{2,1,0:T(8,128)(2,1)}), bf16[16,24,1536]{2,1,0:T(8,128)(2,1)}, u32[]{:S(2)}, u32[]{:S(2)}) async-start(bf16[16,24,1536]{2,1,0:T(8,128)(2,1)} %bitcast.146), calls=%async_computation.1 | async-start | bytes 2359296 | tf_op jit(solution)/shard_map/all_to_all | solution.py:443
  541.9 101.1 %all-gather.7.cloned.1.call-start = ((), (), s32[]{:S(2)}) async-start(), calls=%async_computation.6 | async-start | bytes 2433024 | tf_op jit(solution)/shard_map/all_gather | solution.py:769
  561.1 19.6 %collective-permute-start.107 = (bf16[2,512,256]{2,1,0:T(8,128)(2,1)}, bf16[2,512,256]{2,1,0:T(8,128)(2,1)}, u32[]{:S(2)}, u32[]{:S(2)}) collective-permute-start(bf16[2,512,256]{2,1,0:T(8,128)(2,1)} %get-tuple-element.258), channel_id=1, source_target_pairs={{0,4},{2,18},{4,8},{6,22},{8,12},{10,26},{12,0},{14,30},{16,20},{1... | collective-permute-start | bytes 1572872 | tf_op jit(solution)/shard_map/ppermute | solution.py:412
  561.2 19.5 %collective-permute-start.108 = (bf16[2,512,256]{2,1,0:T(8,128)(2,1)}, bf16[2,512,256]{2,1,0:T(8,128)(2,1)}, u32[]{:S(2)}, u32[]{:S(2)}) collective-permute-start(bf16[2,512,256]{2,1,0:T(8,128)(2,1)} %get-tuple-element.259), channel_id=1, source_target_pairs={{0,8},{2,34},{4,12},{6,38},{8,0},{10,42},{12,4},{14,46},{16,24},{1... | collective-permute-start | bytes 1572872 | tf_op jit(solution)/shard_map/ppermute | solution.py:412
  580.6 33.8 %collective-permute-start.113 = (bf16[256,1536]{1,0:T(8,128)(2,1)}, bf16[256,1536]{1,0:T(8,128)(2,1)}, u32[]{:S(2)}, u32[]{:S(2)}) collective-permute-start(bf16[256,1536]{1,0:T(8,128)(2,1)} %get-tuple-element.273), channel_id=1, source_target_pairs={{0,1},{1,0},{2,3},{3,2},{4,5},{5,4},{6,7},{7,6},{8,9},{9,8},{10,11... | collective-permute-start | bytes 2359304 | tf_op jit(solution)/shard_map/ppermute | solution.py:392
  584.9 35.5 %all-to-all-start.3 = ((bf16[16,96,384]{2,1,0:T(8,128)(2,1)}), bf16[16,96,384]{2,1,0:T(8,128)(2,1)}, u32[]{:S(2)}, u32[]{:S(2)}) async-start(bf16[16,96,384]{2,1,0:T(8,128)(2,1)} %bitcast.141), calls=%async_computation.3 | async-start | bytes 2359296 | tf_op jit(solution)/shard_map/all_to_all | solution.py:443
  594.3 20.1 %collective-permute-start.111 = (bf16[2,128,256]{2,1,0:T(8,128)(2,1)S(1)}, bf16[2,128,256]{2,1,0:T(8,128)(2,1)S(1)}, u32[]{:S(2)}, u32[]{:S(2)}) collective-permute-start(bf16[2,128,256]{2,1,0:T(8,128)(2,1)S(1)} %get-tuple-element.339), channel_id=1, source_target_pairs={{0,32},{2,10},{4,36},{6,14},{8,40},{10,2},{12,44},{14,6},{16,48},{... | collective-permute-start | bytes 393224 | tf_op jit(solution)/shard_map/ppermute | solution.py:412
  596.7 17.7 %collective-permute-start.112 = (bf16[2,128,256]{2,1,0:T(8,128)(2,1)S(1)}, bf16[2,128,256]{2,1,0:T(8,128)(2,1)S(1)}, u32[]{:S(2)}, u32[]{:S(2)}) collective-permute-start(bf16[2,128,256]{2,1,0:T(8,128)(2,1)S(1)} %get-tuple-element.338), channel_id=1, source_target_pairs={{0,48},{2,14},{4,52},{6,2},{8,56},{10,6},{12,60},{14,10},{16,0},{1... | collective-permute-start | bytes 393224 | tf_op jit(solution)/shard_map/ppermute | solution.py:412
  614.4 28.5 %collective-permute-start.114 = (bf16[384,1536]{1,0:T(8,128)(2,1)}, bf16[384,1536]{1,0:T(8,128)(2,1)}, u32[]{:S(2)}, u32[]{:S(2)}) collective-permute-start(bf16[384,1536]{1,0:T(8,128)(2,1)} %get-tuple-element.284), channel_id=1, source_target_pairs={{0,1},{1,0},{2,3},{3,2},{4,5},{5,4},{6,7},{7,6},{8,9},{9,8},{10,11... | collective-permute-start | bytes 3538952 | tf_op jit(solution)/shard_map/ppermute | solution.py:392
  620.4 20.1 %all-to-all-start.2 = ((bf16[16,112,256]{2,1,0:T(8,128)(2,1)}), bf16[16,112,256]{2,1,0:T(8,128)(2,1)S(1)}, u32[]{:S(2)}, u32[]{:S(2)}) async-start(bf16[16,112,256]{2,1,0:T(8,128)(2,1)} %pad_maximum_fusion.1), calls=%async_computation.2 | async-start | bytes 1835008 | tf_op jit(solution)/shard_map/all_to_all | solution.py:443
  652.8 34.3 %all-to-all-start.4 = ((bf16[16,103,640]{2,1,0:T(8,128)(2,1)}), bf16[16,103,640]{2,1,0:T(8,128)(2,1)}, u32[]{:S(2)}, u32[]{:S(2)}) async-start(bf16[16,103,640]{2,1,0:T(8,128)(2,1)} %broadcast_in_dim.42), calls=%async_computation.4 | async-start | bytes 4259840 | tf_op jit(solution)/shard_map/all_to_all | solution.py:443
  (225 other events, 3363.7 us)
Sparse Core Ops, SparseCore 0:
  524.7 43.0 all-gather.4
  570.1 51.0 all-gather.6

commit v4 on v2

--- a/solution.py
+++ b/solution.py
@@ -769,12 +769,11 @@
     all_out = lax.all_gather(out_w_grad, "ep")
     q_grad = tn(a, dq.reshape(both_rows, -1)).astype(bf16)
     q_grad = exchange(q_grad.reshape(CHIPS, -1, 3 * LANES))
-    arrived, (gate_grad, up_grad, near, far, q_grad) = to_owners(
-        dkv, (gate_grad, up_grad, near, far, q_grad)
-    )
+    near_down = other_half(near)
+    arrived, (gate_grad, up_grad, q_grad) = to_owners(dkv, (gate_grad, up_grad, q_grad))
+    *arrived, near_down = pin(*arrived, near_down)
     q_grad = jnp.sum(q_grad.astype(f32), axis=0).astype(bf16)
     dqkv, y, gain_one_grad = after_keys(arrived, dq, x128)
-    near_down = other_half(near)
 
     kv_width = 2 * LANES
     small = jnp.concatenate([router_grad[:experts], gain_one_grad, gain_two_grad[None]], axis=0)
@@ -784,7 +783,7 @@
     small = small.reshape(CHIPS, small_lines, kv_width).astype(bf16)
     wide = tn(a, dqkv[:, 3 * LANES :]).astype(bf16).reshape(CHIPS, -1, kv_width)
     lines = wide.shape[1]
-    wide, near_down, all_out = pin(jnp.concatenate([wide, small], axis=1), near_down, all_out)
+    wide, all_out = pin(jnp.concatenate([wide, small], axis=1), all_out)
     all_q = lax.all_gather(pin(q_grad, all_out)[0], "ep")
     far_down = other_half(pin(far, near_down)[0])
     wide, y, far_down = pin(exchange(wide), y, far_down)

time: 714 us -> 715 us (level)
  transfers between devices with their start and end apart: 128 -> 128, of which waited for: 80 -> 79; matrix products, arithmetic and copies ran while one was open for 11% -> 11% of each run, Pallas kernels for 11% -> 11%
where the time goes in v4:
time: 715 us; the launch traced here: 705 us
  waiting for transfers between devices  283 us (40%)
  starting transfers between devices  169 us (24%)
  Pallas kernels  130 us (18%)
  other arithmetic  60 us (8%)
  local copies, waits for them, and re-layouts  40.8 us (6%)
  between operations  16.4 us (2%)
    pallas_call x10, Pallas kernels, local_call(): pl.pallas_call(kernel, grid=(micros,), out_shape=[jax.ShapeDtypeStruct((m...  123 us
    ppermute x36, waiting for transfers between devices, to_ring(): lax.ppermute(pieces[d], 'ep', ring(stage, d))  97.2 us
    ppermute x30, waiting for transfers between devices, from_ring(): lax.ppermute(value, 'ep', ring(stage, -d))  96.5 us
    ppermute x38, starting transfers between devices, other_core(): return lax.ppermute(value, 'ep', [(i, i ^ 1) for i in range(2 * CHIPS)])  45.1 us
    ppermute x36, starting transfers between devices, to_ring(): lax.ppermute(pieces[d], 'ep', ring(stage, d))  42 us
    ppermute x13, waiting for transfers between devices, other_half(): return lax.ppermute(value, 'tp', [(0, 1), (1, 0)])  35.3 us
    ppermute x30, starting transfers between devices, from_ring(): lax.ppermute(value, 'ep', ring(stage, -d))  32 us
    all_to_all x5, starting transfers between devices, exchange(): lax.all_to_all(pieces, 'ep', 0, 0, tiled=True, axis_index_groups=groups)  26.5 us
  transfers between devices with their start and end apart: 128, of which 79 were waited for; matrix products, arithmetic and copies ran while one was open for 11% of the time, Pallas kernels for 11%

profile of v4, /device:TPU:1, one launch (start us, length us, event | category | flops | bytes accessed | tf_op | source)
XLA Modules:
  0.0 704.9 jit_solution(11246887785071410739)
XLA Ops:
  33.5 7.7 %collective-permute-done.4.kv1 = bf16[2,512,256]{2,1,0:T(8,128)(2,1)} collective-permute-done((bf16[2,512,256]{2,1,0:T(8,128)(2,1)S(1)}, bf16[2,512,256]{2,1,0:T(8,128)(2,1)}, u32[]{:S(2)}, u32[]{:S(2)}) %collective-permute-start.4) | collective-permute-done | bytes 524320 | tf_op jit(solution)/shard_map/ppermute | solution.py:407
  46.9 8.5 %shard_map.221 = (bf16[2,128,384]{2,1,0:T(8,128)(2,1)}, f32[2,8,768]{2,1,0:T(8,128)}, bf16[2,128,1536]{2,1,0:T(8,128)(2,1)S(1)}) custom-call(s32[17]{0:T(128)S(1)} %pad_add_fusion.row_ref, bf16[384,1536]{1,0:T(8,128)(2,1)S(1)} %dynamic-slice_bitcast_fusion.1.wo_ref, bf16[2,128,384]{2,1,0:T(8,128)(2,1)S(1)} %bitcast.134, bf16[2,512,256]{2,1,0:T(8,128)(2,1)S(1)} %copy-done.33, ...), custom_call_target="tpu_custom_call" | custom-call | flops 3221225472 | bytes 4505668 | tf_op jit(solution)/shard_map/pallas_call | solution.py:71
  70.1 6.0 all-to-all-start
  88.8 9.8 %collective-permute-done.12.refs_1_ = bf16[2,128,1536]{2,1,0:T(8,128)(2,1)} collective-permute-done((bf16[2,128,1536]{2,1,0:T(8,128)(2,1)}, bf16[2,128,1536]{2,1,0:T(8,128)(2,1)}, u32[]{:S(2)}, u32[]{:S(2)}) %collective-permute-start.12) | collective-permute-done | bytes 786464 | tf_op jit(solution)/shard_map/ppermute | solution.py:407
  110.1 16.8 %shard_map.222 = (bf16[2,128,1536]{2,1,0:T(8,128)(2,1)S(1)}, bf16[2,128,1536]{2,1,0:T(8,128)(2,1)S(1)}, bf16[2,128,1536]{2,1,0:T(8,128)(2,1)S(1)}, bf16[2,128,15...) custom-call(s32[8]{0:T(128)S(1)} %pad_add_fusion.1.s_ref, ...), custom_call_target="tpu_custom_call" | custom-call | flops 10066329600 | bytes 25198624 | tf_op jit(solution)/shard_map/pallas_call | solution.py:71
  135.9 6.0 collective-permute-done.21
  141.9 9.2 %collective-permute-done.23 = bf16[2,128,1536]{2,1,0:T(8,128)(2,1)S(1)} collective-permute-done((bf16[2,128,1536]{2,1,0:T(8,128)(2,1)S(1)}, bf16[2,128,1536]{2,1,0:T(8,128)(2,1)S(1)}, u32[]{:S(2)}, u32[]{:S(2)}) %collective-permute-start.23) | collective-permute-done | bytes 786464 | tf_op jit(solution)/shard_map/ppermute | solution.py:412
  156.5 5.2 collective-permute-done.26
  170.5 5.7 collective-permute-done.30
  193.0 11.1 %collective-permute-done.35.kv1 = bf16[2,512,256]{2,1,0:T(8,128)(2,1)S(1)} collective-permute-done((bf16[2,512,256]{2,1,0:T(8,128)(2,1)S(1)}, bf16[2,512,256]{2,1,0:T(8,128)(2,1)S(1)}, u32[]{:S(2)}, u32[]{:S(2)}) %collective-permute-start.35) | collective-permute-done | bytes 524320 | tf_op jit(solution)/shard_map/ppermute | solution.py:407
  207.8 7.7 %shard_map.224 = (bf16[2,128,384]{2,1,0:T(8,128)(2,1)S(1)}, f32[2,8,768]{2,1,0:T(8,128)S(1)}, bf16[2,128,1536]{2,1,0:T(8,128)(2,1)S(1)}) custom-call(s32[17]{0:T(128)S(1)} %pad_add_fusion.row_ref, bf16[384,1536]{1,0:T(8,128)(2,1)S(1)} %copy-done.12, bf16[2,128,384]{2,1,0:T(8,128)(2,1)S(1)} %bitcast.131, bf16[2,512,256]{2,1,0:T(8,128)(2,1)S(1)} %pad_maximum_fusion.9.kv0, ...), custom_call_target="tpu_custom_call" | custom-call | flops 3221225472 | bytes 4505668 | tf_op jit(solution)/shard_map/pallas_call | solution.py:71
  240.6 7.1 %collective-permute-done.43.refs_1_ = bf16[2,128,1536]{2,1,0:T(8,128)(2,1)S(1)} collective-permute-done((bf16[2,128,1536]{2,1,0:T(8,128)(2,1)S(1)}, bf16[2,128,1536]{2,1,0:T(8,128)(2,1)S(1)}, u32[]{:S(2)}, u32[]{:S(2)}) %collective-permute-start.43) | collective-permute-done | bytes 786464 | tf_op jit(solution)/shard_map/ppermute | solution.py:407
  264.4 16.7 %shard_map.225 = (bf16[2,128,1536]{2,1,0:T(8,128)(2,1)S(1)}, bf16[2,128,1536]{2,1,0:T(8,128)(2,1)S(1)}, bf16[2,128,1536]{2,1,0:T(8,128)(2,1)S(1)}, bf16[2,128,15...) custom-call(s32[8]{0:T(128)S(1)} %pad_add_fusion.1.s_ref, ...), custom_call_target="tpu_custom_call" | custom-call | flops 10066329600 | bytes 25198624 | tf_op jit(solution)/shard_map/pallas_call | solution.py:71
  283.2 16.2 %shard_map.226 = (bf16[2,128,1536]{2,1,0:T(8,128)(2,1)}, bf16[2,128,1536]{2,1,0:T(8,128)(2,1)}, bf16[2,128,1536]{2,1,0:T(8,128)(2,1)}, bf16[2,128,1536]{2,1,0:T(...) custom-call(s32[8]{0:T(128)S(1)} %pad_add_fusion.1.s_ref, ...), custom_call_target="tpu_custom_call" | custom-call | flops 10066329600 | bytes 27164704 | tf_op jit(solution)/shard_map/pallas_call | solution.py:71
  310.7 14.4 %collective-permute-done.52 = bf16[2,128,1536]{2,1,0:T(8,128)(2,1)S(1)} collective-permute-done((bf16[2,128,1536]{2,1,0:T(8,128)(2,1)S(1)}, bf16[2,128,1536]{2,1,0:T(8,128)(2,1)S(1)}, u32[]{:S(2)}, u32[]{:S(2)}) %collective-permute-start.52) | collective-permute-done | bytes 786464 | tf_op jit(solution)/shard_map/ppermute | solution.py:412
  352.0 13.6 %shard_map.227 = (bf16[2,128,384]{2,1,0:T(8,128)(2,1)}, bf16[2,512,256]{2,1,0:T(8,128)(2,1)}, bf16[2,512,256]{2,1,0:T(8,128)(2,1)}, bf16[2,512,256]{2,1,0:T(8,128)(2,1)}, bf16[2,512,256]{2,1,0:T(8,128)(2,1)}) custom-call(s32[17]{0:T(128)} %copy-done.61, bf16[384,1536]{1,0:T(8,128)(2,1)} %copy-done.11, f32[128,128]{1,0:T(8,128)} %copy.68.cos_ref, ...), custom_call_target="tpu_custom_call" | custom-call | flops 8053063680 | bytes 6930500 | tf_op jit(solution)/shard_map/pallas_call | solution.py:71
  374.9 5.8 collective-permute-done.69
  380.8 6.2 collective-permute-done.70
  417.1 5.5 collective-permute-done.81
  437.4 8.8 %collective-permute-done.86.refs_1_ = bf16[2,128,1536]{2,1,0:T(8,128)(2,1)S(1)} collective-permute-done((bf16[2,128,1536]{2,1,0:T(8,128)(2,1)S(1)}, bf16[2,128,1536]{2,1,0:T(8,128)(2,1)S(1)}, u32[]{:S(2)}, u32[]{:S(2)}) %collective-permute-start.86) | collective-permute-done | bytes 786464 | tf_op jit(solution)/shard_map/ppermute | solution.py:407
  448.2 8.4 %collective-permute-done.88.refs_3_ = bf16[2,128,1536]{2,1,0:T(8,128)(2,1)S(1)} collective-permute-done((bf16[2,128,1536]{2,1,0:T(8,128)(2,1)S(1)}, bf16[2,128,1536]{2,1,0:T(8,128)(2,1)S(1)}, u32[]{:S(2)}, u32[]{:S(2)}) %collective-permute-start.88) | collective-permute-done | bytes 786464 | tf_op jit(solution)/shard_map/ppermute | solution.py:407
  456.6 6.5 collective-permute-start.89
  469.4 15.9 %shard_map.229 = (bf16[2,128,1536]{2,1,0:T(8,128)(2,1)}, bf16[2,128,1536]{2,1,0:T(8,128)(2,1)}, bf16[2,128,1536]{2,1,0:T(8,128)(2,1)}, bf16[2,128,1536]{2,1,0:T(...) custom-call(s32[8]{0:T(128)S(1)} %pad_add_fusion.1.s_ref, ...), custom_call_target="tpu_custom_call" | custom-call | flops 10066329600 | bytes 27164704 | tf_op jit(solution)/shard_map/pallas_call | solution.py:71
  496.5 13.7 %collective-permute-done.96 = bf16[2,128,1536]{2,1,0:T(8,128)(2,1)S(1)} collective-permute-done((bf16[2,128,1536]{2,1,0:T(8,128)(2,1)S(1)}, bf16[2,128,1536]{2,1,0:T(8,128)(2,1)S(1)}, u32[]{:S(2)}, u32[]{:S(2)}) %collective-permute-start.96) | collective-permute-done | bytes 786464 | tf_op jit(solution)/shard_map/ppermute | solution.py:412
  515.9 5.5 collective-permute-done.102
  535.8 5.7 all-to-all-start.1
  543.8 13.5 %shard_map.231 = (bf16[2,128,384]{2,1,0:T(8,128)(2,1)}, bf16[2,512,256]{2,1,0:T(8,128)(2,1)}, bf16[2,512,256]{2,1,0:T(8,128)(2,1)}, bf16[2,512,256]{2,1,0:T(8,128)(2,1)}, bf16[2,512,256]{2,1,0:T(8,128)(2,1)}) custom-call(s32[17]{0:T(128)} %copy-done.61, bf16[384,1536]{1,0:T(8,128)(2,1)} %copy-done.11, f32[128,128]{1,0:T(8,128)} %copy.68.cos_ref, ...), custom_call_target="tpu_custom_call" | custom-call | flops 8053063680 | bytes 6930500 | tf_op jit(solution)/shard_map/pallas_call | solution.py:71
  563.5 5.3 all-to-all-start.2
  573.8 13.3 %shard_map.232 = (f32[1536,640]{1,0:T(8,128)}, f32[1536,640]{1,0:T(8,128)}, bf16[256,1536]{1,0:T(8,128)(2,1)}, bf16[384,1536]{1,0:T(8,128)(2,1)}) custom-call(s32[8]{0:T(128)} %copy-done.54, bf16[2,512,1536]{2,1,0:T(8,128)(2,1)} %get-tuple-element.196.b_own, bf16[2,256,1536]{2,1,0:T(8,128)(2,1)} %collective-permute-done.75.o0, ...), custom_call_target="tpu_custom_call" | custom-call | flops 5033164800 | bytes 12714016 | tf_op jit(solution)/shard_map/pallas_call | solution.py:71
  592.0 6.3 collective-permute-done.108
  639.1 14.5 %collective-permute-done.114 = bf16[384,1536]{1,0:T(8,128)(2,1)} collective-permute-done((bf16[384,1536]{1,0:T(8,128)(2,1)}, bf16[384,1536]{1,0:T(8,128)(2,1)}, u32[]{:S(2)}, u32[]{:S(2)}) %collective-permute-start.114) | collective-permute-done | bytes 1179680 | tf_op jit(solution)/shard_map/ppermute | solution.py:392
  671.1 10.9 %all-to-all-done.4 = bf16[16,112,256]{2,1,0:T(8,128)(2,1)} async-done(((bf16[16,112,256]{2,1,0:T(8,128)(2,1)}), bf16[16,112,256]{2,1,0:T(8,128)(2,1)}, u32[]{:S(2)}, u32[]{:S(2)}) %all-to-all-start.4) | async-done | bytes 917536 | tf_op jit(solution)/shard_map/all_to_all | solution.py:443
  (713 shorter events, 381.0 us)
Async XLA Ops:
  76.1 497.8 %all-gather.7.cloned.1.call-start = ((), (), s32[]{:S(2)}) async-start(), calls=%async_computation.5 | async-start | bytes 3932160 | tf_op jit(solution)/shard_map/all_gather | solution.py:744
  78.2 20.4 %collective-permute-start.12 = (bf16[2,128,1536]{2,1,0:T(8,128)(2,1)}, bf16[2,128,1536]{2,1,0:T(8,128)(2,1)}, u32[]{:S(2)}, u32[]{:S(2)}) collective-permute-start(bf16[2,128,1536]{2,1,0:T(8,128)(2,1)} %pad_maximum_fusion.3.refs_0_), channel_id=1, source_target_pairs={{0,12},{2,50},{4,0},{6,54},{8,4},{10,58},{12,8},{14,62},{16,28},{1... | collective-permute-start | bytes 2359304 | tf_op jit(solution)/shard_map/ppermute | solution.py:407
  81.4 20.9 %collective-permute-start.14 = (bf16[2,128,1536]{2,1,0:T(8,128)(2,1)}, bf16[2,128,1536]{2,1,0:T(8,128)(2,1)}, u32[]{:S(2)}, u32[]{:S(2)}) collective-permute-start(bf16[2,128,1536]{2,1,0:T(8,128)(2,1)} %pad_maximum_fusion.3.refs_0_), channel_id=1, source_target_pairs={{0,4},{2,18},{4,8},{6,22},{8,12},{10,26},{12,0},{14,30},{16,20},{1... | collective-permute-start | bytes 2359304 | tf_op jit(solution)/shard_map/ppermute | solution.py:407
  131.9 19.1 %collective-permute-start.23 = (bf16[2,128,1536]{2,1,0:T(8,128)(2,1)S(1)}, bf16[2,128,1536]{2,1,0:T(8,128)(2,1)S(1)}, u32[]{:S(2)}, u32[]{:S(2)}) collective-permute-start(bf16[2,128,1536]{2,1,0:T(8,128)(2,1)S(1)} %add_convert_fusion.17), channel_id=1, source_target_pairs={{0,8},{2,34},{4,12},{6,38},{8,0},{10,42},{12,4},{14,46},{16,24},{1... | collective-permute-start | bytes 2359304 | tf_op jit(solution)/shard_map/ppermute | solution.py:412
  237.1 20.8 %collective-permute-start.45 = (bf16[2,128,1536]{2,1,0:T(8,128)(2,1)S(1)}, bf16[2,128,1536]{2,1,0:T(8,128)(2,1)S(1)}, u32[]{:S(2)}, u32[]{:S(2)}) collective-permute-start(bf16[2,128,1536]{2,1,0:T(8,128)(2,1)S(1)} %pad_maximum_fusion.5.refs_0_), channel_id=1, source_target_pairs={{0,4},{2,18},{4,8},{6,22},{8,12},{10,26},{12,0},{14,30},{16,20},{1... | collective-permute-start | bytes 2359304 | tf_op jit(solution)/shard_map/ppermute | solution.py:407
  238.0 23.5 %collective-permute-start.46 = (bf16[2,128,1536]{2,1,0:T(8,128)(2,1)S(1)}, bf16[2,128,1536]{2,1,0:T(8,128)(2,1)S(1)}, u32[]{:S(2)}, u32[]{:S(2)}) collective-permute-start(bf16[2,128,1536]{2,1,0:T(8,128)(2,1)S(1)} %pad_maximum_fusion.5.refs_0_), channel_id=1, source_target_pairs={{0,2},{2,0},{4,6},{6,4},{8,10},{10,8},{12,14},{14,12},{16,18},{18,... | collective-permute-start | bytes 2359304 | tf_op jit(solution)/shard_map/ppermute | solution.py:388
  281.9 18.7 %collective-permute-start.63 = (bf16[2,128,1536]{2,1,0:T(8,128)(2,1)}, bf16[2,128,1536]{2,1,0:T(8,128)(2,1)S(1)}, u32[]{:S(2)}, u32[]{:S(2)}) collective-permute-start(bf16[2,128,1536]{2,1,0:T(8,128)(2,1)} %get-tuple-element.194), channel_id=1, source_target_pairs={{0,2},{2,0},{4,6},{6,4},{8,10},{10,8},{12,14},{14,12},{16,18},{18,... | collective-permute-start | bytes 2359304 | tf_op jit(solution)/shard_map/ppermute | solution.py:388
  304.3 20.8 %collective-permute-start.52 = (bf16[2,128,1536]{2,1,0:T(8,128)(2,1)S(1)}, bf16[2,128,1536]{2,1,0:T(8,128)(2,1)S(1)}, u32[]{:S(2)}, u32[]{:S(2)}) collective-permute-start(bf16[2,128,1536]{2,1,0:T(8,128)(2,1)S(1)} %add_convert_fusion.13), channel_id=1, source_target_pairs={{0,4},{2,18},{4,8},{6,22},{8,12},{10,26},{12,0},{14,30},{16,20},{1... | collective-permute-start | bytes 2359304 | tf_op jit(solution)/shard_map/ppermute | solution.py:412
  306.5 18.5 %collective-permute-start.54 = (bf16[2,128,1536]{2,1,0:T(8,128)(2,1)S(1)}, bf16[2,128,1536]{2,1,0:T(8,128)(2,1)S(1)}, u32[]{:S(2)}, u32[]{:S(2)}) collective-permute-start(bf16[2,128,1536]{2,1,0:T(8,128)(2,1)S(1)} %add_convert_fusion.12), channel_id=1, source_target_pairs={{0,8},{2,34},{4,12},{6,38},{8,0},{10,42},{12,4},{14,46},{16,24},{1... | collective-permute-start | bytes 2359304 | tf_op jit(solution)/shard_map/ppermute | solution.py:412
  307.4 18.8 %collective-permute-start.56 = (bf16[2,128,1536]{2,1,0:T(8,128)(2,1)S(1)}, bf16[2,128,1536]{2,1,0:T(8,128)(2,1)S(1)}, u32[]{:S(2)}, u32[]{:S(2)}) collective-permute-start(bf16[2,128,1536]{2,1,0:T(8,128)(2,1)S(1)} %add_convert_fusion.11), channel_id=1, source_target_pairs={{0,12},{2,50},{4,0},{6,54},{8,4},{10,58},{12,8},{14,62},{16,28},{1... | collective-permute-start | bytes 2359304 | tf_op jit(solution)/shard_map/ppermute | solution.py:412
  309.6 19.9 %collective-permute-start.60 = (bf16[2,128,1536]{2,1,0:T(8,128)(2,1)S(1)}, bf16[2,128,1536]{2,1,0:T(8,128)(2,1)S(1)}, u32[]{:S(2)}, u32[]{:S(2)}) collective-permute-start(bf16[2,128,1536]{2,1,0:T(8,128)(2,1)S(1)} %get-tuple-element.188), channel_id=1, source_target_pairs={{0,2},{2,0},{4,6},{6,4},{8,10},{10,8},{12,14},{14,12},{16,18},{18,... | collective-permute-start | bytes 2359304 | tf_op jit(solution)/shard_map/ppermute | solution.py:388
  346.3 19.3 %collective-permute-start.66 = (bf16[2,128,1536]{2,1,0:T(8,128)(2,1)}, bf16[2,128,1536]{2,1,0:T(8,128)(2,1)}, u32[]{:S(2)}, u32[]{:S(2)}) collective-permute-start(bf16[2,128,1536]{2,1,0:T(8,128)(2,1)} %add_convert_fusion.8), channel_id=1, source_target_pairs={{0,4},{2,18},{4,8},{6,22},{8,12},{10,26},{12,0},{14,30},{16,20},{1... | collective-permute-start | bytes 2359304 | tf_op jit(solution)/shard_map/ppermute | solution.py:412
  346.3 21.9 %collective-permute-start.67 = (bf16[2,128,1536]{2,1,0:T(8,128)(2,1)}, bf16[2,128,1536]{2,1,0:T(8,128)(2,1)}, u32[]{:S(2)}, u32[]{:S(2)}) collective-permute-start(bf16[2,128,1536]{2,1,0:T(8,128)(2,1)} %add_convert_fusion.7), channel_id=1, source_target_pairs={{0,8},{2,34},{4,12},{6,38},{8,0},{10,42},{12,4},{14,46},{16,24},{1... | collective-permute-start | bytes 2359304 | tf_op jit(solution)/shard_map/ppermute | solution.py:412
  349.8 18.4 %collective-permute-start.68 = (bf16[2,128,1536]{2,1,0:T(8,128)(2,1)}, bf16[2,128,1536]{2,1,0:T(8,128)(2,1)}, u32[]{:S(2)}, u32[]{:S(2)}) collective-permute-start(bf16[2,128,1536]{2,1,0:T(8,128)(2,1)} %add_convert_fusion.6), channel_id=1, source_target_pairs={{0,12},{2,50},{4,0},{6,54},{8,4},{10,58},{12,8},{14,62},{16,28},{1... | collective-permute-start | bytes 2359304 | tf_op jit(solution)/shard_map/ppermute | solution.py:412
  350.9 45.1 %collective-permute-start.75 = (bf16[2,256,1536]{2,1,0:T(8,128)(2,1)}, bf16[2,256,1536]{2,1,0:T(8,128)(2,1)}, u32[]{:S(2)}, u32[]{:S(2)}) collective-permute-start(bf16[2,256,1536]{2,1,0:T(8,128)(2,1)} %slice.142), channel_id=1, source_target_pairs={{0,1},{1,0},{2,3},{3,2},{4,5},{5,4},{6,7},{7,6},{8,9},{9,8},{10,11... | collective-permute-start | bytes 4718600 | tf_op jit(solution)/shard_map/ppermute | solution.py:392
  436.5 20.1 %collective-permute-start.88 = (bf16[2,128,1536]{2,1,0:T(8,128)(2,1)S(1)}, bf16[2,128,1536]{2,1,0:T(8,128)(2,1)S(1)}, u32[]{:S(2)}, u32[]{:S(2)}) collective-permute-start(bf16[2,128,1536]{2,1,0:T(8,128)(2,1)S(1)} %constant_dynamic-update-slice_fusion.refs_0_), channel_id=1, source_target_pairs={{0,4},{2,18},{4,8},{6,22},{8,12},{10,26},{12,0},{14,30},{16,20},{1... | collective-permute-start | bytes 2359304 | tf_op jit(solution)/shard_map/ppermute | solution.py:407
  463.7 21.6 %collective-permute-start.93 = (bf16[2,128,1536]{2,1,0:T(8,128)(2,1)S(1)}, bf16[2,128,1536]{2,1,0:T(8,128)(2,1)S(1)}, u32[]{:S(2)}, u32[]{:S(2)}) collective-permute-start(bf16[2,128,1536]{2,1,0:T(8,128)(2,1)S(1)} %get-tuple-element.237), channel_id=1, source_target_pairs={{0,1},{1,0},{2,3},{3,2},{4,5},{5,4},{6,7},{7,6},{8,9},{9,8},{10,11... | collective-permute-start | bytes 2359304 | tf_op jit(solution)/shard_map/ppermute | solution.py:392
  489.4 20.8 %collective-permute-start.96 = (bf16[2,128,1536]{2,1,0:T(8,128)(2,1)S(1)}, bf16[2,128,1536]{2,1,0:T(8,128)(2,1)S(1)}, u32[]{:S(2)}, u32[]{:S(2)}) collective-permute-start(bf16[2,128,1536]{2,1,0:T(8,128)(2,1)S(1)} %add_convert_fusion.3), channel_id=1, source_target_pairs={{0,4},{2,18},{4,8},{6,22},{8,12},{10,26},{12,0},{14,30},{16,20},{1... | collective-permute-start | bytes 2359304 | tf_op jit(solution)/shard_map/ppermute | solution.py:412
  491.1 19.2 %collective-permute-start.98 = (bf16[2,128,1536]{2,1,0:T(8,128)(2,1)S(1)}, bf16[2,128,1536]{2,1,0:T(8,128)(2,1)S(1)}, u32[]{:S(2)}, u32[]{:S(2)}) collective-permute-start(bf16[2,128,1536]{2,1,0:T(8,128)(2,1)S(1)} %add_convert_fusion.2), channel_id=1, source_target_pairs={{0,8},{2,34},{4,12},{6,38},{8,0},{10,42},{12,4},{14,46},{16,24},{1... | collective-permute-start | bytes 2359304 | tf_op jit(solution)/shard_map/ppermute | solution.py:412
  493.4 19.2 %collective-permute-start.100 = (bf16[2,128,1536]{2,1,0:T(8,128)(2,1)S(1)}, bf16[2,128,1536]{2,1,0:T(8,128)(2,1)S(1)}, u32[]{:S(2)}, u32[]{:S(2)}) collective-permute-start(bf16[2,128,1536]{2,1,0:T(8,128)(2,1)S(1)} %add_convert_fusion.1), channel_id=1, source_target_pairs={{0,12},{2,50},{4,0},{6,54},{8,4},{10,58},{12,8},{14,62},{16,28},{1... | collective-permute-start | bytes 2359304 | tf_op jit(solution)/shard_map/ppermute | solution.py:412
  494.1 18.9 %collective-permute-start.101 = (bf16[2,128,1536]{2,1,0:T(8,128)(2,1)S(1)}, bf16[2,128,1536]{2,1,0:T(8,128)(2,1)S(1)}, u32[]{:S(2)}, u32[]{:S(2)}) collective-permute-start(bf16[2,128,1536]{2,1,0:T(8,128)(2,1)S(1)} %get-tuple-element.255), channel_id=1, source_target_pairs={{0,1},{1,0},{2,3},{3,2},{4,5},{5,4},{6,7},{7,6},{8,9},{9,8},{10,11... | collective-permute-start | bytes 2359304 | tf_op jit(solution)/shard_map/ppermute | solution.py:392
  535.8 22.8 %all-to-all-start.1 = ((bf16[16,24,1536]{2,1,0:T(8,128)(2,1)}), bf16[16,24,1536]{2,1,0:T(8,128)(2,1)}, u32[]{:S(2)}, u32[]{:S(2)}) async-start(bf16[16,24,1536]{2,1,0:T(8,128)(2,1)} %bitcast.145), calls=%async_computation.1 | async-start | bytes 2359296 | tf_op jit(solution)/shard_map/all_to_all | solution.py:443
  541.6 83.6 %all-gather.9.cloned.1.call-start = ((), (), s32[]{:S(2)}) async-start(), calls=%async_computation.6 | async-start | bytes 2433024 | tf_op jit(solution)/shard_map/all_gather | solution.py:769
  563.5 37.2 %all-to-all-start.2 = ((bf16[16,96,384]{2,1,0:T(8,128)(2,1)}), bf16[16,96,384]{2,1,0:T(8,128)(2,1)}, u32[]{:S(2)}, u32[]{:S(2)}) async-start(bf16[16,96,384]{2,1,0:T(8,128)(2,1)} %bitcast.135), calls=%async_computation.2 | async-start | bytes 2359296 | tf_op jit(solution)/shard_map/all_to_all | solution.py:443
  568.8 113.9 %all-gather.11.cloned.1.call-start = ((), (), s32[]{:S(2)}) async-start(), calls=%async_computation.7 | async-start | bytes 2433024 | tf_op jit(solution)/shard_map/all_gather | solution.py:787
  568.9 23.2 %collective-permute-start.107 = (bf16[2,512,256]{2,1,0:T(8,128)(2,1)}, bf16[2,512,256]{2,1,0:T(8,128)(2,1)}, u32[]{:S(2)}, u32[]{:S(2)}) collective-permute-start(bf16[2,512,256]{2,1,0:T(8,128)(2,1)} %get-tuple-element.259), channel_id=1, source_target_pairs={{0,4},{2,18},{4,8},{6,22},{8,12},{10,26},{12,0},{14,30},{16,20},{1... | collective-permute-start | bytes 1572872 | tf_op jit(solution)/shard_map/ppermute | solution.py:412
  570.2 28.1 %collective-permute-start.108 = (bf16[2,512,256]{2,1,0:T(8,128)(2,1)}, bf16[2,512,256]{2,1,0:T(8,128)(2,1)}, u32[]{:S(2)}, u32[]{:S(2)}) collective-permute-start(bf16[2,512,256]{2,1,0:T(8,128)(2,1)} %get-tuple-element.260), channel_id=1, source_target_pairs={{0,8},{2,34},{4,12},{6,38},{8,0},{10,42},{12,4},{14,46},{16,24},{1... | collective-permute-start | bytes 1572872 | tf_op jit(solution)/shard_map/ppermute | solution.py:412
  572.6 25.7 %collective-permute-start.109 = (bf16[2,512,256]{2,1,0:T(8,128)(2,1)}, bf16[2,512,256]{2,1,0:T(8,128)(2,1)}, u32[]{:S(2)}, u32[]{:S(2)}) collective-permute-start(bf16[2,512,256]{2,1,0:T(8,128)(2,1)} %get-tuple-element.261), channel_id=1, source_target_pairs={{0,12},{2,50},{4,0},{6,54},{8,4},{10,58},{12,8},{14,62},{16,28},{1... | collective-permute-start | bytes 1572872 | tf_op jit(solution)/shard_map/ppermute | solution.py:412
  587.1 24.1 %collective-permute-start.113 = (bf16[256,1536]{1,0:T(8,128)(2,1)}, bf16[256,1536]{1,0:T(8,128)(2,1)}, u32[]{:S(2)}, u32[]{:S(2)}) collective-permute-start(bf16[256,1536]{1,0:T(8,128)(2,1)} %get-tuple-element.273), channel_id=1, source_target_pairs={{0,1},{1,0},{2,3},{3,2},{4,5},{5,4},{6,7},{7,6},{8,9},{9,8},{10,11... | collective-permute-start | bytes 2359304 | tf_op jit(solution)/shard_map/ppermute | solution.py:392
  626.0 27.6 %collective-permute-start.114 = (bf16[384,1536]{1,0:T(8,128)(2,1)}, bf16[384,1536]{1,0:T(8,128)(2,1)}, u32[]{:S(2)}, u32[]{:S(2)}) collective-permute-start(bf16[384,1536]{1,0:T(8,128)(2,1)} %get-tuple-element.286), channel_id=1, source_target_pairs={{0,1},{1,0},{2,3},{3,2},{4,5},{5,4},{6,7},{7,6},{8,9},{9,8},{10,11... | collective-permute-start | bytes 3538952 | tf_op jit(solution)/shard_map/ppermute | solution.py:392
  629.7 23.9 %all-to-all-start.3 = ((bf16[16,112,256]{2,1,0:T(8,128)(2,1)}), bf16[16,112,256]{2,1,0:T(8,128)(2,1)}, u32[]{:S(2)}, u32[]{:S(2)}) async-start(bf16[16,112,256]{2,1,0:T(8,128)(2,1)} %pad_maximum_fusion.1), calls=%async_computation.3 | async-start | bytes 1835008 | tf_op jit(solution)/shard_map/all_to_all | solution.py:443
  657.7 24.3 %all-to-all-start.4 = ((bf16[16,112,256]{2,1,0:T(8,128)(2,1)}), bf16[16,112,256]{2,1,0:T(8,128)(2,1)}, u32[]{:S(2)}, u32[]{:S(2)}) async-start(bf16[16,112,256]{2,1,0:T(8,128)(2,1)} %broadcast_in_dim.42), calls=%async_computation.4 | async-start | bytes 1835008 | tf_op jit(solution)/shard_map/all_to_all | solution.py:443
  (247 other events, 2973.0 us)
Sparse Core Ops, SparseCore 0:
  524.2 44.1 all-gather.6
  570.6 54.4 all-gather.8
  627.4 55.2 all-gather.10
